TPU v7x, 256 devices: a whole 4x4x8 slice. The times are simulated.
256 devices in a mesh: ctx: 16 (over z, core), ulys: 16 (over y, x).
Axes of the slice: x: 4, y: 4, z: 8, core: 2. Of those that a mesh axis runs over, the one named last changes fastest.
Arguments:
- query_rows: bfloat16 [32768, 4096], P(('ctx', 'ulys')), may hold values from -8 to 8
- key_rows: bfloat16 [32768, 512], P(('ctx', 'ulys')), may hold values from -8 to 8
- value_rows: bfloat16 [32768, 512], P(('ctx', 'ulys')), may hold values from -6 to 6
- column_blocks: int32 [32, 8], replicated, may hold values from 0 to 511, as said below
- column_count: int32 [32], replicated, may hold values from 1 to 8, as said below
- slash_offsets: int32 [32, 24], replicated, may hold values from 1 to 504, as said below
- slash_count: int32 [32], replicated, may hold values from 1 to 24, as said below
Outputs:
- attended: bfloat16 [32768, 4096], P(('ctx', 'ulys'))
Inputs may be any that keep to these rules, and one draw needn't show every extreme that they name: `column_blocks`: within a head the entries increase; the a-th lies among blocks a * (512 // 8) to (a + 1) * (512 // 8) - 1, with 512 // 8 = 64. `column_count`: some head uses all 8. `slash_offsets`: within a head the entries increase; the s-th lies among offsets 1 + s * ((512 - 1) // 24) to (s + 1) * ((512 - 1) // 24). `slash_count`: some head uses all 24.
All inputs are finite; a program needn't handle non-finite values.
Results may differ from a plain program's by a relative error of at most 0.0049.
Values may be sent and summed in bfloat16 or wider, within the bound.
No kernel may reach another device: no remote copies, remote signals or barrier semaphores. Data moves between devices by JAX's collectives and lax.ppermute only.
A program may use at most 128 MiB of HBM per device.

v0:
```python
import math

import jax
import jax.numpy as jnp
from jax import lax
from jax.sharding import PartitionSpec as P

H = 32
KVH = 4
DH = 128
BLK = 64
NV = 8
NS = 24


step_blocks = 8
neg_fill = -1e30


def attend(head_inputs, kv_blocks, first_block, rescale_factor):
    query_head, column_row, column_live, slash_row, slash_live = head_inputs
    row_count = query_head.shape[0]
    block_count = row_count // BLK
    total_blocks = kv_blocks.shape[0]
    q_blocks = query_head.reshape(block_count, BLK, DH)
    query_block = first_block + jnp.arange(block_count, dtype=jnp.int32)
    live_blocks = 1 + column_live + slash_live
    step_count = (live_blocks + step_blocks - 1) // step_blocks
    causal = jnp.arange(BLK)[None, :] <= jnp.arange(BLK)[:, None]
    upto_column = jnp.arange(NV, dtype=jnp.int32) < column_live

    def advance(step_index, carry):
        running, denominator, weight_totals = carry
        places = step_index * step_blocks + jnp.arange(step_blocks, dtype=jnp.int32)
        column_slot = places - 1
        slash_slot = places - 1 - column_live
        is_local = places == 0
        is_column = (column_slot >= 0) & (column_slot < column_live)
        is_slash = (slash_slot >= 0) & (slash_slot < slash_live)
        column_block = column_row[jnp.clip(column_slot, 0, NV - 1)]
        slash_block = query_block[:, None] - slash_row[jnp.clip(slash_slot, 0, NS - 1)][None, :]
        already = jnp.any(
            (column_row[None, None, :] == slash_block[:, :, None]) & upto_column[None, None, :],
            axis=2,
        )
        blocks = jnp.where(
            is_local[None, :],
            query_block[:, None],
            jnp.where(is_column[None, :], column_block[None, :], slash_block),
        )
        usable = (
            is_local[None, :]
            | is_column[None, :] & (column_block[None, :] < query_block[:, None])
            | is_slash[None, :] & (slash_block >= 0) & jnp.logical_not(already)
        )
        picked = kv_blocks[jnp.clip(blocks, 0, total_blocks - 1)]
        logit_scores = (
            jnp.einsum(
                "oyi,ojsi->oyjs",
                q_blocks,
                picked[:, :, :, 0, :],
                preferred_element_type=jnp.float32,
            )
            * rescale_factor
        )
        visible = usable[:, None, :, None] & (
            jnp.logical_not(is_local)[None, None, :, None] | causal[None, :, None, :]
        )
        logit_scores = jnp.where(visible, logit_scores, neg_fill)
        new_top = jnp.maximum(running, jnp.max(logit_scores, axis=(2, 3)))
        exponent = jnp.where(visible, jnp.exp(logit_scores - new_top[:, :, None, None]), 0.0)
        shrink = jnp.exp(running - new_top)
        denominator = denominator * shrink + jnp.sum(exponent, axis=(2, 3))
        weight_totals = weight_totals * shrink[:, :, None] + jnp.einsum(
            "axjz,ajzo->axo",
            exponent.astype(jnp.bfloat16),
            picked[:, :, :, 1, :],
            preferred_element_type=jnp.float32,
        )
        return (new_top, denominator, weight_totals)

    initial = (
        jnp.full((block_count, BLK), neg_fill, jnp.float32),
        jnp.zeros((block_count, BLK), jnp.float32),
        jnp.zeros((block_count, BLK, DH), jnp.float32),
    )
    running, denominator, weight_totals = lax.fori_loop(0, step_count, advance, initial)
    return (weight_totals / denominator[:, :, None]).astype(jnp.bfloat16).reshape(row_count, DH)


def per_device(
    query_rows, key_rows, value_rows, column_blocks, column_count, slash_offsets, slash_count
):
    across = lax.axis_size("ulys")
    tok_count = query_rows.shape[0]
    per_dev = H // across
    sharers = across // KVH
    rescale_factor = 1.0 / math.sqrt(DH)
    queries = query_rows.reshape(tok_count, H, DH)
    ordering = jnp.arange(H, dtype=jnp.int32)
    query_slots = queries.reshape(tok_count, across, per_dev, DH)
    paired = jnp.stack(
        [key_rows.reshape(tok_count, KVH, DH), value_rows.reshape(tok_count, KVH, DH)], axis=2
    )
    widened = jnp.repeat(paired, sharers, axis=1)
    own_queries, own_pairs = (
        lax.all_to_all(query_slots, "ulys", split_axis=1, concat_axis=0, tiled=True),
        lax.all_to_all(widened, "ulys", split_axis=1, concat_axis=0, tiled=True),
    )
    all_pairs = lax.all_gather(
        own_pairs.reshape(tok_count * across, 2, DH), "ctx", axis=0, tiled=True
    )
    kv_blocks = all_pairs.reshape(-1, BLK, 2, DH)
    group_rows = tok_count * across
    own_heads = lax.dynamic_slice_in_dim(ordering, lax.axis_index("ulys") * per_dev, per_dev)
    first_block = lax.axis_index("ctx") * (group_rows // BLK)
    head_queries = jnp.transpose(own_queries.reshape(group_rows, per_dev, DH), (1, 0, 2))
    head_inputs = (
        head_queries,
        jnp.take(column_blocks, own_heads, axis=0),
        jnp.take(column_count, own_heads),
        jnp.take(slash_offsets, own_heads, axis=0),
        jnp.take(slash_count, own_heads),
    )
    outputs = lax.map(
        lambda entry_inputs: attend(entry_inputs, kv_blocks, first_block, rescale_factor),
        head_inputs,
    )
    returned = jnp.transpose(outputs, (1, 0, 2)).reshape(across, tok_count, per_dev, DH)
    restored = lax.all_to_all(returned, "ulys", split_axis=0, concat_axis=2, tiled=True).reshape(
        tok_count, H, DH
    )
    return restored.reshape(tok_count, H * DH)


def solution(mesh):
    in_specs = (
        P(("ctx", "ulys"), None),
        P(("ctx", "ulys"), None),
        P(("ctx", "ulys"), None),
        P(),
        P(),
        P(),
        P(),
    )
    out_specs = P(("ctx", "ulys"), None)
    return jax.shard_map(
        per_device, mesh=mesh, in_specs=in_specs, out_specs=out_specs, check_vma=False
    )
```

profile of v0, /device:TPU:1, one launch (start us, length us, event | category | flops | bytes accessed | tf_op | source)
XLA Modules:
  0.0 691.4 jit_solution(10329167566730902675)
XLA Ops:
  6.6 1.0 stack_reshape.6
  7.5 0.9 stack_reshape.7
  9.0 0.8 broadcast_in_dim.103
  9.8 23.6 %all_to_all.45 = bf16[128,16,2,128]{3,2,0,1:T(2,128)(2,1)} all-to-all(bf16[128,16,2,128]{3,2,0,1:T(2,128)(2,1)S(1)} %bitcast.116), channel_id=1, replica_groups=mesh['ctx'=16,'ulys'=16] {'ulys'}, dimensions={1} | all-to-all | bytes 2097152 | tf_op jit(solution)/shard_map/all_to_all | solution.py:108
  33.4 1.6 copy.44
  35.1 1.3 copy.45
  36.4 3.7 all-to-all-start
  42.9 12.2 %all-to-all-done = bf16[128,16,2,128]{3,0,2,1:T(8,128)(2,1)S(1)} async-done(((bf16[128,16,2,128]{3,0,2,1:T(8,128)(2,1)}), bf16[128,16,2,128]{3,0,2,1:T(8,128)(2,1)S(1)}, u32[]{:S(2)}, u32[]{:S(2)}) %all-to-all-start) | async-done | bytes 1048608 | tf_op jit(solution)/shard_map/all_to_all | solution.py:107
  55.2 74.6 %all-gather.2.cloned.1.call-done = bf16[32768,2,128]{2,1,0:T(2,128)(2,1)} async-done(((bf16[2048,2,128]{2,1,0:T(2,128)(2,1)}), bf16[32768,2,128]{2,1,0:T(2,128)(2,1)}) %all-gather.2.cloned.1.call-update) | async-done | bytes 16777232 | tf_op jit(solution)/shard_map/all_gather | solution.py:110
  129.8 239.7 %while.55 = (s32[]{:T(128)}, bf16[2,2048,128]{2,1,0:T(8,128)(2,1)}, s32[2]{0:T(128)S(1)}, s32[2]{0:T(128)S(1)}, s32[2,8]{1,0:T(2,128)S(1)}, /*index=5*/s32[]{:T(...) while((s32[]{:T(128)}, bf16[2,2048,128]{2,1,0:T(8,128)(2,1)}, ...), condition=%wide.region_6.8_spmd, body=%wide.region_0.7_spmd.sunk | while | flops 554751232 | bytes 104181096 | solution.py:125
  131.1 0.7 dynamic_slice.76
  132.7 115.7 %while.56 = (s32[]{:T(128)}, f32[32,64]{1,0:T(8,128)S(1)}, f32[32,64]{1,0:T(8,128)S(1)}, f32[32,64,128]{2,1,0:T(8,128)S(1)}, s32[]{:T(128)}, /*index=5*/s32[]{:T...) while((s32[]{:T(128)}, f32[32,64]{1,0:T(8,128)S(1)}, ...), condition=%wide.region_5.6_spmd.clone.clone, body=%wide.region_1.5_spmd.clone.clone.sunk | while | flops 554226944 | bytes 99436640 | solution.py:87
  135.5 1.3 compare_and_fusion.4
  137.2 27.3 %gather_fusion.2 = bf16[256,64,2,128]{3,2,1,0:T(2,128)(2,1)} fusion(bf16[512,64,2,128]{3,2,1,0:T(2,128)(2,1)} %get-tuple-element.723, s32[1024]{0:T(1024)S(1)} %pad_clamp_fusion.9), kind=kCustom, calls=%fused_computation.3.clone.clone.clone.1 | custom fusion | bytes 16778240 | tf_op jit(solution)/shard_map/while/body/eval_jaxpr/while/body/gather | solution.py:56
  164.5 8.9 %copy.57 = bf16[256,64,2,128]{3,1,0,2:T(8,128)(2,1)} copy(bf16[256,64,2,128]{3,2,1,0:T(2,128)(2,1)} %gather_fusion.2) | data formatting | bytes 16777216 | tf_op jit(solution)/shard_map/while/body/eval_jaxpr/while/body/gather | solution.py:56
  173.6 3.9 fusion.47
  177.5 3.2 copy-done.1
  180.7 3.3 fusion.48
  184.1 6.7 fusion.49
  193.5 1.3 compare_and_fusion.4
  195.2 27.0 %gather_fusion.2 = bf16[256,64,2,128]{3,2,1,0:T(2,128)(2,1)} fusion(bf16[512,64,2,128]{3,2,1,0:T(2,128)(2,1)} %get-tuple-element.723, s32[1024]{0:T(1024)S(1)} %pad_clamp_fusion.9), kind=kCustom, calls=%fused_computation.3.clone.clone.clone.1 | custom fusion | bytes 16778240 | tf_op jit(solution)/shard_map/while/body/eval_jaxpr/while/body/gather | solution.py:56
  222.2 8.9 %copy.57 = bf16[256,64,2,128]{3,1,0,2:T(8,128)(2,1)} copy(bf16[256,64,2,128]{3,2,1,0:T(2,128)(2,1)} %gather_fusion.2) | data formatting | bytes 16777216 | tf_op jit(solution)/shard_map/while/body/eval_jaxpr/while/body/gather | solution.py:56
  231.3 3.9 fusion.47
  235.2 3.2 copy-done.1
  238.4 3.3 fusion.48
  241.8 6.7 fusion.49
  248.8 0.8 bitcast_dynamic-update-slice_fusion.2
  250.9 0.7 dynamic_slice.76
  252.5 115.7 %while.56 = (s32[]{:T(128)}, f32[32,64]{1,0:T(8,128)S(1)}, f32[32,64]{1,0:T(8,128)S(1)}, f32[32,64,128]{2,1,0:T(8,128)S(1)}, s32[]{:T(128)}, /*index=5*/s32[]{:T...) while((s32[]{:T(128)}, f32[32,64]{1,0:T(8,128)S(1)}, ...), condition=%wide.region_5.6_spmd.clone.clone, body=%wide.region_1.5_spmd.clone.clone.sunk | while | flops 554226944 | bytes 99436640 | solution.py:87
  255.3 1.3 compare_and_fusion.4
  257.0 27.1 %gather_fusion.2 = bf16[256,64,2,128]{3,2,1,0:T(2,128)(2,1)} fusion(bf16[512,64,2,128]{3,2,1,0:T(2,128)(2,1)} %get-tuple-element.723, s32[1024]{0:T(1024)S(1)} %pad_clamp_fusion.9), kind=kCustom, calls=%fused_computation.3.clone.clone.clone.1 | custom fusion | bytes 16778240 | tf_op jit(solution)/shard_map/while/body/eval_jaxpr/while/body/gather | solution.py:56
  284.1 8.9 %copy.57 = bf16[256,64,2,128]{3,1,0,2:T(8,128)(2,1)} copy(bf16[256,64,2,128]{3,2,1,0:T(2,128)(2,1)} %gather_fusion.2) | data formatting | bytes 16777216 | tf_op jit(solution)/shard_map/while/body/eval_jaxpr/while/body/gather | solution.py:56
  293.2 3.9 fusion.47
  297.1 3.2 copy-done.1
  300.3 3.3 fusion.48
  303.7 6.7 fusion.49
  313.1 1.3 compare_and_fusion.4
  314.8 27.2 %gather_fusion.2 = bf16[256,64,2,128]{3,2,1,0:T(2,128)(2,1)} fusion(bf16[512,64,2,128]{3,2,1,0:T(2,128)(2,1)} %get-tuple-element.723, s32[1024]{0:T(1024)S(1)} %pad_clamp_fusion.9), kind=kCustom, calls=%fused_computation.3.clone.clone.clone.1 | custom fusion | bytes 16778240 | tf_op jit(solution)/shard_map/while/body/eval_jaxpr/while/body/gather | solution.py:56
  342.0 8.9 %copy.57 = bf16[256,64,2,128]{3,1,0,2:T(8,128)(2,1)} copy(bf16[256,64,2,128]{3,2,1,0:T(2,128)(2,1)} %gather_fusion.2) | data formatting | bytes 16777216 | tf_op jit(solution)/shard_map/while/body/eval_jaxpr/while/body/gather | solution.py:56
  351.1 3.9 fusion.47
  355.0 3.2 copy-done.1
  358.2 3.3 fusion.48
  361.6 6.7 fusion.49
  368.6 0.8 bitcast_dynamic-update-slice_fusion.2
  369.4 2.8 copy.48
  372.3 310.1 %all_to_all.46 = bf16[16,128,2,128]{3,2,1,0:T(2,128)(2,1)S(1)} all-to-all(bf16[16,128,2,128]{3,2,1,0:T(2,128)(2,1)S(1)} %bitcast.118), channel_id=1, replica_groups=mesh['ctx'=16,'ulys'=16] {'ulys'}, dimensions={0} | all-to-all | bytes 2097152 | tf_op jit(solution)/shard_map/all_to_all | solution.py:130
  682.4 0.8 copy.49
  683.3 1.3 copy.50
  (146 shorter events, 18.7 us)
Async XLA Ops:
  6.5 33.6 %copy-start = (s32[32]{0:T(128)S(1)}, s32[32]{0:T(128)}, u32[]{:S(2)}) copy-start(s32[32]{0:T(128)} %param.17) | copy-start | bytes 388
  6.5 34.3 %copy-start.2 = (s32[32]{0:T(128)S(1)}, s32[32]{0:T(128)}, u32[]{:S(2)}) copy-start(s32[32]{0:T(128)} %param.19) | copy-start | bytes 388
  6.5 34.9 %copy-start.3 = (s32[32,24]{0,1:T(8,128)S(1)}, s32[32,24]{0,1:T(8,128)}, u32[]{:S(2)}) copy-start(s32[32,24]{0,1:T(8,128)} %param.18) | copy-start | bytes 9220
  6.5 35.5 %copy-start.4 = (s32[32,8]{0,1:T(8,128)S(1)}, s32[32,8]{0,1:T(8,128)}, u32[]{:S(2)}) copy-start(s32[32,8]{0,1:T(8,128)} %param.16) | copy-start | bytes 3076
  6.5 123.2 %all-gather.2.cloned.1.call-start = ((), (), s32[]{:S(2)}) async-start(), calls=%async_computation.3 | async-start | bytes 17825792 | tf_op jit(solution)/shard_map/all_gather | solution.py:110
  36.4 18.7 %all-to-all-start = ((bf16[128,16,2,128]{3,0,2,1:T(8,128)(2,1)}), bf16[128,16,2,128]{3,0,2,1:T(8,128)(2,1)S(1)}, u32[]{:S(2)}, u32[]{:S(2)}) async-start(bf16[128,16,2,128]{3,0,2,1:T(8,128)(2,1)} %copy.45), calls=%async_computation | async-start | bytes 2097152 | tf_op jit(solution)/shard_map/all_to_all | solution.py:107
  173.6 10.5 %slice-start = ((s8[8388608]{0:T(1024)(128)(4,1)}), s8[4194304]{0:T(1024)(128)(4,1)S(1)}, s32[]{:S(2)}) async-start(s8[8388608]{0:T(1024)(128)(4,1)} %bitcast.109), calls=%async_computation.4 | async-start | bytes 8388608 | tf_op jit(solution)/shard_map/while/body/eval_jaxpr/while
  173.6 10.5 %slice-start.1 = ((s8[8388608]{0:T(1024)(128)(4,1)}), s8[4194304]{0:T(1024)(128)(4,1)S(1)}, s32[]{:S(2)}) async-start(s8[8388608]{0:T(1024)(128)(4,1)} %bitcast.109), calls=%async_computation.5 | async-start | bytes 8388608 | tf_op jit(solution)/shard_map/while/body/eval_jaxpr/while
  177.5 3.2 copy-start.1
  231.3 10.5 %slice-start = ((s8[8388608]{0:T(1024)(128)(4,1)}), s8[4194304]{0:T(1024)(128)(4,1)S(1)}, s32[]{:S(2)}) async-start(s8[8388608]{0:T(1024)(128)(4,1)} %bitcast.109), calls=%async_computation.4 | async-start | bytes 8388608 | tf_op jit(solution)/shard_map/while/body/eval_jaxpr/while
  231.3 10.5 %slice-start.1 = ((s8[8388608]{0:T(1024)(128)(4,1)}), s8[4194304]{0:T(1024)(128)(4,1)S(1)}, s32[]{:S(2)}) async-start(s8[8388608]{0:T(1024)(128)(4,1)} %bitcast.109), calls=%async_computation.5 | async-start | bytes 8388608 | tf_op jit(solution)/shard_map/while/body/eval_jaxpr/while
  235.2 3.2 copy-start.1
  293.2 10.5 %slice-start = ((s8[8388608]{0:T(1024)(128)(4,1)}), s8[4194304]{0:T(1024)(128)(4,1)S(1)}, s32[]{:S(2)}) async-start(s8[8388608]{0:T(1024)(128)(4,1)} %bitcast.109), calls=%async_computation.4 | async-start | bytes 8388608 | tf_op jit(solution)/shard_map/while/body/eval_jaxpr/while
  293.2 10.5 %slice-start.1 = ((s8[8388608]{0:T(1024)(128)(4,1)}), s8[4194304]{0:T(1024)(128)(4,1)S(1)}, s32[]{:S(2)}) async-start(s8[8388608]{0:T(1024)(128)(4,1)} %bitcast.109), calls=%async_computation.5 | async-start | bytes 8388608 | tf_op jit(solution)/shard_map/while/body/eval_jaxpr/while
  297.1 3.2 copy-start.1
  351.1 10.5 %slice-start = ((s8[8388608]{0:T(1024)(128)(4,1)}), s8[4194304]{0:T(1024)(128)(4,1)S(1)}, s32[]{:S(2)}) async-start(s8[8388608]{0:T(1024)(128)(4,1)} %bitcast.109), calls=%async_computation.4 | async-start | bytes 8388608 | tf_op jit(solution)/shard_map/while/body/eval_jaxpr/while
  351.1 10.5 %slice-start.1 = ((s8[8388608]{0:T(1024)(128)(4,1)}), s8[4194304]{0:T(1024)(128)(4,1)S(1)}, s32[]{:S(2)}) async-start(s8[8388608]{0:T(1024)(128)(4,1)} %bitcast.109), calls=%async_computation.5 | async-start | bytes 8388608 | tf_op jit(solution)/shard_map/while/body/eval_jaxpr/while
  355.0 3.2 copy-start.1
Sparse Core Ops, SparseCore 0:
  33.5 96.2 all-gather.1
where the time goes:
time: 694 us; the launch traced here: 691 us
  blocking collectives  334 us (48%)
  local copies, waits for them, and re-layouts  181 us (26%)
  waiting for transfers between devices  86.9 us (13%)
  matrix products  42.1 us (6%)
  other arithmetic  26.7 us (4%)
  between operations  13.5 us (2%)
    all_to_all x1, blocking collectives, per_device(): lax.all_to_all(returned, 'ulys', split_axis=0, concat_axis=2, tiled=True)  310 us
    gather x8, local copies, waits for them, and re-layouts, advance(): picked = kv_blocks[jnp.clip(blocks, 0, total_blocks - 1)]  144 us
    all_gather x1, waiting for transfers between devices, per_device(): lax.all_gather(own_pairs.reshape(tok_count * across, 2, DH), 'ctx', axis=...  74.6 us
    dot_general x4, matrix products, advance(): jnp.einsum('axjz,ajzo->axo', exponent.astype(jnp.bfloat16), picked[:, :,...  26.6 us
    all_to_all x1, blocking collectives, per_device(): lax.all_to_all(widened, 'ulys', split_axis=1, concat_axis=0, tiled=True)  23.6 us
    dot_general x4, matrix products, advance(): jnp.einsum('oyi,ojsi->oyjs', q_blocks, picked[:, :, :, 0, :], preferred_e...  15.5 us
  transfers between devices with their start and end apart: 2, of which 2 were waited for; matrix products, arithmetic and copies ran while one was open for 1% of the time, Pallas kernels for 0%

commit v1 on v0

v1 whole, which is shorter than its diff:
```python
import math

import jax
import jax.numpy as jnp
from jax import lax
from jax.experimental import pallas as pl
from jax.experimental.pallas import tpu as pltpu
from jax.sharding import Mesh, PartitionSpec as P

H = 32
KVH = 4
DH = 128
BLK = 64
NV = 8
NS = 24
SEQ = 32768

QB = 8
HG = H // KVH
CB = 4
CHUNKS = -(-(1 + NV + NS) // CB)
LMAX = CHUNKS * CB
SKEW = 4
C2 = math.log2(math.e) / math.sqrt(DH)
NEG = -1e30
NT = (((1,), (1,)), ((), ()))


def attend_kernel(
    lists, counts, q_ref, kv_hbm, o_ref, k_s, v_s, top_s, sum_s, acc_s, score_s, sem
):
    copy_k = pltpu.make_async_copy(kv_hbm.at[:, pl.ds(0, DH)], k_s, sem.at[0])
    copy_v = pltpu.make_async_copy(kv_hbm.at[:, pl.ds(DH, DH)], v_s, sem.at[1])
    copy_k.start()
    copy_v.start()
    copy_k.wait()
    copy_v.wait()
    lane = lax.broadcasted_iota(jnp.int32, (BLK, CB * BLK), 1)
    row = lax.broadcasted_iota(jnp.int32, (BLK, CB * BLK), 0)
    lane_row = lax.broadcasted_iota(jnp.int32, (1, CB * BLK), 1)

    def rows(i):
        return slice(i * BLK, (i + 1) * BLK)

    def head(h, _):
        columns = pl.ds(pl.multiple_of(h * DH, DH), DH)

        def gather(ref, i, c):
            base = (h * QB + i) * LMAX + c * CB
            return jnp.concatenate(
                [
                    ref[pl.ds(pl.multiple_of(lists[base + j] * BLK, BLK), BLK), :]
                    for j in range(CB)
                ],
                axis=0,
            )

        def scores(i, c):
            return lax.dot_general(
                q_ref[rows(i), columns],
                gather(k_s, i, c),
                NT,
                preferred_element_type=jnp.float32,
            )

        def weighted(i, c, p):
            return jnp.dot(p, gather(v_s, i, c), preferred_element_type=jnp.float32)

        def first_weights(i, s):
            live = counts[HG + h * QB + i]
            s = jnp.where((lane < live * BLK) & ((lane >= BLK) | (lane <= row)), s, NEG)
            top = jnp.max(jnp.maximum(s[:, :128], s[:, 128:]), axis=1, keepdims=True)
            shift = top * C2
            parts = [jnp.exp2(s[:, t * 128 : (t + 1) * 128] * C2 - shift) for t in range(2)]
            top_s[rows(i), :] = jnp.broadcast_to(top, (BLK, DH))
            sum_s[rows(i), :] = parts[0] + parts[1]
            return jnp.concatenate([x.astype(jnp.bfloat16) for x in parts], axis=1)

        def next_weights(i, c, s):
            live = counts[HG + h * QB + i]
            s = s + jnp.where(lane_row < (live - c * CB) * BLK, 0.0, NEG)
            old = top_s[rows(i), :]
            top = jnp.maximum(
                old, jnp.max(jnp.maximum(s[:, :128], s[:, 128:]), axis=1, keepdims=True)
            )
            shrink = jnp.exp2((old - top) * C2)
            shift = top * C2
            parts = [jnp.exp2(s[:, t * 128 : (t + 1) * 128] * C2 - shift) for t in range(2)]
            top_s[rows(i), :] = top
            sum_s[rows(i), :] = sum_s[rows(i), :] * shrink + (parts[0] + parts[1])
            return jnp.concatenate([x.astype(jnp.bfloat16) for x in parts], axis=1), shrink

        opening = [scores(i, 0) for i in range(QB)]
        for i in range(QB):
            score_s[rows(i), :] = scores(i, 1)
        weights = [first_weights(i, s) for i, s in enumerate(opening)]
        for i, p in enumerate(weights):
            acc_s[rows(i), :] = weighted(i, 0, p)

        def chunk(c, _):
            ahead = jnp.minimum(c + 1, CHUNKS - 1)
            held = {}
            for t in range(QB + SKEW):
                if t < QB:
                    s = score_s[rows(t), :]
                    score_s[rows(t), :] = scores(t, ahead)
                    held[t] = next_weights(t, c, s)
                i = t - SKEW
                if i >= 0:
                    p, shrink = held.pop(i)
                    acc_s[rows(i), :] = acc_s[rows(i), :] * shrink + weighted(i, c, p)
            return 0

        lax.fori_loop(1, counts[h], chunk, 0)
        for i in range(QB):
            total = jnp.sum(sum_s[rows(i), :], axis=1, keepdims=True)
            o_ref[rows(i), columns] = (acc_s[rows(i), :] / total).astype(jnp.bfloat16)
        return 0

    lax.fori_loop(0, HG, head, 0)


def attend(lists, counts, queries, pairs):
    any_space = pl.BlockSpec(memory_space=pl.ANY)
    vmem = pl.BlockSpec(memory_space=pltpu.VMEM)
    smem = pl.BlockSpec(memory_space=pltpu.SMEM)
    return pl.pallas_call(
        attend_kernel,
        out_shape=jax.ShapeDtypeStruct((QB * BLK, HG * DH), jnp.bfloat16),
        in_specs=[smem, smem, vmem, any_space],
        out_specs=vmem,
        scratch_shapes=[pltpu.VMEM((SEQ, DH), jnp.bfloat16)] * 2
        + [pltpu.VMEM((QB * BLK, DH), jnp.float32)] * 3
        + [pltpu.VMEM((QB * BLK, CB * BLK), jnp.float32), pltpu.SemaphoreType.DMA((2,))],
        compiler_params=pltpu.CompilerParams(vmem_limit_bytes=40 * 1024 * 1024),
    )(lists, counts, queries, pairs)


def block_lists(first_block, column_blocks, column_count, slash_offsets, slash_count):
    own = first_block + jnp.arange(QB, dtype=jnp.int32)[None, :, None]
    own = jnp.broadcast_to(own, (HG, QB, 1))
    column = jnp.broadcast_to(column_blocks[:, None, :], (HG, QB, NV))
    column_used = jnp.arange(NV, dtype=jnp.int32) < column_count[:, None, None]
    slash = own - slash_offsets[:, None, :]
    slash_used = jnp.arange(NS, dtype=jnp.int32) < slash_count[:, None, None]
    twice = jnp.any(
        (column[:, :, None, :] == slash[:, :, :, None]) & column_used[:, :, None, :], axis=3
    )
    blocks = jnp.concatenate([own, column, slash], axis=2)
    usable = jnp.concatenate(
        [
            jnp.ones(own.shape, bool),
            column_used & (column < own),
            slash_used & (slash >= 0) & jnp.logical_not(twice),
        ],
        axis=2,
    )
    width = 1 + NV + NS
    earlier = jnp.arange(width)[None, :] < jnp.arange(width)[:, None]
    place = jnp.sum(usable[:, :, None, :] & earlier, axis=3, dtype=jnp.int32)
    live = jnp.sum(usable, axis=2, dtype=jnp.int32)
    slot = jnp.arange(LMAX, dtype=jnp.int32)
    chosen = usable[:, :, None, :] & (place[:, :, None, :] == slot[:, None])
    packed = jnp.sum(jnp.where(chosen, blocks[:, :, None, :], 0), axis=3)
    packed = jnp.where(slot < live[:, :, None], packed, own)
    steps = (jnp.max(live, axis=1) + CB - 1) // CB
    return packed.reshape(-1), jnp.concatenate([steps, live.reshape(-1)])


def per_device(
    query_rows, key_rows, value_rows, column_blocks, column_count, slash_offsets, slash_count
):
    tokens = query_rows.shape[0]
    group = lax.axis_index("x")
    place = (lax.axis_index("z") * 2 + lax.axis_index("core")) * 4 + lax.axis_index("y")
    pairs = jnp.concatenate(
        [key_rows.reshape(tokens, KVH, DH), value_rows.reshape(tokens, KVH, DH)], axis=2
    )
    pairs = lax.all_to_all(pairs, "x", split_axis=1, concat_axis=0, tiled=True)
    pairs = pairs.reshape(QB * BLK, 2 * DH)
    queries = lax.all_to_all(
        query_rows.reshape(tokens, KVH, HG * DH), "x", split_axis=1, concat_axis=0, tiled=True
    ).reshape(QB * BLK, HG * DH)
    all_pairs = lax.all_gather(pairs, ("z", "core", "y"), axis=0, tiled=True)

    def mine(array):
        return lax.dynamic_slice_in_dim(array, group * HG, HG, 0)

    lists, counts = block_lists(
        place * QB, mine(column_blocks), mine(column_count), mine(slash_offsets), mine(slash_count)
    )
    outputs = attend(lists, counts, queries, all_pairs)
    returned = lax.all_to_all(
        outputs.reshape(KVH, tokens, HG * DH), "x", split_axis=0, concat_axis=2, tiled=True
    )
    return returned.reshape(tokens, H * DH)


def solution(mesh):
    fine = Mesh(mesh.devices.reshape(8, 2, 4, 4), ("z", "core", "y", "x"))
    split = P(("z", "core", "y", "x"), None)
    return jax.shard_map(
        per_device,
        mesh=fine,
        in_specs=(split, split, split, P(), P(), P(), P()),
        out_specs=split,
        check_vma=False,
    )
```

time: 694 us -> 172 us (0.25)
  the two profiles are of different devices: /device:TPU:1 before, /device:TPU:224 now
where the time goes in v1:
time: 172 us; the launch traced here: 171 us
  waiting for transfers between devices  83.8 us (49%)
  blocking collectives  29.7 us (17%)
  Pallas kernels  27.5 us (16%)
  between operations  13.5 us (8%)
  other arithmetic  6.93 us (4%)
  local copies, waits for them, and re-layouts  6.07 us (4%)
  starting transfers between devices  3.66 us (2%)
    all_gather x1, waiting for transfers between devices, per_device(): all_pairs = lax.all_gather(pairs, ('z', 'core', 'y'), axis=0, tiled=True)  77.8 us
    pallas_call x1, Pallas kernels, attend(): pl.pallas_call(attend_kernel, out_shape=jax.ShapeDtypeStruct((QB * BLK, H...  27.5 us
    all_to_all x1, blocking collectives, per_device(): lax.all_to_all(outputs.reshape(KVH, tokens, HG * DH), 'x', split_axis=0,...  18.8 us
    all_to_all x1, blocking collectives, per_device(): pairs = lax.all_to_all(pairs, 'x', split_axis=1, concat_axis=0, tiled=True)  10.9 us
    all_to_all x1, waiting for transfers between devices, per_device(): lax.all_to_all(query_rows.reshape(tokens, KVH, HG * DH), 'x', split_axis=...  5.97 us
    reduce_sum x1, other arithmetic, block_lists(): place = jnp.sum(usable[:, :, None, :] & earlier, axis=3, dtype=jnp.int32)  4.53 us
    all_to_all x1, starting transfers between devices, per_device(): lax.all_to_all(query_rows.reshape(tokens, KVH, HG * DH), 'x', split_axis=...  3.66 us
  transfers between devices with their start and end apart: 2, of which 2 were waited for; matrix products, arithmetic and copies ran while one was open for 5% of the time, Pallas kernels for 0%

profile of v1, /device:TPU:224, one launch (start us, length us, event | category | flops | bytes accessed | tf_op | source)
XLA Modules:
  0.0 171.1 jit_solution(2094433811268055877)
XLA Ops:
  6.5 0.0 copy-start
  6.5 0.0 copy-start.1
  6.5 0.0 all-gather.2.cloned.1.call-start
  6.5 0.9 copy-done
  7.4 0.9 copy_bitcast_fusion.1
  8.4 10.9 %all_to_all.45 = bf16[128,4,256]{2,0,1:T(8,128)(2,1)} all-to-all(bf16[128,4,256]{2,0,1:T(8,128)(2,1)S(1)} %pad_maximum_fusion), channel_id=1, replica_groups=mesh['z'=8,'core'=2,'y'=4,'x'=4] {'x'}, dimensions={1} | all-to-all | bytes 524288 | tf_op jit(solution)/shard_map/all_to_all | solution.py:179
  19.3 0.0 all-gather.2.cloned.1.call-update
  19.3 0.0 copy-done.1
  19.4 1.1 copy.31
  20.4 0.0 copy-start.2
  20.4 0.0 copy-start.3
  20.4 0.0 copy-start.4
  20.4 0.0 copy-start.5
  20.4 3.7 %all-to-all-start = ((bf16[128,4,1024]{2,0,1:T(8,128)(2,1)}), bf16[128,4,1024]{2,0,1:T(8,128)(2,1)S(1)}, u32[]{:S(2)}, u32[]{:S(2)}) async-start(bf16[128,4,1024]{2,0,1:T(8,128)(2,1)} %bitcast.31), calls=%async_computation | async-start | bytes 2097152 | tf_op jit(solution)/shard_map/all_to_all | solution.py:181
  24.1 0.0 copy-done.2
  24.1 0.1 constant_dynamic-slice_fusion
  24.2 0.1 copy.16
  24.3 0.0 copy-done.3
  24.3 0.1 constant_dynamic-slice_fusion.1
  24.3 0.1 copy.15
  24.4 0.1 broadcast_subtract_fusion
  24.5 0.1 broadcast_in_dim.21
  24.6 0.1 pad_add_fusion
  24.6 0.1 copy.19
  24.8 0.0 copy-done.4
  24.8 0.1 dynamic_slice.12
  24.9 0.0 copy-done.5
  24.9 0.1 dynamic_slice.14
  24.9 0.1 iota_compare_fusion.4
  25.0 0.2 and_reduce_fusion
  25.2 0.1 iota_compare_fusion.3
  25.3 0.1 compare_and_fusion
  25.4 0.1 not_and_fusion
  25.4 0.3 convert_reduce_fusion.1
  25.7 0.2 copy.18
  25.9 0.1 reshape.109
  26.0 4.5 %convert_reduce_fusion = s32[8,8,33]{1,2,0:T(8,128)S(1)} fusion(pred[33,33]{1,0:T(8,128)(4,1)S(1)} %iota_compare_fusion.2, pred[8,8,33]{2,1,0:T(8,128)(4,1)S(1)} %get-tuple-element.6), kind=kLoop, calls=%fused_computation.2 | loop fusion | flops 206976 | bytes 11649 | tf_op jit(solution)/shard_map/reduce_sum | solution.py:160
  30.5 1.1 select_reduce_fusion
  31.7 0.1 fusion.1
  31.7 0.1 select_n.26.lists
  31.8 0.1 reduce_max.9
  32.0 0.1 pad_add_fusion.2.counts
  32.1 6.0 %all-to-all-done = bf16[128,4,1024]{2,0,1:T(8,128)(2,1)S(1)} async-done(((bf16[128,4,1024]{2,0,1:T(8,128)(2,1)}), bf16[128,4,1024]{2,0,1:T(8,128)(2,1)S(1)}, u32[]{:S(2)}, u32[]{:S(2)}) %all-to-all-start) | async-done | bytes 1048608 | tf_op jit(solution)/shard_map/all_to_all | solution.py:181
  38.0 77.8 %all-gather.2.cloned.1.call-done.kv_hbm = bf16[32768,256]{1,0:T(8,128)(2,1)} async-done(((bf16[512,256]{1,0:T(8,128)(2,1)}), bf16[32768,256]{1,0:T(8,128)(2,1)}) %all-gather.2.cloned.1.call-update) | async-done | bytes 16777232 | tf_op jit(solution)/shard_map/all_gather | solution.py:184
  115.9 27.5 %shard_map.73 = bf16[512,1024]{1,0:T(8,128)(2,1)S(1)} custom-call(s32[2304]{0:T(1024)S(1)} %select_n.26.lists, s32[72]{0:T(128)S(1)} %pad_add_fusion.2.counts, bf16[512,1024]{1,0:T(8,128)(2,1)S(1)} %bitcast.32, bf16[32768,256]{1,0:T(8,128)(2,1)} %all-gather.2.cloned.1.call-done.kv_hbm), custom_call_target="tpu_custom_call" | custom-call | tf_op jit(solution)/shard_map/pallas_call | solution.py:127
  143.3 18.8 %all_to_all.46 = bf16[4,128,1024]{2,1,0:T(8,128)(2,1)S(1)} all-to-all(bf16[4,128,1024]{2,1,0:T(8,128)(2,1)S(1)} %bitcast.33), channel_id=1, replica_groups=mesh['z'=8,'core'=2,'y'=4,'x'=4] {'x'}, dimensions={0} | all-to-all | bytes 2097152 | tf_op jit(solution)/shard_map/all_to_all | solution.py:193
  162.1 0.8 copy.23
  163.0 1.3 copy.27
  (6 shorter events, 0.1 us)
Async XLA Ops:
  6.5 0.9 copy-start
  6.5 12.8 %copy-start.1 = (bf16[128,4096]{1,0:T(8,128)(2,1)S(1)}, bf16[128,4096]{1,0:T(8,128)(2,1)}, u32[]{:S(2)}) copy-start(bf16[128,4096]{1,0:T(8,128)(2,1)} %param.7) | copy-start | bytes 3145732
  6.5 109.3 %all-gather.2.cloned.1.call-start = ((), (), s32[]{:S(2)}) async-start(), calls=%async_computation.3 | async-start | bytes 17039360 | tf_op jit(solution)/shard_map/all_gather | solution.py:184
  20.4 3.7 %copy-start.2 = (s32[32,24]{0,1:T(8,128)S(1)}, s32[32,24]{0,1:T(8,128)}, u32[]{:S(2)}) copy-start(s32[32,24]{0,1:T(8,128)} %param.12) | copy-start | bytes 9220
  20.4 3.8 %copy-start.3 = (s32[32,8]{0,1:T(8,128)S(1)}, s32[32,8]{0,1:T(8,128)}, u32[]{:S(2)}) copy-start(s32[32,8]{0,1:T(8,128)} %param.10) | copy-start | bytes 3076
  20.4 4.4 %copy-start.4 = (s32[32]{0:T(128)S(1)}, s32[32]{0:T(128)}, u32[]{:S(2)}) copy-start(s32[32]{0:T(128)} %param.11) | copy-start | bytes 388
  20.4 4.5 %copy-start.5 = (s32[32]{0:T(128)S(1)}, s32[32]{0:T(128)}, u32[]{:S(2)}) copy-start(s32[32]{0:T(128)} %param.13) | copy-start | bytes 388
  20.4 17.6 %all-to-all-start = ((bf16[128,4,1024]{2,0,1:T(8,128)(2,1)}), bf16[128,4,1024]{2,0,1:T(8,128)(2,1)S(1)}, u32[]{:S(2)}, u32[]{:S(2)}) async-start(bf16[128,4,1024]{2,0,1:T(8,128)(2,1)} %bitcast.31), calls=%async_computation | async-start | bytes 2097152 | tf_op jit(solution)/shard_map/all_to_all | solution.py:181
Sparse Core Ops, SparseCore 0:
  19.5 96.3 all-gather.1

commit v2 on v1

--- a/solution.py
+++ b/solution.py
@@ -24,17 +24,40 @@
 C2 = math.log2(math.e) / math.sqrt(DH)
 NEG = -1e30
 NT = (((1,), (1,)), ((), ()))
-
-
-def attend_kernel(
-    lists, counts, q_ref, kv_hbm, o_ref, k_s, v_s, top_s, sum_s, acc_s, score_s, sem
-):
-    copy_k = pltpu.make_async_copy(kv_hbm.at[:, pl.ds(0, DH)], k_s, sem.at[0])
-    copy_v = pltpu.make_async_copy(kv_hbm.at[:, pl.ds(DH, DH)], v_s, sem.at[1])
-    copy_k.start()
-    copy_v.start()
-    copy_k.wait()
-    copy_v.wait()
+PIECE = SEQ // 8
+
+
+def attend_kernel(k_lists, v_lists, counts, q_ref, *refs):
+    held, swapped, o_ref = refs[:10], refs[10:20], refs[20]
+    k_s, v_s, top_s, sum_s, acc_s, score_s, sem = refs[21:]
+    is_first = counts[HG + HG * QB] == 0
+
+    def load(keys, values):
+        copies = []
+        for p in range(7):
+            copies.append((keys[p], k_s.at[pl.ds(p * PIECE, PIECE), :]))
+            copies.append((values[p], v_s.at[pl.ds(p * PIECE, PIECE), :]))
+        half = PIECE // 2
+        copies.append((keys[7], k_s.at[pl.ds(7 * PIECE, half), :]))
+        copies.append((keys[8], k_s.at[pl.ds(7 * PIECE + half, half), :]))
+        copies.append((values[9], v_s.at[pl.ds(7 * PIECE, PIECE), :]))
+        started = [
+            pltpu.make_async_copy(source, target, sem.at[n])
+            for n, (source, target) in enumerate(copies)
+        ]
+        for copy in started:
+            copy.start()
+        for copy in started:
+            copy.wait()
+
+    @pl.when(is_first)
+    def _():
+        load(held, swapped)
+
+    @pl.when(jnp.logical_not(is_first))
+    def _():
+        load(swapped, held)
+
     lane = lax.broadcasted_iota(jnp.int32, (BLK, CB * BLK), 1)
     row = lax.broadcasted_iota(jnp.int32, (BLK, CB * BLK), 0)
     lane_row = lax.broadcasted_iota(jnp.int32, (1, CB * BLK), 1)
@@ -45,7 +68,7 @@
     def head(h, _):
         columns = pl.ds(pl.multiple_of(h * DH, DH), DH)
 
-        def gather(ref, i, c):
+        def gather(ref, lists, i, c):
             base = (h * QB + i) * LMAX + c * CB
             return jnp.concatenate(
                 [
@@ -58,13 +81,13 @@
         def scores(i, c):
             return lax.dot_general(
                 q_ref[rows(i), columns],
-                gather(k_s, i, c),
+                gather(k_s, k_lists, i, c),
                 NT,
                 preferred_element_type=jnp.float32,
             )
 
         def weighted(i, c, p):
-            return jnp.dot(p, gather(v_s, i, c), preferred_element_type=jnp.float32)
+            return jnp.dot(p, gather(v_s, v_lists, i, c), preferred_element_type=jnp.float32)
 
         def first_weights(i, s):
             live = counts[HG + h * QB + i]
@@ -120,20 +143,20 @@
     lax.fori_loop(0, HG, head, 0)
 
 
-def attend(lists, counts, queries, pairs):
+def attend(k_lists, v_lists, counts, queries, held, swapped):
     any_space = pl.BlockSpec(memory_space=pl.ANY)
     vmem = pl.BlockSpec(memory_space=pltpu.VMEM)
     smem = pl.BlockSpec(memory_space=pltpu.SMEM)
     return pl.pallas_call(
         attend_kernel,
         out_shape=jax.ShapeDtypeStruct((QB * BLK, HG * DH), jnp.bfloat16),
-        in_specs=[smem, smem, vmem, any_space],
+        in_specs=[smem] * 3 + [vmem] + [any_space] * 20,
         out_specs=vmem,
         scratch_shapes=[pltpu.VMEM((SEQ, DH), jnp.bfloat16)] * 2
         + [pltpu.VMEM((QB * BLK, DH), jnp.float32)] * 3
-        + [pltpu.VMEM((QB * BLK, CB * BLK), jnp.float32), pltpu.SemaphoreType.DMA((2,))],
+        + [pltpu.VMEM((QB * BLK, CB * BLK), jnp.float32), pltpu.SemaphoreType.DMA((17,))],
         compiler_params=pltpu.CompilerParams(vmem_limit_bytes=40 * 1024 * 1024),
-    )(lists, counts, queries, pairs)
+    )(k_lists, v_lists, counts, queries, *held, *swapped)
 
 
 def block_lists(first_block, column_blocks, column_count, slash_offsets, slash_count):
@@ -164,7 +187,77 @@
     packed = jnp.sum(jnp.where(chosen, blocks[:, :, None, :], 0), axis=3)
     packed = jnp.where(slot < live[:, :, None], packed, own)
     steps = (jnp.max(live, axis=1) + CB - 1) // CB
-    return packed.reshape(-1), jnp.concatenate([steps, live.reshape(-1)])
+    return packed, steps, live
+
+
+def ring_place(d, size):
+    return jnp.where(d < size // 2, 2 * d, 2 * size - 1 - 2 * d)
+
+
+def piece_places(blocks, z, y):
+    dz = ring_place((blocks // 64 - z) % 8, 8)
+    dy = (blocks // 8 % 4 - y) % 4
+    inner = blocks // 32 % 2 * 8 + blocks % 8
+    keys = dz * 64 + ring_place(dy, 4) * 16 + inner
+    far = dz // 4
+    piece = jnp.where(
+        dy == 0,
+        7 * far,
+        jnp.where(dy == 3, 1 + 2 * far, jnp.where(dy == 1, 2 + 2 * far, 5 + far)),
+    )
+    values = piece * 64 + dz % 4 * 16 + inner
+    return keys, values
+
+
+def device_index(z, core, y, x):
+    return ((z * 2 + core) * 4 + y) * 4 + x
+
+
+def send(array, first, second):
+    pairs = []
+    for z in range(8):
+        for y in range(4):
+            for x in range(4):
+                for core, way in enumerate((first, second)):
+                    if way is not None:
+                        dz, dc, dy = way
+                        pairs.append(
+                            (
+                                device_index(z, core, y, x),
+                                device_index((z + dz) % 8, core ^ dc, (y + dy) % 4, x),
+                            )
+                        )
+    return lax.ppermute(array, AXES, pairs)
+
+
+UP_Z, DOWN_Z, UP_Y, DOWN_Y, OTHER = (1, 0, 0), (-1, 0, 0), (0, 0, 1), (0, 0, -1), (0, 1, 0)
+AXES = ("z", "core", "y", "x")
+
+
+def gather_pairs(own):
+    is_first = lax.axis_index("core") == 0
+    half = PIECE // 2
+    up1 = send(own, UP_Y, UP_Z)
+    down1 = send(own, DOWN_Y, DOWN_Z)
+    up2 = send(up1, UP_Y, UP_Z)
+    near = jnp.concatenate([own, up1, down1, up2])
+    down2 = send(down1, None, DOWN_Z)
+    up3 = send(up2, None, UP_Z)
+    a1 = send(near, UP_Z, UP_Y)
+    b1 = send(near, DOWN_Z, DOWN_Y)
+    down3 = send(down2, None, DOWN_Z)
+    up4 = send(up3, None, UP_Z)
+    far = jnp.concatenate([down2, up3, down3, up4])
+    a2 = send(jnp.where(is_first, a1, far), UP_Z, UP_Y)
+    b2 = send(jnp.where(is_first, b1, far), DOWN_Z, DOWN_Y)
+    a3 = send(jnp.where(is_first, a2, a1), UP_Z, UP_Y)
+    b3 = send(b2, DOWN_Z, DOWN_Y)
+    a4 = send(a3[:half], UP_Z, None)
+    b4 = send(b3[half:], DOWN_Z, None)
+    held = (near, a1, b1, a2, b2, a3, b3)
+    swapped = tuple(send(piece, OTHER, OTHER) for piece in held)
+    ends = (send(a4, OTHER, None), send(b4, OTHER, None), send(far, None, OTHER))
+    return held + (a4, b4, far), swapped + ends
 
 
 def per_device(
@@ -172,24 +265,32 @@
 ):
     tokens = query_rows.shape[0]
     group = lax.axis_index("x")
-    place = (lax.axis_index("z") * 2 + lax.axis_index("core")) * 4 + lax.axis_index("y")
+    z, core, y = (lax.axis_index(name) for name in ("z", "core", "y"))
     pairs = jnp.concatenate(
-        [key_rows.reshape(tokens, KVH, DH), value_rows.reshape(tokens, KVH, DH)], axis=2
-    )
-    pairs = lax.all_to_all(pairs, "x", split_axis=1, concat_axis=0, tiled=True)
-    pairs = pairs.reshape(QB * BLK, 2 * DH)
+        [
+            array.reshape(tokens, KVH, DH).transpose(1, 0, 2)
+            for array in (key_rows, value_rows)
+        ]
+    )
+    own = lax.all_to_all(pairs, ("core", "x"), split_axis=0, concat_axis=0, tiled=True)
+    held, swapped = gather_pairs(own.reshape(8 * tokens, DH))
     queries = lax.all_to_all(
         query_rows.reshape(tokens, KVH, HG * DH), "x", split_axis=1, concat_axis=0, tiled=True
     ).reshape(QB * BLK, HG * DH)
-    all_pairs = lax.all_gather(pairs, ("z", "core", "y"), axis=0, tiled=True)
 
     def mine(array):
         return lax.dynamic_slice_in_dim(array, group * HG, HG, 0)
 
-    lists, counts = block_lists(
-        place * QB, mine(column_blocks), mine(column_count), mine(slash_offsets), mine(slash_count)
-    )
-    outputs = attend(lists, counts, queries, all_pairs)
+    blocks, steps, live = block_lists(
+        ((z * 2 + core) * 4 + y) * QB,
+        mine(column_blocks),
+        mine(column_count),
+        mine(slash_offsets),
+        mine(slash_count),
+    )
+    k_lists, v_lists = piece_places(blocks, z, y)
+    counts = jnp.concatenate([steps, live.reshape(-1), core[None]])
+    outputs = attend(k_lists.reshape(-1), v_lists.reshape(-1), counts, queries, held, swapped)
     returned = lax.all_to_all(
         outputs.reshape(KVH, tokens, HG * DH), "x", split_axis=0, concat_axis=2, tiled=True
     )

time: 172 us -> 163 us (0.948)
  waiting for transfers between devices: 83.8 us -> 43.7 us
  starting transfers between devices: 3.66 us -> 38.1 us
  between operations: 13.5 us -> 0.31 us
  local copies, waits for them, and re-layouts: 6.07 us -> 11.8 us
  other arithmetic: 6.93 us -> 10.8 us
    all_gather x1 -> x0, waiting for transfers between devices: 77.8 us -> none  [per_device(): all_pairs = lax.all_gather(pairs, ('z', 'core', 'y'), axis=0, tiled=True)]
    ppermute x0 -> x25, waiting for transfers between devices: none -> 43.7 us  [send(): return lax.ppermute(array, AXES, pairs)]
    ppermute x0 -> x25, starting transfers between devices: none -> 33.7 us  [send(): return lax.ppermute(array, AXES, pairs)]
    all_to_all x1, waiting for transfers between devices: 5.97 us -> 0.01 us  [per_device(): lax.all_to_all(query_rows.reshape(tokens, KVH, HG * DH), 'x', split_axis=...]
    slice x0 -> x2, local copies, waits for them, and re-layouts: none -> 3.73 us  [the longest x1 1.87 us: gather_pairs(): a4 = send(a3[:half], UP_Z, None)]
    select_n x0 -> x2, other arithmetic: none -> 3.71 us  [the longest x1 2.32 us: gather_pairs(): a3 = send(jnp.where(is_first, a2, a1), UP_Z, UP_Y)]
    unnamed x13 -> x16, local copies, waits for them, and re-layouts: 2.25 us -> 4.25 us
  transfers between devices with their start and end apart: 2 -> 26, of which waited for: 2 -> 8; matrix products, arithmetic and copies ran while one was open for 5% -> 11% of each run, Pallas kernels for 0% -> 0%
where the time goes in v2:
time: 163 us; the launch traced here: 162 us
  waiting for transfers between devices  43.7 us (27%)
  starting transfers between devices  38.1 us (23%)
  blocking collectives  30.8 us (19%)
  Pallas kernels  26.8 us (16%)
  local copies, waits for them, and re-layouts  11.8 us (7%)
  other arithmetic  10.8 us (7%)
    ppermute x25, waiting for transfers between devices, send(): return lax.ppermute(array, AXES, pairs)  43.7 us
    ppermute x25, starting transfers between devices, send(): return lax.ppermute(array, AXES, pairs)  33.7 us
    pallas_call x1, Pallas kernels, attend(): pl.pallas_call(attend_kernel, out_shape=jax.ShapeDtypeStruct((QB * BLK, H...  26.8 us
    all_to_all x1, blocking collectives, per_device(): lax.all_to_all(outputs.reshape(KVH, tokens, HG * DH), 'x', split_axis=0,...  19.8 us
    all_to_all x1, blocking collectives, per_device(): lax.all_to_all(pairs, ('core', 'x'), split_axis=0, concat_axis=0, tiled=T...  11 us
    reduce_sum x1, other arithmetic, block_lists(): place = jnp.sum(usable[:, :, None, :] & earlier, axis=3, dtype=jnp.int32)  4.53 us
    all_to_all x1, starting transfers between devices, per_device(): lax.all_to_all(query_rows.reshape(tokens, KVH, HG * DH), 'x', split_axis=...  4.41 us
    unnamed x16, local copies, waits for them, and re-layouts  4.25 us
  transfers between devices with their start and end apart: 26, of which 8 were waited for; matrix products, arithmetic and copies ran while one was open for 11% of the time, Pallas kernels for 0%

profile of v2, /device:TPU:224, one launch (start us, length us, event | category | flops | bytes accessed | tf_op | source)
XLA Modules:
  0.0 162.3 jit_solution(2513252284527993862)
XLA Ops:
  0.0 0.9 copy-done
  0.9 0.9 bitcast_bitcast_fusion
  1.9 11.0 %all_to_all.35 = bf16[8,128,128]{2,1,0:T(8,128)(2,1)S(1)} all-to-all(bf16[8,128,128]{2,1,0:T(8,128)(2,1)S(1)} %pad_maximum_fusion.1), channel_id=1, replica_groups=mesh['z'=8,'core'=2,'y'=4,'x'=4] {'core','x'}, dimensions={0} | all-to-all | bytes 524288 | tf_op jit(solution)/shard_map/all_to_all | solution.py:275
  12.9 1.6 collective-permute-start
  14.5 1.7 %collective-permute-start.1 = (bf16[1024,128]{1,0:T(8,128)(2,1)S(1)}, bf16[1024,128]{1,0:T(8,128)(2,1)S(1)}, u32[]{:S(2)}, u32[]{:S(2)}) collective-permute-start(bf16[1024,128]{1,0:T(8,128)(2,1)S(1)} %bitcast.39), channel_id=1, source_target_pairs={{0,12},{16,240},{1,13},{17,241},{2,14},{18,242},{3,15},{19,243},{4... | collective-permute-start | bytes 786440 | tf_op jit(solution)/shard_map/ppermute | solution.py:230
  16.1 4.3 %collective-permute-done = bf16[1024,128]{1,0:T(8,128)(2,1)S(1)} collective-permute-done((bf16[1024,128]{1,0:T(8,128)(2,1)S(1)}, bf16[1024,128]{1,0:T(8,128)(2,1)S(1)}, u32[]{:S(2)}, u32[]{:S(2)}) %collective-permute-start) | collective-permute-done | bytes 262176 | tf_op jit(solution)/shard_map/ppermute | solution.py:230
  20.5 0.4 collective-permute-start.2
  20.9 7.2 %collective-permute-done.2 = bf16[1024,128]{1,0:T(8,128)(2,1)S(1)} collective-permute-done((bf16[1024,128]{1,0:T(8,128)(2,1)S(1)}, bf16[1024,128]{1,0:T(8,128)(2,1)S(1)}, u32[]{:S(2)}, u32[]{:S(2)}) %collective-permute-start.2) | collective-permute-done | bytes 262176 | tf_op jit(solution)/shard_map/ppermute | solution.py:230
  28.2 1.1 collective-permute-start.4
  29.2 2.2 %collective-permute-start.3 = (bf16[4096,128]{1,0:T(8,128)(2,1)S(1)}, bf16[4096,128]{1,0:T(8,128)(2,1)S(1)}, u32[]{:S(2)}, u32[]{:S(2)}) collective-permute-start(bf16[4096,128]{1,0:T(8,128)(2,1)S(1)} %pad_maximum_fusion.refs_0_), channel_id=1, source_target_pairs={{0,32},{16,20},{1,33},{17,21},{2,34},{18,22},{3,35},{19,23},{4,36}... | collective-permute-start | bytes 3145736 | tf_op jit(solution)/shard_map/ppermute | solution.py:230
  31.5 1.4 collective-permute-start.5
  32.8 0.7 collective-permute-start.6
  33.5 1.4 collective-permute-start.7
  34.9 0.7 collective-permute-start.8
  35.5 1.0 constant_dynamic-update-slice_fusion.3
  36.6 1.0 constant_dynamic-update-slice_fusion.1
  37.6 11.8 %collective-permute-done.4.refs_2_ = bf16[4096,128]{1,0:T(8,128)(2,1)} collective-permute-done((bf16[4096,128]{1,0:T(8,128)(2,1)S(1)}, bf16[4096,128]{1,0:T(8,128)(2,1)}, u32[]{:S(2)}, u32[]{:S(2)}) %collective-permute-start.4) | collective-permute-done | bytes 1048608 | tf_op jit(solution)/shard_map/ppermute | solution.py:230
  49.4 1.4 broadcast_select_fusion.1
  50.9 3.2 %collective-permute-start.9 = (bf16[4096,128]{1,0:T(8,128)(2,1)S(1)}, bf16[4096,128]{1,0:T(8,128)(2,1)}, u32[]{:S(2)}, u32[]{:S(2)}) collective-permute-start(bf16[4096,128]{1,0:T(8,128)(2,1)S(1)} %get-tuple-element.8), channel_id=1, source_target_pairs={{0,32},{16,20},{1,33},{17,21},{2,34},{18,22},{3,35},{19,23},{4,36}... | collective-permute-start | bytes 3145736 | tf_op jit(solution)/shard_map/ppermute | solution.py:230
  54.1 12.9 %collective-permute-done.10.refs_4_ = bf16[4096,128]{1,0:T(8,128)(2,1)} collective-permute-done((bf16[4096,128]{1,0:T(8,128)(2,1)S(1)}, bf16[4096,128]{1,0:T(8,128)(2,1)}, u32[]{:S(2)}, u32[]{:S(2)}) %collective-permute-start.10) | collective-permute-done | bytes 1048608 | tf_op jit(solution)/shard_map/ppermute | solution.py:230
  67.0 2.3 %broadcast_select_fusion = bf16[4096,128]{1,0:T(8,128)(2,1)} fusion(bf16[4096,128]{1,0:T(8,128)(2,1)} %collective-permute-done.9.refs_3_, bf16[4096,128]{1,0:T(8,128)(2,1)S(1)} %collective-permute-done.3.refs_1_, pred[]{:T(512)S(6)} %eq.53), kind=kLoop, calls=%fused_computation.6 | loop fusion | flops 524288 | bytes 3145729 | tf_op jit(solution)/shard_map/jit(_where)/select_n | solution.py:253
  69.3 3.2 %collective-permute-start.11 = (bf16[4096,128]{1,0:T(8,128)(2,1)}, bf16[4096,128]{1,0:T(8,128)(2,1)}, u32[]{:S(2)}, u32[]{:S(2)}) collective-permute-start(bf16[4096,128]{1,0:T(8,128)(2,1)} %broadcast_select_fusion), channel_id=1, source_target_pairs={{0,32},{16,20},{1,33},{17,21},{2,34},{18,22},{3,35},{19,23},{4,36}... | collective-permute-start | bytes 3145736 | tf_op jit(solution)/shard_map/ppermute | solution.py:230
  72.5 1.1 copy.31
  73.6 4.4 %all-to-all-start = ((bf16[128,4,1024]{2,0,1:T(8,128)(2,1)}), bf16[128,4,1024]{2,0,1:T(8,128)(2,1)}, u32[]{:S(2)}, u32[]{:S(2)}) async-start(bf16[128,4,1024]{2,0,1:T(8,128)(2,1)} %bitcast.34), calls=%async_computation | async-start | bytes 2097152 | tf_op jit(solution)/shard_map/all_to_all | solution.py:277
  78.8 1.3 collective-permute-start.24
  80.1 2.1 %collective-permute-start.17 = (bf16[4096,128]{1,0:T(8,128)(2,1)}, bf16[4096,128]{1,0:T(8,128)(2,1)}, u32[]{:S(2)}, u32[]{:S(2)}) collective-permute-start(bf16[4096,128]{1,0:T(8,128)(2,1)} %collective-permute-done.4.refs_2_), channel_id=1, source_target_pairs={{0,16},{16,0},{1,17},{17,1},{2,18},{18,2},{3,19},{19,3},{4,20},{20... | collective-permute-start | bytes 3145736 | tf_op jit(solution)/shard_map/ppermute | solution.py:230
  82.2 1.1 collective-permute-done.12.refs_6_
  83.3 1.9 %collective-permute-done.11.refs_5_ = bf16[4096,128]{1,0:T(8,128)(2,1)} collective-permute-done((bf16[4096,128]{1,0:T(8,128)(2,1)}, bf16[4096,128]{1,0:T(8,128)(2,1)}, u32[]{:S(2)}, u32[]{:S(2)}) %collective-permute-start.11) | collective-permute-done | bytes 1048608 | tf_op jit(solution)/shard_map/ppermute | solution.py:230
  85.2 0.2 and_reduce_fusion
  85.5 0.3 convert_reduce_fusion.1
  86.0 0.2 copy.18
  86.3 0.1 copy.19
  86.5 4.5 %convert_reduce_fusion = s32[8,8,33]{1,2,0:T(8,128)S(1)} fusion(pred[33,33]{1,0:T(8,128)(4,1)S(1)} %iota_compare_fusion.2, pred[8,8,33]{2,1,0:T(8,128)(4,1)S(1)} %get-tuple-element.6), kind=kLoop, calls=%fused_computation.2 | loop fusion | flops 206976 | bytes 11649 | tf_op jit(solution)/shard_map/reduce_sum | solution.py:183
  91.0 1.9 %slice.9 = bf16[2048,128]{1,0:T(8,128)(2,1)} slice(bf16[4096,128]{1,0:T(8,128)(2,1)} %collective-permute-done.12.refs_6_), slice={[2048:4096], [0:128]} | slice | bytes 1048576 | tf_op jit(solution)/shard_map/slice | solution.py:256
  92.9 1.9 %slice.8 = bf16[2048,128]{1,0:T(8,128)(2,1)} slice(bf16[4096,128]{1,0:T(8,128)(2,1)} %collective-permute-done.11.refs_5_), slice={[0:2048], [0:128]} | slice | bytes 1048576 | tf_op jit(solution)/shard_map/slice | solution.py:255
  94.8 0.5 collective-permute-start.18
  95.3 1.9 %collective-permute-start.14 = (bf16[2048,128]{1,0:T(8,128)(2,1)}, bf16[2048,128]{1,0:T(8,128)(2,1)}, u32[]{:S(2)}, u32[]{:S(2)}) collective-permute-start(bf16[2048,128]{1,0:T(8,128)(2,1)} %slice.9), channel_id=1, source_target_pairs={{0,224},{1,225},{2,226},{3,227},{4,228},{5,229},{6,230},{7,231},{8... | collective-permute-start | bytes 1572872 | tf_op jit(solution)/shard_map/ppermute | solution.py:230
  97.2 5.6 %collective-permute-start.13 = (bf16[2048,128]{1,0:T(8,128)(2,1)}, bf16[2048,128]{1,0:T(8,128)(2,1)}, u32[]{:S(2)}, u32[]{:S(2)}) collective-permute-start(bf16[2048,128]{1,0:T(8,128)(2,1)} %slice.8), channel_id=1, source_target_pairs={{0,32},{1,33},{2,34},{3,35},{4,36},{5,37},{6,38},{7,39},{8,40},{9,... | collective-permute-start | bytes 1572872 | tf_op jit(solution)/shard_map/ppermute | solution.py:230
  102.9 0.5 collective-permute-start.20
  103.4 1.1 select_reduce_fusion
  104.8 3.6 %collective-permute-done.14.refs_8_ = bf16[2048,128]{1,0:T(8,128)(2,1)} collective-permute-done((bf16[2048,128]{1,0:T(8,128)(2,1)}, bf16[2048,128]{1,0:T(8,128)(2,1)}, u32[]{:S(2)}, u32[]{:S(2)}) %collective-permute-start.14) | collective-permute-done | bytes 524320 | tf_op jit(solution)/shard_map/ppermute | solution.py:230
  108.3 2.1 %collective-permute-start.23 = (bf16[2048,128]{1,0:T(8,128)(2,1)}, bf16[2048,128]{1,0:T(8,128)(2,1)}, u32[]{:S(2)}, u32[]{:S(2)}) collective-permute-start(bf16[2048,128]{1,0:T(8,128)(2,1)} %collective-permute-done.14.refs_8_), channel_id=1, source_target_pairs={{0,16},{1,17},{2,18},{3,19},{4,20},{5,21},{6,22},{7,23},{8,24},{9,... | collective-permute-start | bytes 1572872 | tf_op jit(solution)/shard_map/ppermute | solution.py:230
  110.4 2.1 %collective-permute-start.22 = (bf16[2048,128]{1,0:T(8,128)(2,1)}, bf16[2048,128]{1,0:T(8,128)(2,1)}, u32[]{:S(2)}, u32[]{:S(2)}) collective-permute-start(bf16[2048,128]{1,0:T(8,128)(2,1)} %collective-permute-done.13.refs_7_), channel_id=1, source_target_pairs={{0,16},{1,17},{2,18},{3,19},{4,20},{5,21},{6,22},{7,23},{8,24},{9,... | collective-permute-start | bytes 1572872 | tf_op jit(solution)/shard_map/ppermute | solution.py:230
  112.7 0.9 collective-permute-done.22.refs_17_
  113.6 26.8 %shard_map.73 = bf16[512,1024]{1,0:T(8,128)(2,1)S(1)} custom-call(s32[2304]{0:T(1024)S(1)} %get-tuple-element.10.k_lists, s32[2304]{0:T(1024)S(1)} %get-tuple-element.9.v_lists, s32[73]{0:T(128)S(1)} %pad_add_fusion.2.counts, bf16[512,1024]{1,0:T(8,128)(2,1)} %bitcast.3.q_ref, bf16[4096,128]{1,0:T(8,128)(2,1)S(1)} %pad_maximum_fusion.refs_0_, ...), custom_call_target="tpu_custom_call" | custom-call | tf_op jit(solution)/shard_map/pallas_call | solution.py:150
  140.4 19.8 %all_to_all.36 = bf16[4,128,1024]{2,1,0:T(8,128)(2,1)S(1)} all-to-all(bf16[4,128,1024]{2,1,0:T(8,128)(2,1)S(1)} %bitcast.33), channel_id=1, replica_groups=mesh['z'=8,'core'=2,'y'=4,'x'=4] {'x'}, dimensions={0} | all-to-all | bytes 2097152 | tf_op jit(solution)/shard_map/all_to_all | solution.py:294
  160.2 0.8 copy.23
  161.0 1.3 copy.27
  (63 shorter events, 2.0 us)
Async XLA Ops:
  0.0 0.9 copy-start
  12.9 7.6 %collective-permute-start = (bf16[1024,128]{1,0:T(8,128)(2,1)S(1)}, bf16[1024,128]{1,0:T(8,128)(2,1)S(1)}, u32[]{:S(2)}, u32[]{:S(2)}) collective-permute-start(bf16[1024,128]{1,0:T(8,128)(2,1)S(1)} %bitcast.38), channel_id=1, source_target_pairs={{0,4},{16,48},{1,5},{17,49},{2,6},{18,50},{3,7},{19,51},{4,8},{20,... | collective-permute-start | bytes 786440 | tf_op jit(solution)/shard_map/ppermute | solution.py:230
  14.5 6.4 %collective-permute-start.1 = (bf16[1024,128]{1,0:T(8,128)(2,1)S(1)}, bf16[1024,128]{1,0:T(8,128)(2,1)S(1)}, u32[]{:S(2)}, u32[]{:S(2)}) collective-permute-start(bf16[1024,128]{1,0:T(8,128)(2,1)S(1)} %bitcast.39), channel_id=1, source_target_pairs={{0,12},{16,240},{1,13},{17,241},{2,14},{18,242},{3,15},{19,243},{4... | collective-permute-start | bytes 786440 | tf_op jit(solution)/shard_map/ppermute | solution.py:230
  20.5 7.6 %collective-permute-start.2 = (bf16[1024,128]{1,0:T(8,128)(2,1)S(1)}, bf16[1024,128]{1,0:T(8,128)(2,1)S(1)}, u32[]{:S(2)}, u32[]{:S(2)}) collective-permute-start(bf16[1024,128]{1,0:T(8,128)(2,1)S(1)} %collective-permute-done), channel_id=1, source_target_pairs={{0,4},{16,48},{1,5},{17,49},{2,6},{18,50},{3,7},{19,51},{4,8},{20,... | collective-permute-start | bytes 786440 | tf_op jit(solution)/shard_map/ppermute | solution.py:230
  28.2 21.2 %collective-permute-start.4 = (bf16[4096,128]{1,0:T(8,128)(2,1)S(1)}, bf16[4096,128]{1,0:T(8,128)(2,1)}, u32[]{:S(2)}, u32[]{:S(2)}) collective-permute-start(bf16[4096,128]{1,0:T(8,128)(2,1)S(1)} %pad_maximum_fusion.refs_0_), channel_id=1, source_target_pairs={{0,224},{16,28},{1,225},{17,29},{2,226},{18,30},{3,227},{19,31},{4... | collective-permute-start | bytes 3145736 | tf_op jit(solution)/shard_map/ppermute | solution.py:230
  29.2 20.2 %collective-permute-start.3 = (bf16[4096,128]{1,0:T(8,128)(2,1)S(1)}, bf16[4096,128]{1,0:T(8,128)(2,1)S(1)}, u32[]{:S(2)}, u32[]{:S(2)}) collective-permute-start(bf16[4096,128]{1,0:T(8,128)(2,1)S(1)} %pad_maximum_fusion.refs_0_), channel_id=1, source_target_pairs={{0,32},{16,20},{1,33},{17,21},{2,34},{18,22},{3,35},{19,23},{4,36}... | collective-permute-start | bytes 3145736 | tf_op jit(solution)/shard_map/ppermute | solution.py:230
  31.5 2.0 %collective-permute-start.5 = (bf16[1024,128]{1,0:T(8,128)(2,1)S(1)}, bf16[1024,128]{1,0:T(8,128)(2,1)}, u32[]{:S(2)}, u32[]{:S(2)}) collective-permute-start(bf16[1024,128]{1,0:T(8,128)(2,1)S(1)} %collective-permute-done.1), channel_id=1, source_target_pairs={{16,240},{17,241},{18,242},{19,243},{20,244},{21,245},{22,246},{23... | collective-permute-start | bytes 786440 | tf_op jit(solution)/shard_map/ppermute | solution.py:230
  32.8 2.0 %collective-permute-start.6 = (bf16[1024,128]{1,0:T(8,128)(2,1)S(1)}, bf16[1024,128]{1,0:T(8,128)(2,1)S(1)}, u32[]{:S(2)}, u32[]{:S(2)}) collective-permute-start(bf16[1024,128]{1,0:T(8,128)(2,1)S(1)} %collective-permute-done.2), channel_id=1, source_target_pairs={{16,48},{17,49},{18,50},{19,51},{20,52},{21,53},{22,54},{23,55},{2... | collective-permute-start | bytes 786440 | tf_op jit(solution)/shard_map/ppermute | solution.py:230
  33.5 3.1 %collective-permute-start.7 = (bf16[1024,128]{1,0:T(8,128)(2,1)}, bf16[1024,128]{1,0:T(8,128)(2,1)}, u32[]{:S(2)}, u32[]{:S(2)}) collective-permute-start(bf16[1024,128]{1,0:T(8,128)(2,1)} %collective-permute-done.5), channel_id=1, source_target_pairs={{16,240},{17,241},{18,242},{19,243},{20,244},{21,245},{22,246},{23... | collective-permute-start | bytes 786440 | tf_op jit(solution)/shard_map/ppermute | solution.py:230
  34.9 2.7 %collective-permute-start.8 = (bf16[1024,128]{1,0:T(8,128)(2,1)S(1)}, bf16[1024,128]{1,0:T(8,128)(2,1)S(1)}, u32[]{:S(2)}, u32[]{:S(2)}) collective-permute-start(bf16[1024,128]{1,0:T(8,128)(2,1)S(1)} %collective-permute-done.6), channel_id=1, source_target_pairs={{16,48},{17,49},{18,50},{19,51},{20,52},{21,53},{22,54},{23,55},{2... | collective-permute-start | bytes 786440 | tf_op jit(solution)/shard_map/ppermute | solution.py:230
  50.8 16.2 %collective-permute-start.10 = (bf16[4096,128]{1,0:T(8,128)(2,1)S(1)}, bf16[4096,128]{1,0:T(8,128)(2,1)}, u32[]{:S(2)}, u32[]{:S(2)}) collective-permute-start(bf16[4096,128]{1,0:T(8,128)(2,1)S(1)} %get-tuple-element.7), channel_id=1, source_target_pairs={{0,224},{16,28},{1,225},{17,29},{2,226},{18,30},{3,227},{19,31},{4... | collective-permute-start | bytes 3145736 | tf_op jit(solution)/shard_map/ppermute | solution.py:230
  50.9 21.6 %copy-start.1 = (bf16[128,4096]{1,0:T(8,128)(2,1)S(1)}, bf16[128,4096]{1,0:T(8,128)(2,1)}, u32[]{:S(2)}) copy-start(bf16[128,4096]{1,0:T(8,128)(2,1)} %param.7) | copy-start | bytes 3145732
  50.9 16.1 %collective-permute-start.9 = (bf16[4096,128]{1,0:T(8,128)(2,1)S(1)}, bf16[4096,128]{1,0:T(8,128)(2,1)}, u32[]{:S(2)}, u32[]{:S(2)}) collective-permute-start(bf16[4096,128]{1,0:T(8,128)(2,1)S(1)} %get-tuple-element.8), channel_id=1, source_target_pairs={{0,32},{16,20},{1,33},{17,21},{2,34},{18,22},{3,35},{19,23},{4,36}... | collective-permute-start | bytes 3145736 | tf_op jit(solution)/shard_map/ppermute | solution.py:230
  67.0 16.3 %collective-permute-start.12 = (bf16[4096,128]{1,0:T(8,128)(2,1)}, bf16[4096,128]{1,0:T(8,128)(2,1)}, u32[]{:S(2)}, u32[]{:S(2)}) collective-permute-start(bf16[4096,128]{1,0:T(8,128)(2,1)} %collective-permute-done.10.refs_4_), channel_id=1, source_target_pairs={{0,224},{16,28},{1,225},{17,29},{2,226},{18,30},{3,227},{19,31},{4... | collective-permute-start | bytes 3145736 | tf_op jit(solution)/shard_map/ppermute | solution.py:230
  69.3 15.9 %collective-permute-start.11 = (bf16[4096,128]{1,0:T(8,128)(2,1)}, bf16[4096,128]{1,0:T(8,128)(2,1)}, u32[]{:S(2)}, u32[]{:S(2)}) collective-permute-start(bf16[4096,128]{1,0:T(8,128)(2,1)} %broadcast_select_fusion), channel_id=1, source_target_pairs={{0,32},{16,20},{1,33},{17,21},{2,34},{18,22},{3,35},{19,23},{4,36}... | collective-permute-start | bytes 3145736 | tf_op jit(solution)/shard_map/ppermute | solution.py:230
  73.6 4.4 %copy-start.4 = (s32[32]{0:T(128)S(1)}, s32[32]{0:T(128)}, u32[]{:S(2)}) copy-start(s32[32]{0:T(128)} %param.11) | copy-start | bytes 388
  73.6 4.5 %copy-start.5 = (s32[32]{0:T(128)S(1)}, s32[32]{0:T(128)}, u32[]{:S(2)}) copy-start(s32[32]{0:T(128)} %param.13) | copy-start | bytes 388
  73.6 4.6 %copy-start.3 = (s32[32,8]{0,1:T(8,128)S(1)}, s32[32,8]{0,1:T(8,128)}, u32[]{:S(2)}) copy-start(s32[32,8]{0,1:T(8,128)} %param.10) | copy-start | bytes 3076
  73.6 4.8 %copy-start.2 = (s32[32,24]{0,1:T(8,128)S(1)}, s32[32,24]{0,1:T(8,128)}, u32[]{:S(2)}) copy-start(s32[32,24]{0,1:T(8,128)} %param.12) | copy-start | bytes 9220
  73.6 39.0 %all-to-all-start = ((bf16[128,4,1024]{2,0,1:T(8,128)(2,1)}), bf16[128,4,1024]{2,0,1:T(8,128)(2,1)}, u32[]{:S(2)}, u32[]{:S(2)}) async-start(bf16[128,4,1024]{2,0,1:T(8,128)(2,1)} %bitcast.34), calls=%async_computation | async-start | bytes 2097152 | tf_op jit(solution)/shard_map/all_to_all | solution.py:277
  78.7 16.0 %collective-permute-start.15 = (bf16[4096,128]{1,0:T(8,128)(2,1)S(1)}, bf16[4096,128]{1,0:T(8,128)(2,1)}, u32[]{:S(2)}, u32[]{:S(2)}) collective-permute-start(bf16[4096,128]{1,0:T(8,128)(2,1)S(1)} %pad_maximum_fusion.refs_0_), channel_id=1, source_target_pairs={{0,16},{16,0},{1,17},{17,1},{2,18},{18,2},{3,19},{19,3},{4,20},{20... | collective-permute-start | bytes 3145736 | tf_op jit(solution)/shard_map/ppermute | solution.py:230
  78.8 16.5 %collective-permute-start.24 = (bf16[4096,128]{1,0:T(8,128)(2,1)S(1)}, bf16[4096,128]{1,0:T(8,128)(2,1)}, u32[]{:S(2)}, u32[]{:S(2)}) collective-permute-start(bf16[4096,128]{1,0:T(8,128)(2,1)S(1)} %constant_dynamic-update-slice_fusion.refs_9_), channel_id=1, source_target_pairs={{16,0},{17,1},{18,2},{19,3},{20,4},{21,5},{22,6},{23,7},{24,8},{25... | collective-permute-start | bytes 3145736 | tf_op jit(solution)/shard_map/ppermute | solution.py:230
  80.1 17.1 %collective-permute-start.17 = (bf16[4096,128]{1,0:T(8,128)(2,1)}, bf16[4096,128]{1,0:T(8,128)(2,1)}, u32[]{:S(2)}, u32[]{:S(2)}) collective-permute-start(bf16[4096,128]{1,0:T(8,128)(2,1)} %collective-permute-done.4.refs_2_), channel_id=1, source_target_pairs={{0,16},{16,0},{1,17},{17,1},{2,18},{18,2},{3,19},{19,3},{4,20},{20... | collective-permute-start | bytes 3145736 | tf_op jit(solution)/shard_map/ppermute | solution.py:230
  83.3 19.5 %collective-permute-start.16 = (bf16[4096,128]{1,0:T(8,128)(2,1)S(1)}, bf16[4096,128]{1,0:T(8,128)(2,1)}, u32[]{:S(2)}, u32[]{:S(2)}) collective-permute-start(bf16[4096,128]{1,0:T(8,128)(2,1)S(1)} %collective-permute-done.3.refs_1_), channel_id=1, source_target_pairs={{0,16},{16,0},{1,17},{17,1},{2,18},{18,2},{3,19},{19,3},{4,20},{20... | collective-permute-start | bytes 3145736 | tf_op jit(solution)/shard_map/ppermute | solution.py:230
  85.2 17.7 %collective-permute-start.19 = (bf16[4096,128]{1,0:T(8,128)(2,1)}, bf16[4096,128]{1,0:T(8,128)(2,1)}, u32[]{:S(2)}, u32[]{:S(2)}) collective-permute-start(bf16[4096,128]{1,0:T(8,128)(2,1)} %collective-permute-done.10.refs_4_), channel_id=1, source_target_pairs={{0,16},{16,0},{1,17},{17,1},{2,18},{18,2},{3,19},{19,3},{4,20},{20... | collective-permute-start | bytes 3145736 | tf_op jit(solution)/shard_map/ppermute | solution.py:230
  94.8 17.9 %collective-permute-start.18 = (bf16[4096,128]{1,0:T(8,128)(2,1)}, bf16[4096,128]{1,0:T(8,128)(2,1)}, u32[]{:S(2)}, u32[]{:S(2)}) collective-permute-start(bf16[4096,128]{1,0:T(8,128)(2,1)} %collective-permute-done.9.refs_3_), channel_id=1, source_target_pairs={{0,16},{16,0},{1,17},{17,1},{2,18},{18,2},{3,19},{19,3},{4,20},{20... | collective-permute-start | bytes 3145736 | tf_op jit(solution)/shard_map/ppermute | solution.py:230
  95.3 13.1 %collective-permute-start.14 = (bf16[2048,128]{1,0:T(8,128)(2,1)}, bf16[2048,128]{1,0:T(8,128)(2,1)}, u32[]{:S(2)}, u32[]{:S(2)}) collective-permute-start(bf16[2048,128]{1,0:T(8,128)(2,1)} %slice.9), channel_id=1, source_target_pairs={{0,224},{1,225},{2,226},{3,227},{4,228},{5,229},{6,230},{7,231},{8... | collective-permute-start | bytes 1572872 | tf_op jit(solution)/shard_map/ppermute | solution.py:230
  97.2 13.2 %collective-permute-start.13 = (bf16[2048,128]{1,0:T(8,128)(2,1)}, bf16[2048,128]{1,0:T(8,128)(2,1)}, u32[]{:S(2)}, u32[]{:S(2)}) collective-permute-start(bf16[2048,128]{1,0:T(8,128)(2,1)} %slice.8), channel_id=1, source_target_pairs={{0,32},{1,33},{2,34},{3,35},{4,36},{5,37},{6,38},{7,39},{8,40},{9,... | collective-permute-start | bytes 1572872 | tf_op jit(solution)/shard_map/ppermute | solution.py:230
  102.8 10.7 %collective-permute-start.21 = (bf16[4096,128]{1,0:T(8,128)(2,1)}, bf16[4096,128]{1,0:T(8,128)(2,1)}, u32[]{:S(2)}, u32[]{:S(2)}) collective-permute-start(bf16[4096,128]{1,0:T(8,128)(2,1)} %collective-permute-done.12.refs_6_), channel_id=1, source_target_pairs={{0,16},{16,0},{1,17},{17,1},{2,18},{18,2},{3,19},{19,3},{4,20},{20... | collective-permute-start | bytes 3145736 | tf_op jit(solution)/shard_map/ppermute | solution.py:230
  102.9 10.6 %collective-permute-start.20 = (bf16[4096,128]{1,0:T(8,128)(2,1)}, bf16[4096,128]{1,0:T(8,128)(2,1)}, u32[]{:S(2)}, u32[]{:S(2)}) collective-permute-start(bf16[4096,128]{1,0:T(8,128)(2,1)} %collective-permute-done.11.refs_5_), channel_id=1, source_target_pairs={{0,16},{16,0},{1,17},{17,1},{2,18},{18,2},{3,19},{19,3},{4,20},{20... | collective-permute-start | bytes 3145736 | tf_op jit(solution)/shard_map/ppermute | solution.py:230
  108.3 4.3 %collective-permute-start.23 = (bf16[2048,128]{1,0:T(8,128)(2,1)}, bf16[2048,128]{1,0:T(8,128)(2,1)}, u32[]{:S(2)}, u32[]{:S(2)}) collective-permute-start(bf16[2048,128]{1,0:T(8,128)(2,1)} %collective-permute-done.14.refs_8_), channel_id=1, source_target_pairs={{0,16},{1,17},{2,18},{3,19},{4,20},{5,21},{6,22},{7,23},{8,24},{9,... | collective-permute-start | bytes 1572872 | tf_op jit(solution)/shard_map/ppermute | solution.py:230
  110.4 3.1 %collective-permute-start.22 = (bf16[2048,128]{1,0:T(8,128)(2,1)}, bf16[2048,128]{1,0:T(8,128)(2,1)}, u32[]{:S(2)}, u32[]{:S(2)}) collective-permute-start(bf16[2048,128]{1,0:T(8,128)(2,1)} %collective-permute-done.13.refs_7_), channel_id=1, source_target_pairs={{0,16},{1,17},{2,18},{3,19},{4,20},{5,21},{6,22},{7,23},{8,24},{9,... | collective-permute-start | bytes 1572872 | tf_op jit(solution)/shard_map/ppermute | solution.py:230

commit v3 on v1

v3 whole, which is shorter than its diff:
```python
import math

import jax
import jax.numpy as jnp
from jax import lax
from jax.experimental import pallas as pl
from jax.experimental.pallas import tpu as pltpu
from jax.sharding import Mesh, PartitionSpec as P

H = 32
KVH = 4
DH = 128
BLK = 64
NV = 8
NS = 24
SEQ = 32768

QB = 8
HG = H // KVH
CB = 4
CHUNKS = -(-(1 + NV + NS) // CB)
LMAX = CHUNKS * CB
SKEW = 4
C2 = math.log2(math.e) / math.sqrt(DH)
NEG = -1e30
NT = (((1,), (1,)), ((), ()))
PIECE = SEQ // 8


def attend_kernel(k_lists, v_lists, counts, *refs):
    q_refs, held, swapped, o_refs = refs[:4], refs[4:12], refs[12:20], refs[20:24]
    k_s, v_s, top_s, sum_s, acc_s, score_s, sem = refs[24:]
    is_first = counts[HG + HG * QB] == 0

    def copies(source, target, first_sem):
        return [
            pltpu.make_async_copy(
                piece, target.at[pl.ds(p * PIECE, PIECE), :], sem.at[first_sem + p]
            )
            for p, piece in enumerate(source)
        ]

    @pl.when(is_first)
    def _():
        for copy in copies(held, k_s, 0) + copies(swapped, v_s, 8):
            copy.start()

    @pl.when(jnp.logical_not(is_first))
    def _():
        for copy in copies(swapped, k_s, 0) + copies(held, v_s, 8):
            copy.start()

    for copy in copies(held, k_s, 0):
        copy.wait()
    lane = lax.broadcasted_iota(jnp.int32, (BLK, CB * BLK), 1)
    row = lax.broadcasted_iota(jnp.int32, (BLK, CB * BLK), 0)
    lane_row = lax.broadcasted_iota(jnp.int32, (1, CB * BLK), 1)

    def rows(i):
        return slice(i * BLK, (i + 1) * BLK)

    def head(h, _):
        columns = pl.ds(pl.multiple_of(h * DH, DH), DH)

        def gather(ref, lists, i, c):
            base = c * (CB * HG * QB) + (h * QB + i)
            return jnp.concatenate(
                [
                    ref[pl.ds(pl.multiple_of(lists[base + j * (HG * QB)] * BLK, BLK), BLK), :]
                    for j in range(CB)
                ],
                axis=0,
            )

        def scores(i, c):
            return lax.dot_general(
                q_refs[i // 2][rows(i % 2), columns],
                gather(k_s, k_lists, i, c),
                NT,
                preferred_element_type=jnp.float32,
            )

        def weighted(i, c, p):
            return jnp.dot(p, gather(v_s, v_lists, i, c), preferred_element_type=jnp.float32)

        def first_weights(i, s):
            live = counts[HG + h * QB + i]
            s = jnp.where((lane < live * BLK) & ((lane >= BLK) | (lane <= row)), s, NEG)
            top = jnp.max(jnp.maximum(s[:, :128], s[:, 128:]), axis=1, keepdims=True)
            shift = top * C2
            parts = [jnp.exp2(s[:, t * 128 : (t + 1) * 128] * C2 - shift) for t in range(2)]
            top_s[rows(i), :] = jnp.broadcast_to(top, (BLK, DH))
            sum_s[rows(i), :] = parts[0] + parts[1]
            return jnp.concatenate([x.astype(jnp.bfloat16) for x in parts], axis=1)

        def next_weights(i, c, s):
            live = counts[HG + h * QB + i]
            s = s + jnp.where(lane_row < (live - c * CB) * BLK, 0.0, NEG)
            old = top_s[rows(i), :]
            top = jnp.maximum(
                old, jnp.max(jnp.maximum(s[:, :128], s[:, 128:]), axis=1, keepdims=True)
            )
            shrink = jnp.exp2((old - top) * C2)
            shift = top * C2
            parts = [jnp.exp2(s[:, t * 128 : (t + 1) * 128] * C2 - shift) for t in range(2)]
            top_s[rows(i), :] = top
            sum_s[rows(i), :] = sum_s[rows(i), :] * shrink + (parts[0] + parts[1])
            return jnp.concatenate([x.astype(jnp.bfloat16) for x in parts], axis=1), shrink

        opening = [scores(i, 0) for i in range(QB)]
        for i in range(QB):
            score_s[rows(i), :] = scores(i, 1)

        @pl.when(h == 0)
        def _():
            for copy in copies(held, v_s, 8):
                copy.wait()

        weights = [first_weights(i, s) for i, s in enumerate(opening)]
        for i, p in enumerate(weights):
            acc_s[rows(i), :] = weighted(i, 0, p)

        def chunk(c, _):
            ahead = jnp.minimum(c + 1, CHUNKS - 1)
            held = {}
            for t in range(QB + SKEW):
                if t < QB:
                    s = score_s[rows(t), :]
                    score_s[rows(t), :] = scores(t, ahead)
                    held[t] = next_weights(t, c, s)
                i = t - SKEW
                if i >= 0:
                    p, shrink = held.pop(i)
                    acc_s[rows(i), :] = acc_s[rows(i), :] * shrink + weighted(i, c, p)
            return 0

        lax.fori_loop(1, counts[h], chunk, 0)
        for i in range(QB):
            total = jnp.sum(sum_s[rows(i), :], axis=1, keepdims=True)
            o_refs[i // 2][rows(i % 2), columns] = (acc_s[rows(i), :] / total).astype(jnp.bfloat16)
        return 0

    lax.fori_loop(0, HG, head, 0)


def attend(k_lists, v_lists, counts, queries, held, swapped):
    any_space = pl.BlockSpec(memory_space=pl.ANY)
    vmem = pl.BlockSpec(memory_space=pltpu.VMEM)
    smem = pl.BlockSpec(memory_space=pltpu.SMEM)
    return pl.pallas_call(
        attend_kernel,
        out_shape=[jax.ShapeDtypeStruct((2 * BLK, HG * DH), jnp.bfloat16)] * 4,
        in_specs=[smem] * 3 + [vmem] * 4 + [any_space] * 16,
        out_specs=[vmem] * 4,
        scratch_shapes=[pltpu.VMEM((SEQ, DH), jnp.bfloat16)] * 2
        + [pltpu.VMEM((QB * BLK, DH), jnp.float32)] * 3
        + [pltpu.VMEM((QB * BLK, CB * BLK), jnp.float32), pltpu.SemaphoreType.DMA((16,))],
        compiler_params=pltpu.CompilerParams(vmem_limit_bytes=40 * 1024 * 1024),
    )(k_lists, v_lists, counts, *queries, *held, *swapped)


def place_kernel(starts, *refs):
    out_ref = refs[4]
    for n in range(4):
        columns = pl.ds(pl.multiple_of(starts[n] * (HG * DH), HG * DH), HG * DH)
        out_ref[:, columns] = refs[n][...]


def place_heads(starts, pieces):
    return pl.pallas_call(
        place_kernel,
        out_shape=jax.ShapeDtypeStruct((2 * BLK, H * DH), jnp.bfloat16),
        in_specs=[pl.BlockSpec(memory_space=pltpu.SMEM)]
        + [pl.BlockSpec(memory_space=pltpu.VMEM)] * 4,
        out_specs=pl.BlockSpec(memory_space=pltpu.VMEM),
    )(starts, *pieces)


def block_lists(own_blocks, column_blocks, column_count, slash_offsets, slash_count):
    own = jnp.tile(own_blocks, HG)[None, :]
    column = jnp.repeat(column_blocks.T, QB, axis=1)
    column_used = jnp.arange(NV, dtype=jnp.int32)[:, None] < jnp.repeat(column_count, QB)
    slash = own - jnp.repeat(slash_offsets.T, QB, axis=1)
    slash_used = jnp.arange(NS, dtype=jnp.int32)[:, None] < jnp.repeat(slash_count, QB)
    twice = jnp.any((column[None] == slash[:, None]) & column_used[None], axis=1)
    blocks = jnp.concatenate([own, column, slash])
    usable = jnp.concatenate(
        [
            jnp.ones(own.shape, bool),
            column_used & (column < own),
            slash_used & (slash >= 0) & jnp.logical_not(twice),
        ]
    )
    width = 1 + NV + NS
    earlier = jnp.arange(width)[None, :] < jnp.arange(width)[:, None]
    place = jnp.sum(usable[None] & earlier[:, :, None], axis=1, dtype=jnp.int32)
    live = jnp.sum(usable, axis=0, dtype=jnp.int32)
    slot = jnp.arange(LMAX, dtype=jnp.int32)
    chosen = usable[None] & (place[None] == slot[:, None, None])
    packed = jnp.sum(jnp.where(chosen, blocks[None], 0), axis=1)
    packed = jnp.where(slot[:, None] < live, packed, own)
    steps = (jnp.max(live.reshape(HG, QB), axis=1) + CB - 1) // CB
    return packed, steps, live


def piece_places(blocks, y, x):
    dy, dx = (blocks // 8 - y) % 4, (blocks // 2 - x) % 4
    inner = blocks // 32 * 2 + blocks % 2

    def place(small, big):
        slot = jnp.where(small < 2, 2 * small, 7 - 2 * small)
        far = slot // 2
        piece = jnp.where(
            big == 0,
            far,
            jnp.where(big == 3, 2 + 2 * far, jnp.where(big == 1, 3 + 2 * far, 6 + far)),
        )
        return piece * 64 + slot % 2 * 32 + inner

    return place(dx, dy), place(dy, dx)


def device_index(z, core, y, x):
    return ((z * 2 + core) * 4 + y) * 4 + x


def send(array, first, second=None):
    pairs = []
    for z in range(8):
        for y in range(4):
            for x in range(4):
                for core, (dz, dc, dy, dx) in enumerate((first, second or first)):
                    target = ((z + dz) % 8, core ^ dc, (y + dy) % 4, (x + dx) % 4)
                    pairs.append((device_index(z, core, y, x), device_index(*target)))
    return lax.ppermute(array, AXES, pairs)


AXES = ("z", "core", "y", "x")
UP_Y, DOWN_Y, UP_X, DOWN_X = (0, 0, 1, 0), (0, 0, -1, 0), (0, 0, 0, 1), (0, 0, 0, -1)
UP_Z, DOWN_Z, UP_2, DOWN_2 = (1, 0, 0, 0), (-1, 0, 0, 0), (2, 0, 0, 0), (-2, 0, 0, 0)
OTHER = (0, 1, 0, 0)


def gather_pairs(own, lists, late):
    up1 = send(own, UP_X, UP_Y)
    down1 = send(own, DOWN_X, DOWN_Y)
    up1, down1, lists = lax.optimization_barrier((up1, down1, lists))
    up2 = send(up1, UP_X, UP_Y)
    near = jnp.concatenate([own, up1])
    a1 = send(near, UP_Y, UP_X)
    b1 = send(near, DOWN_Y, DOWN_X)
    up2, late = lax.optimization_barrier((up2, late))
    far = jnp.concatenate([down1, up2])
    a2 = send(far, UP_Y, UP_X)
    b2 = send(far, DOWN_Y, DOWN_X)
    a3 = send(a1, UP_Y, UP_X)
    b3 = send(b2, DOWN_Y, DOWN_X)
    held = (near, far, a1, b1, a2, b2, a3, b3)
    return held, tuple(send(piece, OTHER) for piece in held), lists, late


def per_device(
    query_rows, key_rows, value_rows, column_blocks, column_count, slash_offsets, slash_count
):
    tokens = query_rows.shape[0]
    z, core, y, x = (lax.axis_index(name) for name in AXES)
    group = z % KVH
    pairs = jnp.stack(
        [array.reshape(tokens, KVH, DH).transpose(1, 0, 2) for array in (key_rows, value_rows)],
        axis=1,
    )
    own = lax.all_to_all(
        jnp.concatenate([pairs, pairs]).reshape(4 * KVH, tokens, DH),
        ("z", "core"),
        split_axis=0,
        concat_axis=0,
        tiled=True,
    ).reshape(16 * tokens, DH)

    def mine(array):
        return lax.dynamic_slice_in_dim(array, group * HG, HG, 0)

    last = jnp.where(core == 0, z + 6, z + 2)
    sources = jnp.stack([z, z + 7, z + 1, last]) % 8
    own_blocks = ((sources * 2 + core) * 32 + (y * 4 + x) * 2)[:, None] + jnp.arange(2)
    blocks, steps, live = block_lists(
        own_blocks.reshape(-1).astype(jnp.int32),
        mine(column_blocks),
        mine(column_count),
        mine(slash_offsets),
        mine(slash_count),
    )
    k_lists, v_lists = piece_places(blocks, y, x)
    counts = jnp.concatenate([steps, live, core[None]])
    lists = (k_lists.reshape(-1), v_lists.reshape(-1), counts)
    held, swapped, lists, query_rows = gather_pairs(own, lists, query_rows)

    def heads(step):
        start = (z + step) % KVH * (HG * DH)
        return lax.dynamic_slice_in_dim(query_rows, start, HG * DH, 1)

    queries = (
        heads(0),
        send(heads(1), UP_Z),
        send(heads(3), DOWN_Z),
        send(heads(2), UP_2, DOWN_2),
    )
    outputs = attend(*lists, queries, held, swapped)
    pieces = (
        outputs[0],
        send(outputs[1], DOWN_Z),
        send(outputs[2], UP_Z),
        send(outputs[3], DOWN_2, UP_2),
    )
    starts = jnp.stack([z, z + 1, z + 3, z + 2]) % KVH
    return place_heads(starts.astype(jnp.int32), pieces)


def solution(mesh):
    fine = Mesh(mesh.devices.reshape(8, 2, 4, 4), AXES)
    split = P(AXES, None)
    return jax.shard_map(
        per_device,
        mesh=fine,
        in_specs=(split, split, split, P(), P(), P(), P()),
        out_specs=split,
        check_vma=False,
    )
```

time: 172 us -> 160 us (0.930)
  the two profiles are of different devices: /device:TPU:224 before, /device:TPU:1 now
where the time goes in v3:
time: 160 us
  waiting for transfers between devices  89.5 us (56%)
  starting transfers between devices  33.1 us (21%)
  Pallas kernels  27.7 us (17%)
  local copies, waits for them, and re-layouts  7.89 us (5%)
  other arithmetic  2.04 us (1%)
    ppermute x23, waiting for transfers between devices, send(): return lax.ppermute(array, AXES, pairs)  74.5 us
    pallas_call x1, Pallas kernels, attend(): pl.pallas_call(attend_kernel, out_shape=[jax.ShapeDtypeStruct((2 * BLK, H...  25.4 us
    ppermute x23, starting transfers between devices, send(): return lax.ppermute(array, AXES, pairs)  23.1 us
    all_to_all x1, waiting for transfers between devices, per_device(): lax.all_to_all(jnp.concatenate([pairs, pairs]).reshape(4 * KVH, tokens, D...  15 us
    all_to_all x1, starting transfers between devices, per_device(): lax.all_to_all(jnp.concatenate([pairs, pairs]).reshape(4 * KVH, tokens, D...  9.98 us
  transfers between devices with their start and end apart: 24, of which 13 were waited for; matrix products, arithmetic and copies ran while one was open for 3% of the time, Pallas kernels for 0%

profile of v3, /device:TPU:1, one launch (start us, length us, event | category | flops | bytes accessed | tf_op | source)
XLA Modules:
  0.0 160.5 jit_solution(10682709580517494548)
XLA Ops:
  0.0 1.0 reshape.203
  1.0 0.9 reshape.204
  1.9 0.2 maximum_maximum_fusion
  2.2 0.9 copy.19
  3.1 10.0 %all-to-all-start = ((bf16[16,128,128]{2,1,0:T(8,128)(2,1)}), bf16[16,128,128]{2,1,0:T(8,128)(2,1)S(1)}, u32[]{:S(2)}, u32[]{:S(2)}) async-start(bf16[16,128,128]{2,1,0:T(8,128)(2,1)} %bitcast.8), calls=%async_computation | async-start | bytes 1048576 | tf_op jit(solution)/shard_map/all_to_all | solution.py:272
  13.1 0.1 fusion.34
  13.2 0.1 add.219
  13.3 0.1 lt.164
  14.3 0.1 reshape.207
  14.5 0.1 convert_reduce_fusion.1
  14.7 0.3 convert_reduce_fusion
  15.0 0.2 select_reduce_fusion
  15.3 0.1 reduce_max.9
  15.4 15.0 %all-to-all-done = bf16[16,128,128]{2,1,0:T(8,128)(2,1)S(1)} async-done(((bf16[16,128,128]{2,1,0:T(8,128)(2,1)}), bf16[16,128,128]{2,1,0:T(8,128)(2,1)S(1)}, u32[]{:S(2)}, u32[]{:S(2)}) %all-to-all-start) | async-done | bytes 524320 | tf_op jit(solution)/shard_map/all_to_all | solution.py:272
  30.4 2.7 %collective-permute-start.1 = (bf16[2048,128]{1,0:T(8,128)(2,1)S(1)}, bf16[2048,128]{1,0:T(8,128)(2,1)S(1)}, u32[]{:S(2)}, u32[]{:S(2)}) collective-permute-start(bf16[2048,128]{1,0:T(8,128)(2,1)S(1)} %bitcast.22), channel_id=1, source_target_pairs={{0,3},{16,28},{1,0},{17,29},{2,1},{18,30},{3,2},{19,31},{4,7},{20,... | collective-permute-start | bytes 1572872 | tf_op jit(solution)/shard_map/ppermute | solution.py:235
  33.3 6.0 %collective-permute-done.1 = bf16[2048,128]{1,0:T(8,128)(2,1)S(1)} collective-permute-done((bf16[2048,128]{1,0:T(8,128)(2,1)S(1)}, bf16[2048,128]{1,0:T(8,128)(2,1)S(1)}, u32[]{:S(2)}, u32[]{:S(2)}) %collective-permute-start.1) | collective-permute-done | bytes 524320 | tf_op jit(solution)/shard_map/ppermute | solution.py:235
  39.3 3.1 %collective-permute-done = bf16[2048,128]{1,0:T(8,128)(2,1)S(1)} collective-permute-done((bf16[2048,128]{1,0:T(8,128)(2,1)S(1)}, bf16[2048,128]{1,0:T(8,128)(2,1)S(1)}, u32[]{:S(2)}, u32[]{:S(2)}) %collective-permute-start) | collective-permute-done | bytes 524320 | tf_op jit(solution)/shard_map/ppermute | solution.py:235
  42.4 0.1 collective-permute-start.12
  42.5 2.9 %collective-permute-start.7 = (bf16[4096,128]{1,0:T(8,128)(2,1)S(1)}, bf16[4096,128]{1,0:T(8,128)(2,1)}, u32[]{:S(2)}, u32[]{:S(2)}) collective-permute-start(bf16[4096,128]{1,0:T(8,128)(2,1)S(1)} %pad_maximum_fusion.refs_4_), channel_id=1, source_target_pairs={{0,12},{16,19},{1,13},{17,16},{2,14},{18,17},{3,15},{19,18},{4,0},... | collective-permute-start | bytes 3145736 | tf_op jit(solution)/shard_map/ppermute | solution.py:235
  45.5 8.0 %collective-permute-done.2 = bf16[2048,128]{1,0:T(8,128)(2,1)S(1)} collective-permute-done((bf16[2048,128]{1,0:T(8,128)(2,1)S(1)}, bf16[2048,128]{1,0:T(8,128)(2,1)S(1)}, u32[]{:S(2)}, u32[]{:S(2)}) %collective-permute-start.2) | collective-permute-done | bytes 524320 | tf_op jit(solution)/shard_map/ppermute | solution.py:235
  53.6 2.5 %collective-permute-start.9 = (bf16[4096,128]{1,0:T(8,128)(2,1)S(1)}, bf16[4096,128]{1,0:T(8,128)(2,1)}, u32[]{:S(2)}, u32[]{:S(2)}) collective-permute-start(bf16[4096,128]{1,0:T(8,128)(2,1)S(1)} %constant_dynamic-update-slice_fusion.refs_5_), channel_id=1, source_target_pairs={{0,12},{16,19},{1,13},{17,16},{2,14},{18,17},{3,15},{19,18},{4,0},... | collective-permute-start | bytes 3145736 | tf_op jit(solution)/shard_map/ppermute | solution.py:235
  56.0 1.3 constant_dynamic-slice_fusion
  57.3 0.1 collective-permute-start.5
  57.4 6.5 %collective-permute-done.5.refs_3_ = bf16[128,1024]{1,0:T(8,128)(2,1)S(1)} collective-permute-done((bf16[128,1024]{1,0:T(8,128)(2,1)S(1)}, bf16[128,1024]{1,0:T(8,128)(2,1)S(1)}, u32[]{:S(2)}, u32[]{:S(2)}) %collective-permute-start.5) | collective-permute-done | bytes 262176 | tf_op jit(solution)/shard_map/ppermute | solution.py:235
  63.8 5.6 %collective-permute-done.4.refs_2_ = bf16[128,1024]{1,0:T(8,128)(2,1)S(1)} collective-permute-done((bf16[128,1024]{1,0:T(8,128)(2,1)S(1)}, bf16[128,1024]{1,0:T(8,128)(2,1)S(1)}, u32[]{:S(2)}, u32[]{:S(2)}) %collective-permute-start.4) | collective-permute-done | bytes 262176 | tf_op jit(solution)/shard_map/ppermute | solution.py:235
  69.5 6.4 %collective-permute-done.3.refs_1_ = bf16[128,1024]{1,0:T(8,128)(2,1)S(1)} collective-permute-done((bf16[128,1024]{1,0:T(8,128)(2,1)S(1)}, bf16[128,1024]{1,0:T(8,128)(2,1)S(1)}, u32[]{:S(2)}, u32[]{:S(2)}) %collective-permute-start.3) | collective-permute-done | bytes 262176 | tf_op jit(solution)/shard_map/ppermute | solution.py:235
  75.9 7.7 %collective-permute-start.13 = (bf16[4096,128]{1,0:T(8,128)(2,1)S(1)}, bf16[4096,128]{1,0:T(8,128)(2,1)S(1)}, u32[]{:S(2)}, u32[]{:S(2)}) collective-permute-start(bf16[4096,128]{1,0:T(8,128)(2,1)S(1)} %constant_dynamic-update-slice_fusion.refs_5_), channel_id=1, source_target_pairs={{0,16},{16,0},{1,17},{17,1},{2,18},{18,2},{3,19},{19,3},{4,20},{20... | collective-permute-start | bytes 3145736 | tf_op jit(solution)/shard_map/ppermute | solution.py:235
  83.6 0.1 collective-permute-start.15
  83.7 0.1 collective-permute-start.10
  83.8 2.8 %collective-permute-start.11 = (bf16[4096,128]{1,0:T(8,128)(2,1)}, bf16[4096,128]{1,0:T(8,128)(2,1)S(1)}, u32[]{:S(2)}, u32[]{:S(2)}) collective-permute-start(bf16[4096,128]{1,0:T(8,128)(2,1)} %collective-permute-done.9.refs_9_), channel_id=1, source_target_pairs={{0,12},{16,19},{1,13},{17,16},{2,14},{18,17},{3,15},{19,18},{4,0},... | collective-permute-start | bytes 3145736 | tf_op jit(solution)/shard_map/ppermute | solution.py:235
  86.7 0.8 collective-permute-start.14
  87.5 11.3 %collective-permute-done.8.refs_8_ = bf16[4096,128]{1,0:T(8,128)(2,1)S(1)} collective-permute-done((bf16[4096,128]{1,0:T(8,128)(2,1)S(1)}, bf16[4096,128]{1,0:T(8,128)(2,1)S(1)}, u32[]{:S(2)}, u32[]{:S(2)}) %collective-permute-start.8) | collective-permute-done | bytes 1048608 | tf_op jit(solution)/shard_map/ppermute | solution.py:235
  98.8 0.9 collective-permute-start.17
  99.6 0.1 collective-permute-start.16
  99.7 10.3 %collective-permute-done.10.refs_10_ = bf16[4096,128]{1,0:T(8,128)(2,1)S(1)} collective-permute-done((bf16[4096,128]{1,0:T(8,128)(2,1)}, bf16[4096,128]{1,0:T(8,128)(2,1)S(1)}, u32[]{:S(2)}, u32[]{:S(2)}) %collective-permute-start.10) | collective-permute-done | bytes 1048608 | tf_op jit(solution)/shard_map/ppermute | solution.py:235
  110.0 0.9 collective-permute-start.18
  110.9 2.2 %collective-permute-done.18.refs_18_ = bf16[4096,128]{1,0:T(8,128)(2,1)S(1)} collective-permute-done((bf16[4096,128]{1,0:T(8,128)(2,1)S(1)}, bf16[4096,128]{1,0:T(8,128)(2,1)S(1)}, u32[]{:S(2)}, u32[]{:S(2)}) %collective-permute-start.18) | collective-permute-done | bytes 1048608 | tf_op jit(solution)/shard_map/ppermute | solution.py:235
  113.2 1.5 collective-permute-done.19.refs_19_
  114.7 0.9 copy-done.6
  115.6 25.4 %shard_map.73 = (bf16[128,1024]{1,0:T(8,128)(2,1)S(1)}, bf16[128,1024]{1,0:T(8,128)(2,1)S(1)}, bf16[128,1024]{1,0:T(8,128)(2,1)S(1)}, bf16[128,1024]{1,0:T(8,128)(2,1)S(1)}) custom-call(s32[2304]{0:T(1024)S(1)} %get-tuple-element.16.k_lists, s32[2304]{0:T(1024)S(1)} %get-tuple-element.17.v_lists, s32[73]{0:T(128)S(1)} %pad_add_fusion.2.counts, ...), custom_call_target="tpu_custom_call" | custom-call | tf_op jit(solution)/shard_map/pallas_call | solution.py:150
  141.1 0.7 copy-done.1
  141.8 0.2 collective-permute-start.20
  142.0 1.3 collective-permute-start.21
  143.2 0.6 and_select_fusion.2.starts
  143.9 6.6 %collective-permute-done.20.refs_1_ = bf16[128,1024]{1,0:T(8,128)(2,1)S(1)} collective-permute-done((bf16[128,1024]{1,0:T(8,128)(2,1)S(1)}, bf16[128,1024]{1,0:T(8,128)(2,1)S(1)}, u32[]{:S(2)}, u32[]{:S(2)}) %collective-permute-start.20) | collective-permute-done | bytes 262176 | tf_op jit(solution)/shard_map/ppermute | solution.py:235
  150.5 7.0 %collective-permute-done.22.refs_3_ = bf16[128,1024]{1,0:T(8,128)(2,1)S(1)} collective-permute-done((bf16[128,1024]{1,0:T(8,128)(2,1)S(1)}, bf16[128,1024]{1,0:T(8,128)(2,1)S(1)}, u32[]{:S(2)}, u32[]{:S(2)}) %collective-permute-start.22) | collective-permute-done | bytes 262176 | tf_op jit(solution)/shard_map/ppermute | solution.py:235
  157.5 0.7 copy-done.9
  158.2 2.2 %shard_map.74 = bf16[128,4096]{1,0:T(8,128)(2,1)} custom-call(s32[4]{0:T(128)} %and_select_fusion.2.starts, bf16[128,1024]{1,0:T(8,128)(2,1)} %copy-done.1, bf16[128,1024]{1,0:T(8,128)(2,1)} %copy-done.7, bf16[128,1024]{1,0:T(8,128)(2,1)} %copy-done.8, bf16[128,1024]{1,0:T(8,128)(2,1)} %copy-done.9), custom_call_target="tpu_custom_call" | custom-call | tf_op jit(solution)/shard_map/pallas_call | solution.py:170
  (72 shorter events, 1.7 us)
Async XLA Ops:
  0.0 14.0 %copy-start = (s32[32,24]{0,1:T(8,128)S(1)}, s32[32,24]{0,1:T(8,128)}, u32[]{:S(2)}) copy-start(s32[32,24]{0,1:T(8,128)} %param.12) | copy-start | bytes 9220
  2.2 11.3 %copy-start.11 = (s32[32]{0:T(128)S(1)}, s32[32]{0:T(128)}, u32[]{:S(2)}) copy-start(s32[32]{0:T(128)} %param.11) | copy-start | bytes 388
  2.2 11.4 %copy-start.12 = (s32[32]{0:T(128)S(1)}, s32[32]{0:T(128)}, u32[]{:S(2)}) copy-start(s32[32]{0:T(128)} %param.13) | copy-start | bytes 388
  2.2 11.8 %copy-start.10 = (s32[32,8]{0,1:T(8,128)S(1)}, s32[32,8]{0,1:T(8,128)}, u32[]{:S(2)}) copy-start(s32[32,8]{0,1:T(8,128)} %param.10) | copy-start | bytes 3076
  3.1 27.3 %all-to-all-start = ((bf16[16,128,128]{2,1,0:T(8,128)(2,1)}), bf16[16,128,128]{2,1,0:T(8,128)(2,1)S(1)}, u32[]{:S(2)}, u32[]{:S(2)}) async-start(bf16[16,128,128]{2,1,0:T(8,128)(2,1)} %bitcast.8), calls=%async_computation | async-start | bytes 1048576 | tf_op jit(solution)/shard_map/all_to_all | solution.py:272
  30.4 8.9 %collective-permute-start.1 = (bf16[2048,128]{1,0:T(8,128)(2,1)S(1)}, bf16[2048,128]{1,0:T(8,128)(2,1)S(1)}, u32[]{:S(2)}, u32[]{:S(2)}) collective-permute-start(bf16[2048,128]{1,0:T(8,128)(2,1)S(1)} %bitcast.22), channel_id=1, source_target_pairs={{0,3},{16,28},{1,0},{17,29},{2,1},{18,30},{3,2},{19,31},{4,7},{20,... | collective-permute-start | bytes 1572872 | tf_op jit(solution)/shard_map/ppermute | solution.py:235
  33.1 9.2 %collective-permute-start = (bf16[2048,128]{1,0:T(8,128)(2,1)S(1)}, bf16[2048,128]{1,0:T(8,128)(2,1)S(1)}, u32[]{:S(2)}, u32[]{:S(2)}) collective-permute-start(bf16[2048,128]{1,0:T(8,128)(2,1)S(1)} %bitcast.23), channel_id=1, source_target_pairs={{0,1},{16,20},{1,2},{17,21},{2,3},{18,22},{3,0},{19,23},{4,5},{20,... | collective-permute-start | bytes 1572872 | tf_op jit(solution)/shard_map/ppermute | solution.py:235
  42.4 11.1 %collective-permute-start.2 = (bf16[2048,128]{1,0:T(8,128)(2,1)S(1)}, bf16[2048,128]{1,0:T(8,128)(2,1)S(1)}, u32[]{:S(2)}, u32[]{:S(2)}) collective-permute-start(bf16[2048,128]{1,0:T(8,128)(2,1)S(1)} %collective-permute-done), channel_id=1, source_target_pairs={{0,1},{16,20},{1,2},{17,21},{2,3},{18,22},{3,0},{19,23},{4,5},{20,... | collective-permute-start | bytes 1572872 | tf_op jit(solution)/shard_map/ppermute | solution.py:235
  42.4 41.2 %collective-permute-start.12 = (bf16[4096,128]{1,0:T(8,128)(2,1)S(1)}, bf16[4096,128]{1,0:T(8,128)(2,1)S(1)}, u32[]{:S(2)}, u32[]{:S(2)}) collective-permute-start(bf16[4096,128]{1,0:T(8,128)(2,1)S(1)} %pad_maximum_fusion.refs_4_), channel_id=1, source_target_pairs={{0,16},{16,0},{1,17},{17,1},{2,18},{18,2},{3,19},{19,3},{4,20},{20... | collective-permute-start | bytes 3145736 | tf_op jit(solution)/shard_map/ppermute | solution.py:235
  42.5 41.1 %collective-permute-start.7 = (bf16[4096,128]{1,0:T(8,128)(2,1)S(1)}, bf16[4096,128]{1,0:T(8,128)(2,1)}, u32[]{:S(2)}, u32[]{:S(2)}) collective-permute-start(bf16[4096,128]{1,0:T(8,128)(2,1)S(1)} %pad_maximum_fusion.refs_4_), channel_id=1, source_target_pairs={{0,12},{16,19},{1,13},{17,16},{2,14},{18,17},{3,15},{19,18},{4,0},... | collective-permute-start | bytes 3145736 | tf_op jit(solution)/shard_map/ppermute | solution.py:235
  45.5 38.3 %collective-permute-start.6 = (bf16[4096,128]{1,0:T(8,128)(2,1)S(1)}, bf16[4096,128]{1,0:T(8,128)(2,1)}, u32[]{:S(2)}, u32[]{:S(2)}) collective-permute-start(bf16[4096,128]{1,0:T(8,128)(2,1)S(1)} %pad_maximum_fusion.refs_4_), channel_id=1, source_target_pairs={{0,4},{16,17},{1,5},{17,18},{2,6},{18,19},{3,7},{19,16},{4,8},{20,... | collective-permute-start | bytes 3145736 | tf_op jit(solution)/shard_map/ppermute | solution.py:235
  53.6 30.3 %collective-permute-start.9 = (bf16[4096,128]{1,0:T(8,128)(2,1)S(1)}, bf16[4096,128]{1,0:T(8,128)(2,1)}, u32[]{:S(2)}, u32[]{:S(2)}) collective-permute-start(bf16[4096,128]{1,0:T(8,128)(2,1)S(1)} %constant_dynamic-update-slice_fusion.refs_5_), channel_id=1, source_target_pairs={{0,12},{16,19},{1,13},{17,16},{2,14},{18,17},{3,15},{19,18},{4,0},... | collective-permute-start | bytes 3145736 | tf_op jit(solution)/shard_map/ppermute | solution.py:235
  57.3 6.6 %collective-permute-start.5 = (bf16[128,1024]{1,0:T(8,128)(2,1)S(1)}, bf16[128,1024]{1,0:T(8,128)(2,1)S(1)}, u32[]{:S(2)}, u32[]{:S(2)}) collective-permute-start(bf16[128,1024]{1,0:T(8,128)(2,1)S(1)} %get-tuple-element.29), channel_id=1, source_target_pairs={{0,64},{16,208},{1,65},{17,209},{2,66},{18,210},{3,67},{19,211},{4... | collective-permute-start | bytes 786440 | tf_op jit(solution)/shard_map/ppermute | solution.py:235
  63.8 5.6 %collective-permute-start.4 = (bf16[128,1024]{1,0:T(8,128)(2,1)S(1)}, bf16[128,1024]{1,0:T(8,128)(2,1)S(1)}, u32[]{:S(2)}, u32[]{:S(2)}) collective-permute-start(bf16[128,1024]{1,0:T(8,128)(2,1)S(1)} %get-tuple-element.30), channel_id=1, source_target_pairs={{0,224},{16,240},{1,225},{17,241},{2,226},{18,242},{3,227},{19,243... | collective-permute-start | bytes 786440 | tf_op jit(solution)/shard_map/ppermute | solution.py:235
  69.5 6.4 %collective-permute-start.3 = (bf16[128,1024]{1,0:T(8,128)(2,1)S(1)}, bf16[128,1024]{1,0:T(8,128)(2,1)S(1)}, u32[]{:S(2)}, u32[]{:S(2)}) collective-permute-start(bf16[128,1024]{1,0:T(8,128)(2,1)S(1)} %get-tuple-element.31), channel_id=1, source_target_pairs={{0,32},{16,48},{1,33},{17,49},{2,34},{18,50},{3,35},{19,51},{4,36}... | collective-permute-start | bytes 786440 | tf_op jit(solution)/shard_map/ppermute | solution.py:235
  75.9 10.8 %collective-permute-start.13 = (bf16[4096,128]{1,0:T(8,128)(2,1)S(1)}, bf16[4096,128]{1,0:T(8,128)(2,1)S(1)}, u32[]{:S(2)}, u32[]{:S(2)}) collective-permute-start(bf16[4096,128]{1,0:T(8,128)(2,1)S(1)} %constant_dynamic-update-slice_fusion.refs_5_), channel_id=1, source_target_pairs={{0,16},{16,0},{1,17},{17,1},{2,18},{18,2},{3,19},{19,3},{4,20},{20... | collective-permute-start | bytes 3145736 | tf_op jit(solution)/shard_map/ppermute | solution.py:235
  83.6 15.2 %collective-permute-start.8 = (bf16[4096,128]{1,0:T(8,128)(2,1)S(1)}, bf16[4096,128]{1,0:T(8,128)(2,1)S(1)}, u32[]{:S(2)}, u32[]{:S(2)}) collective-permute-start(bf16[4096,128]{1,0:T(8,128)(2,1)S(1)} %constant_dynamic-update-slice_fusion.refs_5_), channel_id=1, source_target_pairs={{0,4},{16,17},{1,5},{17,18},{2,6},{18,19},{3,7},{19,16},{4,8},{20,... | collective-permute-start | bytes 3145736 | tf_op jit(solution)/shard_map/ppermute | solution.py:235
  83.6 16.0 %collective-permute-start.15 = (bf16[4096,128]{1,0:T(8,128)(2,1)}, bf16[4096,128]{1,0:T(8,128)(2,1)S(1)}, u32[]{:S(2)}, u32[]{:S(2)}) collective-permute-start(bf16[4096,128]{1,0:T(8,128)(2,1)} %collective-permute-done.7.refs_7_), channel_id=1, source_target_pairs={{0,16},{16,0},{1,17},{17,1},{2,18},{18,2},{3,19},{19,3},{4,20},{20... | collective-permute-start | bytes 3145736 | tf_op jit(solution)/shard_map/ppermute | solution.py:235
  83.7 26.3 %collective-permute-start.10 = (bf16[4096,128]{1,0:T(8,128)(2,1)}, bf16[4096,128]{1,0:T(8,128)(2,1)S(1)}, u32[]{:S(2)}, u32[]{:S(2)}) collective-permute-start(bf16[4096,128]{1,0:T(8,128)(2,1)} %collective-permute-done.6.refs_6_), channel_id=1, source_target_pairs={{0,4},{16,17},{1,5},{17,18},{2,6},{18,19},{3,7},{19,16},{4,8},{20,... | collective-permute-start | bytes 3145736 | tf_op jit(solution)/shard_map/ppermute | solution.py:235
  83.8 27.0 %collective-permute-start.11 = (bf16[4096,128]{1,0:T(8,128)(2,1)}, bf16[4096,128]{1,0:T(8,128)(2,1)S(1)}, u32[]{:S(2)}, u32[]{:S(2)}) collective-permute-start(bf16[4096,128]{1,0:T(8,128)(2,1)} %collective-permute-done.9.refs_9_), channel_id=1, source_target_pairs={{0,12},{16,19},{1,13},{17,16},{2,14},{18,17},{3,15},{19,18},{4,0},... | collective-permute-start | bytes 3145736 | tf_op jit(solution)/shard_map/ppermute | solution.py:235
  86.7 24.2 %collective-permute-start.14 = (bf16[4096,128]{1,0:T(8,128)(2,1)}, bf16[4096,128]{1,0:T(8,128)(2,1)S(1)}, u32[]{:S(2)}, u32[]{:S(2)}) collective-permute-start(bf16[4096,128]{1,0:T(8,128)(2,1)} %collective-permute-done.6.refs_6_), channel_id=1, source_target_pairs={{0,16},{16,0},{1,17},{17,1},{2,18},{18,2},{3,19},{19,3},{4,20},{20... | collective-permute-start | bytes 3145736 | tf_op jit(solution)/shard_map/ppermute | solution.py:235
  98.8 12.1 %collective-permute-start.17 = (bf16[4096,128]{1,0:T(8,128)(2,1)}, bf16[4096,128]{1,0:T(8,128)(2,1)S(1)}, u32[]{:S(2)}, u32[]{:S(2)}) collective-permute-start(bf16[4096,128]{1,0:T(8,128)(2,1)} %collective-permute-done.9.refs_9_), channel_id=1, source_target_pairs={{0,16},{16,0},{1,17},{17,1},{2,18},{18,2},{3,19},{19,3},{4,20},{20... | collective-permute-start | bytes 3145736 | tf_op jit(solution)/shard_map/ppermute | solution.py:235
  99.6 15.0 %copy-start.2 = (bf16[4096,128]{1,0:T(8,128)(2,1)}, bf16[4096,128]{1,0:T(8,128)(2,1)S(1)}, u32[]{:S(2)}) copy-start(bf16[4096,128]{1,0:T(8,128)(2,1)S(1)} %collective-permute-done.15.refs_15_) | copy-start | bytes 3145732
  99.6 11.3 %collective-permute-start.16 = (bf16[4096,128]{1,0:T(8,128)(2,1)S(1)}, bf16[4096,128]{1,0:T(8,128)(2,1)S(1)}, u32[]{:S(2)}, u32[]{:S(2)}) collective-permute-start(bf16[4096,128]{1,0:T(8,128)(2,1)S(1)} %collective-permute-done.8.refs_8_), channel_id=1, source_target_pairs={{0,16},{16,0},{1,17},{17,1},{2,18},{18,2},{3,19},{19,3},{4,20},{20... | collective-permute-start | bytes 3145736 | tf_op jit(solution)/shard_map/ppermute | solution.py:235
  110.0 3.1 %collective-permute-start.18 = (bf16[4096,128]{1,0:T(8,128)(2,1)S(1)}, bf16[4096,128]{1,0:T(8,128)(2,1)S(1)}, u32[]{:S(2)}, u32[]{:S(2)}) collective-permute-start(bf16[4096,128]{1,0:T(8,128)(2,1)S(1)} %collective-permute-done.10.refs_10_), channel_id=1, source_target_pairs={{0,16},{16,0},{1,17},{17,1},{2,18},{18,2},{3,19},{19,3},{4,20},{20... | collective-permute-start | bytes 3145736 | tf_op jit(solution)/shard_map/ppermute | solution.py:235
  110.9 3.8 %collective-permute-start.19 = (bf16[4096,128]{1,0:T(8,128)(2,1)S(1)}, bf16[4096,128]{1,0:T(8,128)(2,1)S(1)}, u32[]{:S(2)}, u32[]{:S(2)}) collective-permute-start(bf16[4096,128]{1,0:T(8,128)(2,1)S(1)} %collective-permute-done.11.refs_11_), channel_id=1, source_target_pairs={{0,16},{16,0},{1,17},{17,1},{2,18},{18,2},{3,19},{19,3},{4,20},{20... | collective-permute-start | bytes 3145736 | tf_op jit(solution)/shard_map/ppermute | solution.py:235
  110.9 3.8 %copy-start.3 = (bf16[4096,128]{1,0:T(8,128)(2,1)}, bf16[4096,128]{1,0:T(8,128)(2,1)S(1)}, u32[]{:S(2)}) copy-start(bf16[4096,128]{1,0:T(8,128)(2,1)S(1)} %collective-permute-done.17.refs_17_) | copy-start | bytes 3145732
  110.9 3.8 %copy-start.4 = (bf16[4096,128]{1,0:T(8,128)(2,1)}, bf16[4096,128]{1,0:T(8,128)(2,1)S(1)}, u32[]{:S(2)}) copy-start(bf16[4096,128]{1,0:T(8,128)(2,1)S(1)} %collective-permute-done.16.refs_16_) | copy-start | bytes 3145732
  113.2 1.5 copy-start.5
  114.7 1.0 copy-start.6
  141.1 0.7 copy-start.1
  141.8 8.7 %collective-permute-start.20 = (bf16[128,1024]{1,0:T(8,128)(2,1)S(1)}, bf16[128,1024]{1,0:T(8,128)(2,1)S(1)}, u32[]{:S(2)}, u32[]{:S(2)}) collective-permute-start(bf16[128,1024]{1,0:T(8,128)(2,1)S(1)} %get-tuple-element.24), channel_id=1, source_target_pairs={{0,224},{16,240},{1,225},{17,241},{2,226},{18,242},{3,227},{19,243... | collective-permute-start | bytes 786440 | tf_op jit(solution)/shard_map/ppermute | solution.py:235
  142.0 8.6 %collective-permute-start.21 = (bf16[128,1024]{1,0:T(8,128)(2,1)S(1)}, bf16[128,1024]{1,0:T(8,128)(2,1)S(1)}, u32[]{:S(2)}, u32[]{:S(2)}) collective-permute-start(bf16[128,1024]{1,0:T(8,128)(2,1)S(1)} %get-tuple-element.25), channel_id=1, source_target_pairs={{0,32},{16,48},{1,33},{17,49},{2,34},{18,50},{3,35},{19,51},{4,36}... | collective-permute-start | bytes 786440 | tf_op jit(solution)/shard_map/ppermute | solution.py:235
  143.2 14.3 %collective-permute-start.22 = (bf16[128,1024]{1,0:T(8,128)(2,1)S(1)}, bf16[128,1024]{1,0:T(8,128)(2,1)S(1)}, u32[]{:S(2)}, u32[]{:S(2)}) collective-permute-start(bf16[128,1024]{1,0:T(8,128)(2,1)S(1)} %get-tuple-element.26), channel_id=1, source_target_pairs={{0,192},{16,80},{1,193},{17,81},{2,194},{18,82},{3,195},{19,83},{4... | collective-permute-start | bytes 786440 | tf_op jit(solution)/shard_map/ppermute | solution.py:235
  150.5 7.0 %copy-start.7 = (bf16[128,1024]{1,0:T(8,128)(2,1)}, bf16[128,1024]{1,0:T(8,128)(2,1)S(1)}, u32[]{:S(2)}) copy-start(bf16[128,1024]{1,0:T(8,128)(2,1)S(1)} %collective-permute-done.20.refs_1_) | copy-start | bytes 786436
  150.5 7.0 %copy-start.8 = (bf16[128,1024]{1,0:T(8,128)(2,1)}, bf16[128,1024]{1,0:T(8,128)(2,1)S(1)}, u32[]{:S(2)}) copy-start(bf16[128,1024]{1,0:T(8,128)(2,1)S(1)} %collective-permute-done.21.refs_2_) | copy-start | bytes 786436
  157.5 0.7 copy-start.9

commit v4 on v3

--- a/solution.py
+++ b/solution.py
@@ -28,16 +28,16 @@
 
 
 def attend_kernel(k_lists, v_lists, counts, *refs):
-    q_refs, held, swapped, o_refs = refs[:4], refs[4:12], refs[12:20], refs[20:24]
-    k_s, v_s, top_s, sum_s, acc_s, score_s, sem = refs[24:]
+    q_refs, held, swapped, o_refs = refs[:4], refs[4:9], refs[9:14], refs[14:18]
+    k_s, v_s, top_s, sum_s, acc_s, score_s, sem = refs[18:]
     is_first = counts[HG + HG * QB] == 0
 
     def copies(source, target, first_sem):
         return [
             pltpu.make_async_copy(
-                piece, target.at[pl.ds(p * PIECE, PIECE), :], sem.at[first_sem + p]
+                piece, target.at[pl.ds(start * PIECE, piece.shape[0]), :], sem.at[first_sem + p]
             )
-            for p, piece in enumerate(source)
+            for p, (piece, start) in enumerate(zip(source, (0, 2, 4, 6, 7)))
         ]
 
     @pl.when(is_first)
@@ -150,7 +150,7 @@
     return pl.pallas_call(
         attend_kernel,
         out_shape=[jax.ShapeDtypeStruct((2 * BLK, HG * DH), jnp.bfloat16)] * 4,
-        in_specs=[smem] * 3 + [vmem] * 4 + [any_space] * 16,
+        in_specs=[smem] * 3 + [vmem] * 4 + [any_space] * 10,
         out_specs=[vmem] * 4,
         scratch_shapes=[pltpu.VMEM((SEQ, DH), jnp.bfloat16)] * 2
         + [pltpu.VMEM((QB * BLK, DH), jnp.float32)] * 3
@@ -213,7 +213,7 @@
         piece = jnp.where(
             big == 0,
             far,
-            jnp.where(big == 3, 2 + 2 * far, jnp.where(big == 1, 3 + 2 * far, 6 + far)),
+            jnp.where(big == 3, 2 + far, jnp.where(big == 1, 4 + far, 6 + far)),
         )
         return piece * 64 + slot % 2 * 32 + inner
 
@@ -242,21 +242,20 @@
 
 
 def gather_pairs(own, lists, late):
+    tie = lax.optimization_barrier
+    own, late = tie((own, late))
     up1 = send(own, UP_X, UP_Y)
     down1 = send(own, DOWN_X, DOWN_Y)
-    up1, down1, lists = lax.optimization_barrier((up1, down1, lists))
-    up2 = send(up1, UP_X, UP_Y)
-    near = jnp.concatenate([own, up1])
+    up2 = send(own, (0, 0, 0, 2), (0, 0, 2, 0))
+    queries = (late[0], send(late[1], UP_Z), send(late[2], DOWN_Z), send(late[3], UP_2, DOWN_2))
+    up1, down1, up2, lists = tie((up1, down1, up2, lists))
+    near = jnp.concatenate([own, up1, down1, up2])
     a1 = send(near, UP_Y, UP_X)
     b1 = send(near, DOWN_Y, DOWN_X)
-    up2, late = lax.optimization_barrier((up2, late))
-    far = jnp.concatenate([down1, up2])
-    a2 = send(far, UP_Y, UP_X)
-    b2 = send(far, DOWN_Y, DOWN_X)
-    a3 = send(a1, UP_Y, UP_X)
-    b3 = send(b2, DOWN_Y, DOWN_X)
-    held = (near, far, a1, b1, a2, b2, a3, b3)
-    return held, tuple(send(piece, OTHER) for piece in held), lists, late
+    a2 = send(a1[:PIECE], UP_Y, UP_X)
+    b2 = send(b1[PIECE:], DOWN_Y, DOWN_X)
+    held = (near, a1, b1, a2, b2)
+    return held, tuple(send(piece, OTHER) for piece in held), lists, queries
 
 
 def per_device(
@@ -293,18 +292,12 @@
     k_lists, v_lists = piece_places(blocks, y, x)
     counts = jnp.concatenate([steps, live, core[None]])
     lists = (k_lists.reshape(-1), v_lists.reshape(-1), counts)
-    held, swapped, lists, query_rows = gather_pairs(own, lists, query_rows)
-
     def heads(step):
         start = (z + step) % KVH * (HG * DH)
         return lax.dynamic_slice_in_dim(query_rows, start, HG * DH, 1)
 
-    queries = (
-        heads(0),
-        send(heads(1), UP_Z),
-        send(heads(3), DOWN_Z),
-        send(heads(2), UP_2, DOWN_2),
-    )
+    late = (heads(0), heads(1), heads(3), heads(2))
+    held, swapped, lists, queries = gather_pairs(own, lists, late)
     outputs = attend(*lists, queries, held, swapped)
     pieces = (
         outputs[0],

time: 160 us -> 143 us (0.89); the launches traced: 160 us -> 142 us
  waiting for transfers between devices: 89.5 us -> 75.9 us
  starting transfers between devices: 33.1 us -> 28.6 us
    ppermute x23 -> x18, waiting for transfers between devices: 74.5 us -> 61.1 us  [send(): return lax.ppermute(array, AXES, pairs)]
    ppermute x23 -> x18, starting transfers between devices: 23.1 us -> 18.7 us  [send(): return lax.ppermute(array, AXES, pairs)]
  transfers between devices with their start and end apart: 24 -> 19, of which waited for: 13 -> 11; matrix products, arithmetic and copies ran while one was open for 3% -> 2% of each run, Pallas kernels for 0% -> 0%
where the time goes in v4:
time: 143 us; the launch traced here: 142 us
  waiting for transfers between devices  75.9 us (53%)
  starting transfers between devices  28.6 us (20%)
  Pallas kernels  27.5 us (19%)
  local copies, waits for them, and re-layouts  7.4 us (5%)
  other arithmetic  2 us (1%)
    ppermute x18, waiting for transfers between devices, send(): return lax.ppermute(array, AXES, pairs)  61.1 us
    pallas_call x1, Pallas kernels, attend(): pl.pallas_call(attend_kernel, out_shape=[jax.ShapeDtypeStruct((2 * BLK, H...  25.2 us
    ppermute x18, starting transfers between devices, send(): return lax.ppermute(array, AXES, pairs)  18.7 us
    all_to_all x1, waiting for transfers between devices, per_device(): lax.all_to_all(jnp.concatenate([pairs, pairs]).reshape(4 * KVH, tokens, D...  14.8 us
    all_to_all x1, starting transfers between devices, per_device(): lax.all_to_all(jnp.concatenate([pairs, pairs]).reshape(4 * KVH, tokens, D...  9.98 us
    unnamed x27, local copies, waits for them, and re-layouts  2.9 us
  transfers between devices with their start and end apart: 19, of which 11 were waited for; matrix products, arithmetic and copies ran while one was open for 2% of the time, Pallas kernels for 0%

profile of v4, /device:TPU:1, one launch (start us, length us, event | category | flops | bytes accessed | tf_op | source)
XLA Modules:
  0.0 141.7 jit_solution(14167045889463051563)
XLA Ops:
  0.0 1.0 reshape.203
  1.1 0.9 reshape.204
  2.0 0.2 maximum_maximum_fusion
  2.3 0.9 copy.19
  3.2 10.0 %all-to-all-start = ((bf16[16,128,128]{2,1,0:T(8,128)(2,1)}), bf16[16,128,128]{2,1,0:T(8,128)(2,1)S(1)}, u32[]{:S(2)}, u32[]{:S(2)}) async-start(bf16[16,128,128]{2,1,0:T(8,128)(2,1)} %bitcast.8), calls=%async_computation | async-start | bytes 1048576 | tf_op jit(solution)/shard_map/all_to_all | solution.py:271
  13.1 0.1 fusion.34
  13.3 0.1 add.226
  13.4 0.1 lt.171
  13.5 0.1 broadcast_in_dim_tile.3
  13.6 0.1 dynamic_slice.28
  13.8 0.1 lt.175
  13.9 0.1 lt.167
  14.4 0.1 reshape.207
  14.6 0.1 convert_reduce_fusion.1
  14.8 0.3 convert_reduce_fusion
  15.1 0.2 select_reduce_fusion
  15.4 0.1 reduce_max.9
  15.5 0.1 constant_dynamic-slice_fusion
  15.7 14.8 %all-to-all-done = bf16[16,128,128]{2,1,0:T(8,128)(2,1)S(1)} async-done(((bf16[16,128,128]{2,1,0:T(8,128)(2,1)}), bf16[16,128,128]{2,1,0:T(8,128)(2,1)S(1)}, u32[]{:S(2)}, u32[]{:S(2)}) %all-to-all-start) | async-done | bytes 524320 | tf_op jit(solution)/shard_map/all_to_all | solution.py:271
  30.5 2.9 %collective-permute-start.2 = (bf16[2048,128]{1,0:T(8,128)(2,1)S(1)}, bf16[2048,128]{1,0:T(8,128)(2,1)S(1)}, u32[]{:S(2)}, u32[]{:S(2)}) collective-permute-start(bf16[2048,128]{1,0:T(8,128)(2,1)S(1)} %bitcast.22), channel_id=1, source_target_pairs={{0,2},{16,24},{1,3},{17,25},{2,0},{18,26},{3,1},{19,27},{4,6},{20,... | collective-permute-start | bytes 1572872 | tf_op jit(solution)/shard_map/ppermute | solution.py:235
  33.4 0.8 collective-permute-start.1
  34.2 0.7 collective-permute-start
  35.0 5.1 %collective-permute-done.2 = bf16[2048,128]{1,0:T(8,128)(2,1)S(1)} collective-permute-done((bf16[2048,128]{1,0:T(8,128)(2,1)S(1)}, bf16[2048,128]{1,0:T(8,128)(2,1)S(1)}, u32[]{:S(2)}, u32[]{:S(2)}) %collective-permute-start.2) | collective-permute-done | bytes 524320 | tf_op jit(solution)/shard_map/ppermute | solution.py:235
  40.1 5.9 %collective-permute-done.1 = bf16[2048,128]{1,0:T(8,128)(2,1)S(1)} collective-permute-done((bf16[2048,128]{1,0:T(8,128)(2,1)S(1)}, bf16[2048,128]{1,0:T(8,128)(2,1)S(1)}, u32[]{:S(2)}, u32[]{:S(2)}) %collective-permute-start.1) | collective-permute-done | bytes 524320 | tf_op jit(solution)/shard_map/ppermute | solution.py:235
  46.2 2.6 %collective-permute-start.7 = (bf16[8192,128]{1,0:T(8,128)(2,1)S(1)}, bf16[8192,128]{1,0:T(8,128)(2,1)S(1)}, u32[]{:S(2)}, u32[]{:S(2)}) collective-permute-start(bf16[8192,128]{1,0:T(8,128)(2,1)S(1)} %constant_dynamic-update-slice_fusion.refs_4_), channel_id=1, source_target_pairs={{0,12},{16,19},{1,13},{17,16},{2,14},{18,17},{3,15},{19,18},{4,0},... | collective-permute-start | bytes 6291464 | tf_op jit(solution)/shard_map/ppermute | solution.py:235
  48.8 2.7 %collective-permute-start.4 = (bf16[128,1024]{1,0:T(8,128)(2,1)S(1)}, bf16[128,1024]{1,0:T(8,128)(2,1)S(1)}, u32[]{:S(2)}, u32[]{:S(2)}) collective-permute-start(bf16[128,1024]{1,0:T(8,128)(2,1)S(1)} %get-tuple-element.26), channel_id=1, source_target_pairs={{0,224},{16,240},{1,225},{17,241},{2,226},{18,242},{3,227},{19,243... | collective-permute-start | bytes 786440 | tf_op jit(solution)/shard_map/ppermute | solution.py:235
  51.5 20.3 %collective-permute-done.7.refs_6_ = bf16[8192,128]{1,0:T(8,128)(2,1)S(1)} collective-permute-done((bf16[8192,128]{1,0:T(8,128)(2,1)S(1)}, bf16[8192,128]{1,0:T(8,128)(2,1)S(1)}, u32[]{:S(2)}, u32[]{:S(2)}) %collective-permute-start.7) | collective-permute-done | bytes 2097184 | tf_op jit(solution)/shard_map/ppermute | solution.py:235
  71.8 0.8 collective-permute-start.10
  72.7 2.5 %collective-permute-done.6.refs_5_ = bf16[8192,128]{1,0:T(8,128)(2,1)S(1)} collective-permute-done((bf16[8192,128]{1,0:T(8,128)(2,1)S(1)}, bf16[8192,128]{1,0:T(8,128)(2,1)S(1)}, u32[]{:S(2)}, u32[]{:S(2)}) %collective-permute-start.6) | collective-permute-done | bytes 2097184 | tf_op jit(solution)/shard_map/ppermute | solution.py:235
  75.2 0.2 collective-permute-start.9
  75.4 1.4 collective-permute-start.8
  76.8 1.7 %collective-permute-start.12 = (bf16[8192,128]{1,0:T(8,128)(2,1)S(1)}, bf16[8192,128]{1,0:T(8,128)(2,1)S(1)}, u32[]{:S(2)}, u32[]{:S(2)}) collective-permute-start(bf16[8192,128]{1,0:T(8,128)(2,1)S(1)} %collective-permute-done.7.refs_6_), channel_id=1, source_target_pairs={{0,16},{16,0},{1,17},{17,1},{2,18},{18,2},{3,19},{19,3},{4,20},{20... | collective-permute-start | bytes 6291464 | tf_op jit(solution)/shard_map/ppermute | solution.py:235
  78.5 0.1 collective-permute-start.11
  78.6 10.6 %collective-permute-done.9.refs_8_ = bf16[4096,128]{1,0:T(8,128)(2,1)S(1)} collective-permute-done((bf16[4096,128]{1,0:T(8,128)(2,1)S(1)}, bf16[4096,128]{1,0:T(8,128)(2,1)S(1)}, u32[]{:S(2)}, u32[]{:S(2)}) %collective-permute-start.9) | collective-permute-done | bytes 1048608 | tf_op jit(solution)/shard_map/ppermute | solution.py:235
  89.1 1.9 %collective-permute-start.14 = (bf16[4096,128]{1,0:T(8,128)(2,1)S(1)}, bf16[4096,128]{1,0:T(8,128)(2,1)S(1)}, u32[]{:S(2)}, u32[]{:S(2)}) collective-permute-start(bf16[4096,128]{1,0:T(8,128)(2,1)S(1)} %collective-permute-done.9.refs_8_), channel_id=1, source_target_pairs={{0,16},{16,0},{1,17},{17,1},{2,18},{18,2},{3,19},{19,3},{4,20},{20... | collective-permute-start | bytes 3145736 | tf_op jit(solution)/shard_map/ppermute | solution.py:235
  91.1 1.5 %collective-permute-start.13 = (bf16[4096,128]{1,0:T(8,128)(2,1)S(1)}, bf16[4096,128]{1,0:T(8,128)(2,1)S(1)}, u32[]{:S(2)}, u32[]{:S(2)}) collective-permute-start(bf16[4096,128]{1,0:T(8,128)(2,1)S(1)} %collective-permute-done.8.refs_7_), channel_id=1, source_target_pairs={{0,16},{16,0},{1,17},{17,1},{2,18},{18,2},{3,19},{19,3},{4,20},{20... | collective-permute-start | bytes 3145736 | tf_op jit(solution)/shard_map/ppermute | solution.py:235
  92.6 0.7 collective-permute-done.14.refs_13_
  93.4 1.5 %collective-permute-done.13.refs_12_ = bf16[4096,128]{1,0:T(8,128)(2,1)S(1)} collective-permute-done((bf16[4096,128]{1,0:T(8,128)(2,1)S(1)}, bf16[4096,128]{1,0:T(8,128)(2,1)S(1)}, u32[]{:S(2)}, u32[]{:S(2)}) %collective-permute-start.13) | collective-permute-done | bytes 1048608 | tf_op jit(solution)/shard_map/ppermute | solution.py:235
  94.9 1.3 copy-done.4
  96.2 25.2 %shard_map.73 = (bf16[128,1024]{1,0:T(8,128)(2,1)S(1)}, bf16[128,1024]{1,0:T(8,128)(2,1)S(1)}, bf16[128,1024]{1,0:T(8,128)(2,1)S(1)}, bf16[128,1024]{1,0:T(8,128)(2,1)S(1)}) custom-call(s32[2304]{0:T(1024)S(1)} %get-tuple-element.21.k_lists, s32[2304]{0:T(1024)S(1)} %get-tuple-element.22.v_lists, s32[73]{0:T(128)S(1)} %pad_add_fusion.2.counts, ...), custom_call_target="tpu_custom_call" | custom-call | tf_op jit(solution)/shard_map/pallas_call | solution.py:150
  121.4 0.7 copy-done.1
  122.1 1.5 %collective-permute-start.16 = (bf16[128,1024]{1,0:T(8,128)(2,1)S(1)}, bf16[128,1024]{1,0:T(8,128)(2,1)S(1)}, u32[]{:S(2)}, u32[]{:S(2)}) collective-permute-start(bf16[128,1024]{1,0:T(8,128)(2,1)S(1)} %get-tuple-element.33), channel_id=1, source_target_pairs={{0,32},{16,48},{1,33},{17,49},{2,34},{18,50},{3,35},{19,51},{4,36}... | collective-permute-start | bytes 786440 | tf_op jit(solution)/shard_map/ppermute | solution.py:235
  123.6 0.7 and_select_fusion.2.starts
  124.3 5.9 %collective-permute-done.15.refs_1_ = bf16[128,1024]{1,0:T(8,128)(2,1)S(1)} collective-permute-done((bf16[128,1024]{1,0:T(8,128)(2,1)S(1)}, bf16[128,1024]{1,0:T(8,128)(2,1)S(1)}, u32[]{:S(2)}, u32[]{:S(2)}) %collective-permute-start.15) | collective-permute-done | bytes 262176 | tf_op jit(solution)/shard_map/ppermute | solution.py:235
  130.2 2.0 %collective-permute-done.16.refs_2_ = bf16[128,1024]{1,0:T(8,128)(2,1)S(1)} collective-permute-done((bf16[128,1024]{1,0:T(8,128)(2,1)S(1)}, bf16[128,1024]{1,0:T(8,128)(2,1)S(1)}, u32[]{:S(2)}, u32[]{:S(2)}) %collective-permute-start.16) | collective-permute-done | bytes 262176 | tf_op jit(solution)/shard_map/ppermute | solution.py:235
  132.1 6.6 %collective-permute-done.17.refs_3_ = bf16[128,1024]{1,0:T(8,128)(2,1)S(1)} collective-permute-done((bf16[128,1024]{1,0:T(8,128)(2,1)S(1)}, bf16[128,1024]{1,0:T(8,128)(2,1)S(1)}, u32[]{:S(2)}, u32[]{:S(2)}) %collective-permute-start.17) | collective-permute-done | bytes 262176 | tf_op jit(solution)/shard_map/ppermute | solution.py:235
  138.7 0.7 copy-done.8
  139.4 2.2 %shard_map.74 = bf16[128,4096]{1,0:T(8,128)(2,1)} custom-call(s32[4]{0:T(128)} %and_select_fusion.2.starts, bf16[128,1024]{1,0:T(8,128)(2,1)} %copy-done.1, bf16[128,1024]{1,0:T(8,128)(2,1)} %copy-done.6, bf16[128,1024]{1,0:T(8,128)(2,1)} %copy-done.7, bf16[128,1024]{1,0:T(8,128)(2,1)} %copy-done.8), custom_call_target="tpu_custom_call" | custom-call | tf_op jit(solution)/shard_map/pallas_call | solution.py:170
  (63 shorter events, 1.5 us)
Async XLA Ops:
  0.0 14.1 %copy-start = (s32[32,24]{0,1:T(8,128)S(1)}, s32[32,24]{0,1:T(8,128)}, u32[]{:S(2)}) copy-start(s32[32,24]{0,1:T(8,128)} %param.12) | copy-start | bytes 9220
  0.0 13.6 %copy-start.10 = (s32[32]{0:T(128)S(1)}, s32[32]{0:T(128)}, u32[]{:S(2)}) copy-start(s32[32]{0:T(128)} %param.11) | copy-start | bytes 388
  0.0 13.6 %copy-start.11 = (s32[32]{0:T(128)S(1)}, s32[32]{0:T(128)}, u32[]{:S(2)}) copy-start(s32[32]{0:T(128)} %param.13) | copy-start | bytes 388
  0.0 14.0 %copy-start.9 = (s32[32,8]{0,1:T(8,128)S(1)}, s32[32,8]{0,1:T(8,128)}, u32[]{:S(2)}) copy-start(s32[32,8]{0,1:T(8,128)} %param.10) | copy-start | bytes 3076
  0.0 15.5 %copy-start.5 = (bf16[128,4096]{1,0:T(8,128)(2,1)S(1)}, bf16[128,4096]{1,0:T(8,128)(2,1)}, u32[]{:S(2)}) copy-start(bf16[128,4096]{1,0:T(8,128)(2,1)} %param.7) | copy-start | bytes 3145732
  3.2 27.3 %all-to-all-start = ((bf16[16,128,128]{2,1,0:T(8,128)(2,1)}), bf16[16,128,128]{2,1,0:T(8,128)(2,1)S(1)}, u32[]{:S(2)}, u32[]{:S(2)}) async-start(bf16[16,128,128]{2,1,0:T(8,128)(2,1)} %bitcast.8), calls=%async_computation | async-start | bytes 1048576 | tf_op jit(solution)/shard_map/all_to_all | solution.py:271
  30.5 9.6 %collective-permute-start.2 = (bf16[2048,128]{1,0:T(8,128)(2,1)S(1)}, bf16[2048,128]{1,0:T(8,128)(2,1)S(1)}, u32[]{:S(2)}, u32[]{:S(2)}) collective-permute-start(bf16[2048,128]{1,0:T(8,128)(2,1)S(1)} %bitcast.22), channel_id=1, source_target_pairs={{0,2},{16,24},{1,3},{17,25},{2,0},{18,26},{3,1},{19,27},{4,6},{20,... | collective-permute-start | bytes 1572872 | tf_op jit(solution)/shard_map/ppermute | solution.py:235
  33.4 12.6 %collective-permute-start.1 = (bf16[2048,128]{1,0:T(8,128)(2,1)S(1)}, bf16[2048,128]{1,0:T(8,128)(2,1)S(1)}, u32[]{:S(2)}, u32[]{:S(2)}) collective-permute-start(bf16[2048,128]{1,0:T(8,128)(2,1)S(1)} %bitcast.23), channel_id=1, source_target_pairs={{0,3},{16,28},{1,0},{17,29},{2,1},{18,30},{3,2},{19,31},{4,7},{20,... | collective-permute-start | bytes 1572872 | tf_op jit(solution)/shard_map/ppermute | solution.py:235
  34.2 11.9 %collective-permute-start = (bf16[2048,128]{1,0:T(8,128)(2,1)S(1)}, bf16[2048,128]{1,0:T(8,128)(2,1)S(1)}, u32[]{:S(2)}, u32[]{:S(2)}) collective-permute-start(bf16[2048,128]{1,0:T(8,128)(2,1)S(1)} %bitcast.24), channel_id=1, source_target_pairs={{0,1},{16,20},{1,2},{17,21},{2,3},{18,22},{3,0},{19,23},{4,5},{20,... | collective-permute-start | bytes 1572872 | tf_op jit(solution)/shard_map/ppermute | solution.py:235
  46.2 25.5 %collective-permute-start.7 = (bf16[8192,128]{1,0:T(8,128)(2,1)S(1)}, bf16[8192,128]{1,0:T(8,128)(2,1)S(1)}, u32[]{:S(2)}, u32[]{:S(2)}) collective-permute-start(bf16[8192,128]{1,0:T(8,128)(2,1)S(1)} %constant_dynamic-update-slice_fusion.refs_4_), channel_id=1, source_target_pairs={{0,12},{16,19},{1,13},{17,16},{2,14},{18,17},{3,15},{19,18},{4,0},... | collective-permute-start | bytes 6291464 | tf_op jit(solution)/shard_map/ppermute | solution.py:235
  48.8 26.4 %collective-permute-start.6 = (bf16[8192,128]{1,0:T(8,128)(2,1)S(1)}, bf16[8192,128]{1,0:T(8,128)(2,1)S(1)}, u32[]{:S(2)}, u32[]{:S(2)}) collective-permute-start(bf16[8192,128]{1,0:T(8,128)(2,1)S(1)} %constant_dynamic-update-slice_fusion.refs_4_), channel_id=1, source_target_pairs={{0,4},{16,17},{1,5},{17,18},{2,6},{18,19},{3,7},{19,16},{4,8},{20,... | collective-permute-start | bytes 6291464 | tf_op jit(solution)/shard_map/ppermute | solution.py:235
  48.8 26.6 %collective-permute-start.3 = (bf16[128,1024]{1,0:T(8,128)(2,1)S(1)}, bf16[128,1024]{1,0:T(8,128)(2,1)S(1)}, u32[]{:S(2)}, u32[]{:S(2)}) collective-permute-start(bf16[128,1024]{1,0:T(8,128)(2,1)S(1)} %get-tuple-element.25), channel_id=1, source_target_pairs={{0,32},{16,48},{1,33},{17,49},{2,34},{18,50},{3,35},{19,51},{4,36}... | collective-permute-start | bytes 786440 | tf_op jit(solution)/shard_map/ppermute | solution.py:235
  48.8 28.0 %collective-permute-start.4 = (bf16[128,1024]{1,0:T(8,128)(2,1)S(1)}, bf16[128,1024]{1,0:T(8,128)(2,1)S(1)}, u32[]{:S(2)}, u32[]{:S(2)}) collective-permute-start(bf16[128,1024]{1,0:T(8,128)(2,1)S(1)} %get-tuple-element.26), channel_id=1, source_target_pairs={{0,224},{16,240},{1,225},{17,241},{2,226},{18,242},{3,227},{19,243... | collective-permute-start | bytes 786440 | tf_op jit(solution)/shard_map/ppermute | solution.py:235
  51.5 27.0 %collective-permute-start.5 = (bf16[128,1024]{1,0:T(8,128)(2,1)S(1)}, bf16[128,1024]{1,0:T(8,128)(2,1)S(1)}, u32[]{:S(2)}, u32[]{:S(2)}) collective-permute-start(bf16[128,1024]{1,0:T(8,128)(2,1)S(1)} %get-tuple-element.27), channel_id=1, source_target_pairs={{0,64},{16,208},{1,65},{17,209},{2,66},{18,210},{3,67},{19,211},{4... | collective-permute-start | bytes 786440 | tf_op jit(solution)/shard_map/ppermute | solution.py:235
  71.8 20.8 %collective-permute-start.10 = (bf16[8192,128]{1,0:T(8,128)(2,1)S(1)}, bf16[8192,128]{1,0:T(8,128)(2,1)S(1)}, u32[]{:S(2)}, u32[]{:S(2)}) collective-permute-start(bf16[8192,128]{1,0:T(8,128)(2,1)S(1)} %constant_dynamic-update-slice_fusion.refs_4_), channel_id=1, source_target_pairs={{0,16},{16,0},{1,17},{17,1},{2,18},{18,2},{3,19},{19,3},{4,20},{20... | collective-permute-start | bytes 6291464 | tf_op jit(solution)/shard_map/ppermute | solution.py:235
  75.2 13.9 %collective-permute-start.9 = (bf16[4096,128]{1,0:T(8,128)(2,1)S(1)}, bf16[4096,128]{1,0:T(8,128)(2,1)S(1)}, u32[]{:S(2)}, u32[]{:S(2)}) collective-permute-start(bf16[4096,128]{1,0:T(8,128)(2,1)S(1)} %slice.9), channel_id=1, source_target_pairs={{0,12},{16,19},{1,13},{17,16},{2,14},{18,17},{3,15},{19,18},{4,0},... | collective-permute-start | bytes 3145736 | tf_op jit(solution)/shard_map/ppermute | solution.py:235
  75.4 15.6 %collective-permute-start.8 = (bf16[4096,128]{1,0:T(8,128)(2,1)S(1)}, bf16[4096,128]{1,0:T(8,128)(2,1)S(1)}, u32[]{:S(2)}, u32[]{:S(2)}) collective-permute-start(bf16[4096,128]{1,0:T(8,128)(2,1)S(1)} %slice.8), channel_id=1, source_target_pairs={{0,4},{16,17},{1,5},{17,18},{2,6},{18,19},{3,7},{19,16},{4,8},{20,... | collective-permute-start | bytes 3145736 | tf_op jit(solution)/shard_map/ppermute | solution.py:235
  76.8 16.6 %collective-permute-start.12 = (bf16[8192,128]{1,0:T(8,128)(2,1)S(1)}, bf16[8192,128]{1,0:T(8,128)(2,1)S(1)}, u32[]{:S(2)}, u32[]{:S(2)}) collective-permute-start(bf16[8192,128]{1,0:T(8,128)(2,1)S(1)} %collective-permute-done.7.refs_6_), channel_id=1, source_target_pairs={{0,16},{16,0},{1,17},{17,1},{2,18},{18,2},{3,19},{19,3},{4,20},{20... | collective-permute-start | bytes 6291464 | tf_op jit(solution)/shard_map/ppermute | solution.py:235
  78.5 16.4 %collective-permute-start.11 = (bf16[8192,128]{1,0:T(8,128)(2,1)S(1)}, bf16[8192,128]{1,0:T(8,128)(2,1)S(1)}, u32[]{:S(2)}, u32[]{:S(2)}) collective-permute-start(bf16[8192,128]{1,0:T(8,128)(2,1)S(1)} %collective-permute-done.6.refs_5_), channel_id=1, source_target_pairs={{0,16},{16,0},{1,17},{17,1},{2,18},{18,2},{3,19},{19,3},{4,20},{20... | collective-permute-start | bytes 6291464 | tf_op jit(solution)/shard_map/ppermute | solution.py:235
  89.1 4.2 %collective-permute-start.14 = (bf16[4096,128]{1,0:T(8,128)(2,1)S(1)}, bf16[4096,128]{1,0:T(8,128)(2,1)S(1)}, u32[]{:S(2)}, u32[]{:S(2)}) collective-permute-start(bf16[4096,128]{1,0:T(8,128)(2,1)S(1)} %collective-permute-done.9.refs_8_), channel_id=1, source_target_pairs={{0,16},{16,0},{1,17},{17,1},{2,18},{18,2},{3,19},{19,3},{4,20},{20... | collective-permute-start | bytes 3145736 | tf_op jit(solution)/shard_map/ppermute | solution.py:235
  91.1 3.8 %collective-permute-start.13 = (bf16[4096,128]{1,0:T(8,128)(2,1)S(1)}, bf16[4096,128]{1,0:T(8,128)(2,1)S(1)}, u32[]{:S(2)}, u32[]{:S(2)}) collective-permute-start(bf16[4096,128]{1,0:T(8,128)(2,1)S(1)} %collective-permute-done.8.refs_7_), channel_id=1, source_target_pairs={{0,16},{16,0},{1,17},{17,1},{2,18},{18,2},{3,19},{19,3},{4,20},{20... | collective-permute-start | bytes 3145736 | tf_op jit(solution)/shard_map/ppermute | solution.py:235
  92.6 2.3 %copy-start.2 = (bf16[8192,128]{1,0:T(8,128)(2,1)}, bf16[8192,128]{1,0:T(8,128)(2,1)S(1)}, u32[]{:S(2)}) copy-start(bf16[8192,128]{1,0:T(8,128)(2,1)S(1)} %collective-permute-done.10.refs_9_) | copy-start | bytes 6291460
  93.4 1.5 %copy-start.3 = (bf16[8192,128]{1,0:T(8,128)(2,1)}, bf16[8192,128]{1,0:T(8,128)(2,1)S(1)}, u32[]{:S(2)}) copy-start(bf16[8192,128]{1,0:T(8,128)(2,1)S(1)} %collective-permute-done.12.refs_11_) | copy-start | bytes 6291460
  94.9 1.3 copy-start.4
  121.4 0.7 copy-start.1
  122.1 8.0 %collective-permute-start.15 = (bf16[128,1024]{1,0:T(8,128)(2,1)S(1)}, bf16[128,1024]{1,0:T(8,128)(2,1)S(1)}, u32[]{:S(2)}, u32[]{:S(2)}) collective-permute-start(bf16[128,1024]{1,0:T(8,128)(2,1)S(1)} %get-tuple-element.32), channel_id=1, source_target_pairs={{0,224},{16,240},{1,225},{17,241},{2,226},{18,242},{3,227},{19,243... | collective-permute-start | bytes 786440 | tf_op jit(solution)/shard_map/ppermute | solution.py:235
  122.1 10.0 %collective-permute-start.16 = (bf16[128,1024]{1,0:T(8,128)(2,1)S(1)}, bf16[128,1024]{1,0:T(8,128)(2,1)S(1)}, u32[]{:S(2)}, u32[]{:S(2)}) collective-permute-start(bf16[128,1024]{1,0:T(8,128)(2,1)S(1)} %get-tuple-element.33), channel_id=1, source_target_pairs={{0,32},{16,48},{1,33},{17,49},{2,34},{18,50},{3,35},{19,51},{4,36}... | collective-permute-start | bytes 786440 | tf_op jit(solution)/shard_map/ppermute | solution.py:235
  123.6 15.1 %collective-permute-start.17 = (bf16[128,1024]{1,0:T(8,128)(2,1)S(1)}, bf16[128,1024]{1,0:T(8,128)(2,1)S(1)}, u32[]{:S(2)}, u32[]{:S(2)}) collective-permute-start(bf16[128,1024]{1,0:T(8,128)(2,1)S(1)} %get-tuple-element.34), channel_id=1, source_target_pairs={{0,192},{16,80},{1,193},{17,81},{2,194},{18,82},{3,195},{19,83},{4... | collective-permute-start | bytes 786440 | tf_op jit(solution)/shard_map/ppermute | solution.py:235
  130.2 8.6 %copy-start.6 = (bf16[128,1024]{1,0:T(8,128)(2,1)}, bf16[128,1024]{1,0:T(8,128)(2,1)S(1)}, u32[]{:S(2)}) copy-start(bf16[128,1024]{1,0:T(8,128)(2,1)S(1)} %collective-permute-done.15.refs_1_) | copy-start | bytes 786436
  132.1 6.6 %copy-start.7 = (bf16[128,1024]{1,0:T(8,128)(2,1)}, bf16[128,1024]{1,0:T(8,128)(2,1)S(1)}, u32[]{:S(2)}) copy-start(bf16[128,1024]{1,0:T(8,128)(2,1)S(1)} %collective-permute-done.16.refs_2_) | copy-start | bytes 786436
  138.7 0.7 copy-start.8

commit v5 on v4

v5 whole, which is shorter than its diff:
```python
import functools
import math

import jax
import jax.numpy as jnp
from jax import lax
from jax.experimental import pallas as pl
from jax.experimental.pallas import tpu as pltpu
from jax.sharding import Mesh, PartitionSpec as P

H = 32
KVH = 4
DH = 128
BLK = 64
NV = 8
NS = 24
SEQ = 32768

QB = 8
HG = H // KVH
CB = 4
CHUNKS = -(-(1 + NV + NS) // CB)
LMAX = CHUNKS * CB
SKEW = 4
C2 = math.log2(math.e) / math.sqrt(DH)
NEG = -1e30
NT = (((1,), (1,)), ((), ()))
LIMIT = 8 * 1024 * 1024
PARTS = 2
PIECE = 4 * 2048
ITEMS = HG * QB
STATE = 3 * (jax.ShapeDtypeStruct((ITEMS * BLK, DH), jnp.float32),)
VMEM = pl.BlockSpec(memory_space=pltpu.VMEM)
SMEM = pl.BlockSpec(memory_space=pltpu.SMEM)
ANY = pl.BlockSpec(memory_space=pl.ANY)


def collect_kernel(starts, count, first, *refs):
    held, swapped = refs[:count], refs[count : 2 * count]
    buffer, sem = refs[2 * count + (0 if first else 1) :]
    copies = []
    for p in range(count):
        for other, piece in enumerate((held[p], swapped[p])):
            place = pl.ds(other * 4 * PIECE + starts[p], piece.shape[0])
            copies.append(pltpu.make_async_copy(piece, buffer.at[place, :], sem.at[len(copies)]))
    for copy in copies:
        copy.start()
    for copy in copies:
        copy.wait()


def collect(held, starts, buffer):
    swapped = [send(piece, OTHER) for piece in held]
    count = len(held)
    return pl.pallas_call(
        functools.partial(collect_kernel, starts, count, not buffer),
        out_shape=[jax.ShapeDtypeStruct((8 * PIECE, DH), jnp.bfloat16)],
        in_specs=[ANY] * (2 * count) + [VMEM] * len(buffer),
        out_specs=[VMEM],
        scratch_shapes=[pltpu.SemaphoreType.DMA((2 * count,))],
        input_output_aliases={2 * count: 0} if buffer else {},
        compiler_params=pltpu.CompilerParams(vmem_limit_bytes=LIMIT),
    )(*held, *swapped, *buffer)


def attend_kernel(part, lists, counts, *refs):
    q_refs, pairs = refs[:4], refs[4]
    refs = refs[5:] if part == 0 else refs[8:]
    top_s, sum_s, acc_s = refs[:3]
    o_refs, score_s = refs[3:-1], refs[-1]
    first_list, first_count = part * LMAX * ITEMS, part * (HG + ITEMS)
    lane = lax.broadcasted_iota(jnp.int32, (BLK, CB * BLK), 1)
    row = lax.broadcasted_iota(jnp.int32, (BLK, CB * BLK), 0)
    lane_row = lax.broadcasted_iota(jnp.int32, (1, CB * BLK), 1)

    def rows(i):
        return slice(i * BLK, (i + 1) * BLK)

    def head(h, _):
        columns = pl.ds(pl.multiple_of(h * DH, DH), DH)

        def state(i):
            return pl.ds(pl.multiple_of((h * QB + i) * BLK, BLK), BLK)

        def live(i):
            return counts[first_count + HG + h * QB + i]

        def gather(i, c, ahead):
            base = first_list + c * (CB * ITEMS) + (h * QB + i)
            return jnp.concatenate(
                [
                    pairs[
                        pl.ds(
                            pl.multiple_of((lists[base + j * ITEMS] + ahead) * BLK, BLK), BLK
                        ),
                        :,
                    ]
                    for j in range(CB)
                ],
                axis=0,
            )

        def scores(i, c):
            return lax.dot_general(
                q_refs[i // 2][rows(i % 2), columns],
                gather(i, c, 0),
                NT,
                preferred_element_type=jnp.float32,
            )

        def weighted(i, c, p):
            return jnp.dot(p, gather(i, c, 2), preferred_element_type=jnp.float32)

        def first_weights(i, s):
            s = jnp.where((lane < live(i) * BLK) & ((lane >= BLK) | (lane <= row)), s, NEG)
            top = jnp.max(jnp.maximum(s[:, :128], s[:, 128:]), axis=1, keepdims=True)
            shift = top * C2
            parts = [jnp.exp2(s[:, t * 128 : (t + 1) * 128] * C2 - shift) for t in range(2)]
            top_s[state(i), :] = jnp.broadcast_to(top, (BLK, DH))
            sum_s[state(i), :] = parts[0] + parts[1]
            return jnp.concatenate([x.astype(jnp.bfloat16) for x in parts], axis=1)

        def next_weights(i, c, s):
            s = s + jnp.where(lane_row < (live(i) - c * CB) * BLK, 0.0, NEG)
            old = top_s[state(i), :]
            top = jnp.maximum(
                old, jnp.max(jnp.maximum(s[:, :128], s[:, 128:]), axis=1, keepdims=True)
            )
            shrink = jnp.exp2((old - top) * C2)
            shift = top * C2
            parts = [jnp.exp2(s[:, t * 128 : (t + 1) * 128] * C2 - shift) for t in range(2)]
            top_s[state(i), :] = top
            sum_s[state(i), :] = sum_s[state(i), :] * shrink + (parts[0] + parts[1])
            return jnp.concatenate([x.astype(jnp.bfloat16) for x in parts], axis=1), shrink

        first_chunk = 1 if part == 0 else 0
        if part == 0:
            opening = [scores(i, 0) for i in range(QB)]
        for i in range(QB):
            score_s[rows(i), :] = scores(i, first_chunk)
        if part == 0:
            weights = [first_weights(i, s) for i, s in enumerate(opening)]
            for i, p in enumerate(weights):
                acc_s[state(i), :] = weighted(i, 0, p)

        def chunk(c, _):
            ahead = jnp.minimum(c + 1, CHUNKS - 1)
            held = {}
            for t in range(QB + SKEW):
                if t < QB:
                    s = score_s[rows(t), :]
                    score_s[rows(t), :] = scores(t, ahead)
                    held[t] = next_weights(t, c, s)
                i = t - SKEW
                if i >= 0:
                    p, shrink = held.pop(i)
                    acc_s[state(i), :] = acc_s[state(i), :] * shrink + weighted(i, c, p)
            return 0

        lax.fori_loop(first_chunk, counts[first_count + h], chunk, 0)
        for i in range(QB if o_refs else 0):
            total = jnp.sum(sum_s[state(i), :], axis=1, keepdims=True)
            o_refs[i // 2][rows(i % 2), columns] = (acc_s[state(i), :] / total).astype(
                jnp.bfloat16
            )
        return 0

    lax.fori_loop(0, HG, head, 0)


def attend(part, lists, counts, queries, buffer, state):
    outputs = [jax.ShapeDtypeStruct((2 * BLK, HG * DH), jnp.bfloat16)] * (4 if part == PARTS - 1 else 0)
    return pl.pallas_call(
        functools.partial(attend_kernel, part),
        out_shape=list(STATE) + outputs,
        in_specs=[SMEM] * 2 + [VMEM] * (5 + len(state)),
        out_specs=[VMEM] * (3 + len(outputs)),
        scratch_shapes=[pltpu.VMEM((QB * BLK, CB * BLK), jnp.float32)],
        input_output_aliases={7 + n: n for n in range(len(state))},
        compiler_params=pltpu.CompilerParams(vmem_limit_bytes=LIMIT),
        cost_estimate=pl.CostEstimate(
            flops=3_000_000_000, bytes_accessed=30_000_000, transcendentals=3_000_000
        ),
    )(lists, counts, *queries, *buffer, *state)


def place_kernel(starts, *refs):
    out_ref = refs[4]
    for n in range(4):
        columns = pl.ds(pl.multiple_of(starts[n] * (HG * DH), HG * DH), HG * DH)
        out_ref[:, columns] = refs[n][...]


def place_heads(starts, pieces):
    return pl.pallas_call(
        place_kernel,
        out_shape=jax.ShapeDtypeStruct((2 * BLK, H * DH), jnp.bfloat16),
        in_specs=[pl.BlockSpec(memory_space=pltpu.SMEM)]
        + [pl.BlockSpec(memory_space=pltpu.VMEM)] * 4,
        out_specs=pl.BlockSpec(memory_space=pltpu.VMEM),
    )(starts, *pieces)


def piece_places(blocks, core, y, x):
    dy, dx = (blocks // 8 - y) % 4, (blocks // 2 - x) % 4
    half = blocks // 32 % 2
    small, big = jnp.where(half == 0, dx, dy), jnp.where(half == 0, dy, dx)

    def ring(d):
        return jnp.where(d < 2, 2 * d, 7 - 2 * d)

    inner = blocks // 64 * 4 + blocks % 2
    places = jnp.where(half == core, 0, 512) + ring(big) * 128 + ring(small) * 32 + inner
    return places, jnp.where(big == 0, 0, 1)


def block_lists(place_of, own_blocks, column_blocks, column_count, slash_offsets, slash_count):
    own = jnp.tile(own_blocks, HG)[None, :]
    column = jnp.repeat(column_blocks.T, QB, axis=1)
    column_used = jnp.arange(NV, dtype=jnp.int32)[:, None] < jnp.repeat(column_count, QB)
    slash = own - jnp.repeat(slash_offsets.T, QB, axis=1)
    slash_used = jnp.arange(NS, dtype=jnp.int32)[:, None] < jnp.repeat(slash_count, QB)
    twice = jnp.any((column[None] == slash[:, None]) & column_used[None], axis=1)
    blocks = jnp.concatenate([own, column, jnp.maximum(slash, 0)])
    usable = jnp.concatenate(
        [
            jnp.ones(own.shape, bool),
            column_used & (column < own),
            slash_used & (slash >= 0) & jnp.logical_not(twice),
        ]
    )
    places, parts = place_of(blocks)
    width = 1 + NV + NS
    earlier = (jnp.arange(width)[None, :] < jnp.arange(width)[:, None])[:, :, None]
    slot = jnp.arange(LMAX, dtype=jnp.int32)[:, None, None]
    lists, counts = [], []
    for part in range(PARTS):
        used = usable & (parts == part)
        rank = jnp.sum(used[None] & earlier, axis=1, dtype=jnp.int32)
        live = jnp.sum(used, axis=0, dtype=jnp.int32)
        packed = jnp.where(used[None] & (rank[None] == slot), places[None], 0)
        lists.append(jnp.sum(packed, axis=1))
        counts.append((jnp.max(live.reshape(HG, QB), axis=1) + CB - 1) // CB)
        counts.append(live)
    return jnp.concatenate(lists).reshape(-1), jnp.concatenate(counts)


def device_index(z, core, y, x):
    return ((z * 2 + core) * 4 + y) * 4 + x


def send(array, first, second=None):
    pairs = []
    for z in range(8):
        for y in range(4):
            for x in range(4):
                for core, (dz, dc, dy, dx) in enumerate((first, second or first)):
                    target = ((z + dz) % 8, core ^ dc, (y + dy) % 4, (x + dx) % 4)
                    pairs.append((device_index(z, core, y, x), device_index(*target)))
    return lax.ppermute(array, AXES, pairs)


AXES = ("z", "core", "y", "x")
UP_Y, DOWN_Y, UP_X, DOWN_X = (0, 0, 1, 0), (0, 0, -1, 0), (0, 0, 0, 1), (0, 0, 0, -1)
UP_Z, DOWN_Z, UP_2, DOWN_2 = (1, 0, 0, 0), (-1, 0, 0, 0), (2, 0, 0, 0), (-2, 0, 0, 0)
OTHER = (0, 1, 0, 0)


def gather_and_attend(own, lists, counts, late):
    tie = lax.optimization_barrier
    own, late = tie((own, late))
    up1 = send(own, UP_X, UP_Y)
    down1 = send(own, DOWN_X, DOWN_Y)
    up2 = send(own, (0, 0, 0, 2), (0, 0, 2, 0))
    near_queries = (late[0], send(late[1], UP_Z), send(late[2], DOWN_Z))
    up1, down1, up2, lists, counts, near_queries, far_query = tie(
        (up1, down1, up2, lists, counts, near_queries, late[3])
    )
    queries = near_queries + (send(far_query, UP_2, DOWN_2),)
    near = jnp.concatenate([own, up1, down1, up2])
    a1 = send(near, UP_Y, UP_X)
    b1 = send(near, DOWN_Y, DOWN_X)
    buffer = collect([near], [0], ())
    state = attend(0, lists, counts, queries, buffer, ())
    a1, b1, buffer, state = tie((a1, b1, buffer, state))
    a2 = send(a1[: PIECE // 2], UP_Y, UP_X)
    b2 = send(b1[PIECE // 2 :], DOWN_Y, DOWN_X)
    buffer = collect([a1, b1], [PIECE, 2 * PIECE], buffer)
    a2, b2, buffer = tie((a2, b2, buffer))
    buffer = collect([a2, b2], [3 * PIECE, 3 * PIECE + PIECE // 2], buffer)
    return attend(1, lists, counts, queries, buffer, state)[3:]


def per_device(
    query_rows, key_rows, value_rows, column_blocks, column_count, slash_offsets, slash_count
):
    tokens = query_rows.shape[0]
    z, core, y, x = (lax.axis_index(name) for name in AXES)
    group = z % KVH
    pairs = jnp.stack(
        [array.reshape(tokens, KVH, DH).transpose(1, 0, 2) for array in (key_rows, value_rows)],
        axis=1,
    )
    own = lax.all_to_all(
        jnp.concatenate([pairs, pairs]), "z", split_axis=0, concat_axis=0, tiled=True
    ).reshape(16 * tokens, DH)

    def mine(array):
        return lax.dynamic_slice_in_dim(array, group * HG, HG, 0)

    last = jnp.where(core == 0, z + 6, z + 2)
    sources = jnp.stack([z, z + 7, z + 1, last]) % 8
    own_blocks = ((sources * 2 + core) * 32 + (y * 4 + x) * 2)[:, None] + jnp.arange(2)
    lists, counts = block_lists(
        functools.partial(piece_places, core=core, y=y, x=x),
        own_blocks.reshape(-1).astype(jnp.int32),
        mine(column_blocks),
        mine(column_count),
        mine(slash_offsets),
        mine(slash_count),
    )

    def heads(step):
        start = (z + step) % KVH * (HG * DH)
        return lax.dynamic_slice_in_dim(query_rows, start, HG * DH, 1)

    late = (heads(0), heads(1), heads(3), heads(2))
    outputs = gather_and_attend(own, lists, counts, late)
    pieces = (
        outputs[0],
        send(outputs[1], DOWN_Z),
        send(outputs[2], UP_Z),
        send(outputs[3], DOWN_2, UP_2),
    )
    starts = jnp.stack([z, z + 1, z + 3, z + 2]) % KVH
    return place_heads(starts.astype(jnp.int32), pieces)


def solution(mesh):
    fine = Mesh(mesh.devices.reshape(8, 2, 4, 4), AXES)
    split = P(AXES, None)
    return jax.shard_map(
        per_device,
        mesh=fine,
        in_specs=(split, split, split, P(), P(), P(), P()),
        out_specs=split,
        check_vma=False,
    )
```

time: 143 us -> 136 us (0.951); the launches traced: 142 us -> 138 us
  waiting for transfers between devices: 75.9 us -> 72.8 us
    ppermute x18, waiting for transfers between devices: 61.1 us -> 58.7 us  [send(): return lax.ppermute(array, AXES, pairs)]
    reshape x3, local copies, waits for them, and re-layouts: 2.05 us -> 0.23 us  [the longest x2 0.16 us: block_lists(): counts.append((jnp.max(live.reshape(HG, QB), axis=1) + CB - 1) // CB)]
    pallas_call x1 -> x5, Pallas kernels: 25.2 us -> 26.1 us  [the longest x2 24.9 us: attend(): pl.pallas_call(functools.partial(attend_kernel, part), out_shape=list(STA...]
    unnamed x27 -> x23, local copies, waits for them, and re-layouts: 2.9 us -> 2.49 us
  transfers between devices with their start and end apart: 19 -> 19, of which waited for: 11 -> 15; matrix products, arithmetic and copies ran while one was open for 2% -> 3% of each run, Pallas kernels for 0% -> 7%
where the time goes in v5:
time: 136 us; the launch traced here: 138 us
  waiting for transfers between devices  72.8 us (54%)
  Pallas kernels  28.4 us (21%)
  starting transfers between devices  27.2 us (20%)
  local copies, waits for them, and re-layouts  6.02 us (4%)
  other arithmetic  3.07 us (2%)
    ppermute x18, waiting for transfers between devices, send(): return lax.ppermute(array, AXES, pairs)  58.7 us
    pallas_call x2, Pallas kernels, attend(): pl.pallas_call(functools.partial(attend_kernel, part), out_shape=list(STA...  24.9 us
    ppermute x18, starting transfers between devices, send(): return lax.ppermute(array, AXES, pairs)  18.1 us
    all_to_all x1, waiting for transfers between devices, per_device(): lax.all_to_all(jnp.concatenate([pairs, pairs]), 'z', split_axis=0, concat...  14.1 us
    all_to_all x1, starting transfers between devices, per_device(): lax.all_to_all(jnp.concatenate([pairs, pairs]), 'z', split_axis=0, concat...  9.01 us
  transfers between devices with their start and end apart: 19, of which 15 were waited for; matrix products, arithmetic and copies ran while one was open for 3% of the time, Pallas kernels for 7%

profile of v5, /device:TPU:1, one launch (start us, length us, event | category | flops | bytes accessed | tf_op | source)
XLA Modules:
  0.0 137.7 jit_solution(16090949836795843024)
XLA Ops:
  0.0 0.9 copy-done
  0.9 1.0 bitcast_bitcast_fusion
  2.0 0.8 maximum_maximum_fusion
  2.8 9.0 %all-to-all-start = ((bf16[8,2,128,128]{3,2,1,0:T(8,128)(2,1)}), bf16[8,2,128,128]{3,2,1,0:T(8,128)(2,1)S(1)}, u32[]{:S(2)}, u32[]{:S(2)}) async-start(bf16[8,2,128,128]{3,2,1,0:T(8,128)(2,1)} %maximum_maximum_fusion), calls=%async_computation | async-start | bytes 1048576 | tf_op jit(solution)/shard_map/all_to_all | solution.py:304
  11.8 0.1 fusion.30
  12.9 0.1 dynamic_slice.30
  13.3 0.1 convert_reduce_fusion.3
  13.4 0.1 convert_reduce_fusion.2
  13.7 0.1 reduce_max.19
  13.8 0.1 reduce_max.18
  14.0 0.3 convert_reduce_fusion.1
  14.3 0.4 select_reduce_fusion.1
  14.8 0.9 constant_dynamic-slice_fusion
  15.6 14.1 %all-to-all-done = bf16[8,2,128,128]{3,2,1,0:T(8,128)(2,1)S(1)} async-done(((bf16[8,2,128,128]{3,2,1,0:T(8,128)(2,1)}), bf16[8,2,128,128]{3,2,1,0:T(8,128)(2,1)S(1)}, u32[]{:S(2)}, u32[]{:S(2)}) %all-to-all-start) | async-done | bytes 524320 | tf_op jit(solution)/shard_map/all_to_all | solution.py:304
  29.8 1.3 collective-permute-start
  31.1 1.4 %collective-permute-start.1 = (bf16[2048,128]{1,0:T(8,128)(2,1)S(1)}, bf16[2048,128]{1,0:T(8,128)(2,1)S(1)}, u32[]{:S(2)}, u32[]{:S(2)}) collective-permute-start(bf16[2048,128]{1,0:T(8,128)(2,1)S(1)} %bitcast.33), channel_id=1, source_target_pairs={{0,3},{16,28},{1,0},{17,29},{2,1},{18,30},{3,2},{19,31},{4,7},{20,... | collective-permute-start | bytes 1572872 | tf_op jit(solution)/shard_map/ppermute | solution.py:260
  32.5 1.6 %collective-permute-start.2 = (bf16[2048,128]{1,0:T(8,128)(2,1)S(1)}, bf16[2048,128]{1,0:T(8,128)(2,1)S(1)}, u32[]{:S(2)}, u32[]{:S(2)}) collective-permute-start(bf16[2048,128]{1,0:T(8,128)(2,1)S(1)} %bitcast.34), channel_id=1, source_target_pairs={{0,2},{16,24},{1,3},{17,25},{2,0},{18,26},{3,1},{19,27},{4,6},{20,... | collective-permute-start | bytes 1572872 | tf_op jit(solution)/shard_map/ppermute | solution.py:260
  34.2 2.7 %collective-permute-start.4 = (bf16[128,1024]{1,0:T(8,128)(2,1)}, bf16[128,1024]{1,0:T(8,128)(2,1)S(1)}, u32[]{:S(2)}, u32[]{:S(2)}) collective-permute-start(bf16[128,1024]{1,0:T(8,128)(2,1)} %get-tuple-element.38), channel_id=1, source_target_pairs={{0,224},{16,240},{1,225},{17,241},{2,226},{18,242},{3,227},{19,243... | collective-permute-start | bytes 786440 | tf_op jit(solution)/shard_map/ppermute | solution.py:260
  37.1 5.2 %collective-permute-done.3.refs_1_ = bf16[128,1024]{1,0:T(8,128)(2,1)S(1)} collective-permute-done((bf16[128,1024]{1,0:T(8,128)(2,1)}, bf16[128,1024]{1,0:T(8,128)(2,1)S(1)}, u32[]{:S(2)}, u32[]{:S(2)}) %collective-permute-start.3) | collective-permute-done | bytes 262176 | tf_op jit(solution)/shard_map/ppermute | solution.py:260
  42.3 3.9 %collective-permute-done.2 = bf16[2048,128]{1,0:T(8,128)(2,1)S(1)} collective-permute-done((bf16[2048,128]{1,0:T(8,128)(2,1)S(1)}, bf16[2048,128]{1,0:T(8,128)(2,1)S(1)}, u32[]{:S(2)}, u32[]{:S(2)}) %collective-permute-start.2) | collective-permute-done | bytes 524320 | tf_op jit(solution)/shard_map/ppermute | solution.py:260
  46.4 1.2 collective-permute-start.8
  47.6 1.1 collective-permute-start.6
  48.7 1.5 %collective-permute-start.7 = (bf16[8192,128]{1,0:T(8,128)(2,1)S(1)}, bf16[8192,128]{1,0:T(8,128)(2,1)S(1)}, u32[]{:S(2)}, u32[]{:S(2)}) collective-permute-start(bf16[8192,128]{1,0:T(8,128)(2,1)S(1)} %constant_dynamic-update-slice_fusion.refs_0_), channel_id=1, source_target_pairs={{0,12},{16,19},{1,13},{17,16},{2,14},{18,17},{3,15},{19,18},{4,0},... | collective-permute-start | bytes 6291464 | tf_op jit(solution)/shard_map/ppermute | solution.py:260
  50.3 1.0 collective-permute-done.8.refs_1_
  51.3 0.3 shard_map.73.refs_4_
  51.7 7.8 %collective-permute-done.5.refs_3_ = bf16[128,1024]{1,0:T(8,128)(2,1)S(1)} collective-permute-done((bf16[128,1024]{1,0:T(8,128)(2,1)S(1)}, bf16[128,1024]{1,0:T(8,128)(2,1)S(1)}, u32[]{:S(2)}, u32[]{:S(2)}) %collective-permute-start.5) | collective-permute-done | bytes 262176 | tf_op jit(solution)/shard_map/ppermute | solution.py:260
  59.5 9.2 %shard_map.74 = (f32[4096,128]{1,0:T(8,128)S(1)}, f32[4096,128]{1,0:T(8,128)S(1)}, f32[4096,128]{1,0:T(8,128)S(1)}) custom-call(s32[4608]{0:T(1024)S(1)} %reshape.689.lists, s32[144]{0:T(256)S(1)} %pad_add_fusion.3.counts, bf16[128,1024]{1,0:T(8,128)(2,1)S(1)} %get-tuple-element.42.refs_0_, bf16[128,1024]{1,0:T(8,128)(2,1)S(1)} %collective-permute-done.3.refs_1_, ...), custom_call_target="tpu_custom_call" | custom-call | flops 3000000000 | bytes 30000000 | tf_op jit(solution)/shard_map/pallas_call | solution.py:173
  68.6 5.3 %collective-permute-done.6.refs_0_ = bf16[8192,128]{1,0:T(8,128)(2,1)S(1)} collective-permute-done((bf16[8192,128]{1,0:T(8,128)(2,1)S(1)}, bf16[8192,128]{1,0:T(8,128)(2,1)S(1)}, u32[]{:S(2)}, u32[]{:S(2)}) %collective-permute-start.6) | collective-permute-done | bytes 2097184 | tf_op jit(solution)/shard_map/ppermute | solution.py:260
  74.0 1.3 collective-permute-start.11
  75.4 2.1 %collective-permute-start.10 = (bf16[4096,128]{1,0:T(8,128)(2,1)S(1)}, bf16[4096,128]{1,0:T(8,128)(2,1)S(1)}, u32[]{:S(2)}, u32[]{:S(2)}) collective-permute-start(bf16[4096,128]{1,0:T(8,128)(2,1)S(1)} %slice.7), channel_id=1, source_target_pairs={{0,12},{16,19},{1,13},{17,16},{2,14},{18,17},{3,15},{19,18},{4,0},... | collective-permute-start | bytes 3145736 | tf_op jit(solution)/shard_map/ppermute | solution.py:260
  77.5 1.6 %collective-permute-done.11.refs_2_ = bf16[8192,128]{1,0:T(8,128)(2,1)S(1)} collective-permute-done((bf16[8192,128]{1,0:T(8,128)(2,1)S(1)}, bf16[8192,128]{1,0:T(8,128)(2,1)S(1)}, u32[]{:S(2)}, u32[]{:S(2)}) %collective-permute-start.11) | collective-permute-done | bytes 2097184 | tf_op jit(solution)/shard_map/ppermute | solution.py:260
  79.0 3.0 %collective-permute-done.12.refs_3_ = bf16[8192,128]{1,0:T(8,128)(2,1)S(1)} collective-permute-done((bf16[8192,128]{1,0:T(8,128)(2,1)S(1)}, bf16[8192,128]{1,0:T(8,128)(2,1)S(1)}, u32[]{:S(2)}, u32[]{:S(2)}) %collective-permute-start.12) | collective-permute-done | bytes 2097184 | tf_op jit(solution)/shard_map/ppermute | solution.py:260
  82.0 0.6 shard_map.75.refs_4_
  82.7 6.8 %collective-permute-done.10.refs_1_ = bf16[4096,128]{1,0:T(8,128)(2,1)S(1)} collective-permute-done((bf16[4096,128]{1,0:T(8,128)(2,1)S(1)}, bf16[4096,128]{1,0:T(8,128)(2,1)S(1)}, u32[]{:S(2)}, u32[]{:S(2)}) %collective-permute-start.10) | collective-permute-done | bytes 1048608 | tf_op jit(solution)/shard_map/ppermute | solution.py:260
  89.4 3.2 %collective-permute-done.9.refs_0_ = bf16[4096,128]{1,0:T(8,128)(2,1)S(1)} collective-permute-done((bf16[4096,128]{1,0:T(8,128)(2,1)S(1)}, bf16[4096,128]{1,0:T(8,128)(2,1)S(1)}, u32[]{:S(2)}, u32[]{:S(2)}) %collective-permute-start.9) | collective-permute-done | bytes 1048608 | tf_op jit(solution)/shard_map/ppermute | solution.py:260
  92.6 2.3 %collective-permute-start.13 = (bf16[4096,128]{1,0:T(8,128)(2,1)S(1)}, bf16[4096,128]{1,0:T(8,128)(2,1)S(1)}, u32[]{:S(2)}, u32[]{:S(2)}) collective-permute-start(bf16[4096,128]{1,0:T(8,128)(2,1)S(1)} %collective-permute-done.9.refs_0_), channel_id=1, source_target_pairs={{0,16},{16,0},{1,17},{17,1},{2,18},{18,2},{3,19},{19,3},{4,20},{20... | collective-permute-start | bytes 3145736 | tf_op jit(solution)/shard_map/ppermute | solution.py:260
  94.9 2.3 %collective-permute-done.13.refs_2_ = bf16[4096,128]{1,0:T(8,128)(2,1)S(1)} collective-permute-done((bf16[4096,128]{1,0:T(8,128)(2,1)S(1)}, bf16[4096,128]{1,0:T(8,128)(2,1)S(1)}, u32[]{:S(2)}, u32[]{:S(2)}) %collective-permute-start.13) | collective-permute-done | bytes 1048608 | tf_op jit(solution)/shard_map/ppermute | solution.py:260
  97.2 1.5 %collective-permute-done.14.refs_3_ = bf16[4096,128]{1,0:T(8,128)(2,1)S(1)} collective-permute-done((bf16[4096,128]{1,0:T(8,128)(2,1)S(1)}, bf16[4096,128]{1,0:T(8,128)(2,1)S(1)}, u32[]{:S(2)}, u32[]{:S(2)}) %collective-permute-start.14) | collective-permute-done | bytes 1048608 | tf_op jit(solution)/shard_map/ppermute | solution.py:260
  98.7 0.3 shard_map.76.refs_4_
  99.0 15.8 %shard_map.77 = (f32[4096,128]{1,0:T(8,128)S(1)}, f32[4096,128]{1,0:T(8,128)S(1)}, f32[4096,128]{1,0:T(8,128)S(1)}, bf16[128,1024]{1,0:T(8,128)(2,1)S(1)}, bf16[...) custom-call(s32[4608]{0:T(1024)S(1)} %reshape.689.lists, ...), custom_call_target="tpu_custom_call", output_to_operand_aliasing={{0}: (7, {}), {1}: (8, {}), {2}: (9, {})} | custom-call | flops 3000000000 | bytes 30000000 | tf_op jit(solution)/shard_map/pallas_call | solution.py:173
  114.8 0.7 copy-done.1
  115.5 1.5 %collective-permute-start.16 = (bf16[128,1024]{1,0:T(8,128)(2,1)S(1)}, bf16[128,1024]{1,0:T(8,128)(2,1)S(1)}, u32[]{:S(2)}, u32[]{:S(2)}) collective-permute-start(bf16[128,1024]{1,0:T(8,128)(2,1)S(1)} %get-tuple-element.63), channel_id=1, source_target_pairs={{0,32},{16,48},{1,33},{17,49},{2,34},{18,50},{3,35},{19,51},{4,36}... | collective-permute-start | bytes 786440 | tf_op jit(solution)/shard_map/ppermute | solution.py:260
  116.9 0.7 and_select_fusion.3.starts
  117.6 4.9 %collective-permute-done.15.refs_1_ = bf16[128,1024]{1,0:T(8,128)(2,1)S(1)} collective-permute-done((bf16[128,1024]{1,0:T(8,128)(2,1)S(1)}, bf16[128,1024]{1,0:T(8,128)(2,1)S(1)}, u32[]{:S(2)}, u32[]{:S(2)}) %collective-permute-start.15) | collective-permute-done | bytes 262176 | tf_op jit(solution)/shard_map/ppermute | solution.py:260
  122.5 4.4 %collective-permute-done.16.refs_2_ = bf16[128,1024]{1,0:T(8,128)(2,1)S(1)} collective-permute-done((bf16[128,1024]{1,0:T(8,128)(2,1)S(1)}, bf16[128,1024]{1,0:T(8,128)(2,1)S(1)}, u32[]{:S(2)}, u32[]{:S(2)}) %collective-permute-start.16) | collective-permute-done | bytes 262176 | tf_op jit(solution)/shard_map/ppermute | solution.py:260
  126.9 7.8 %collective-permute-done.17.refs_3_ = bf16[128,1024]{1,0:T(8,128)(2,1)S(1)} collective-permute-done((bf16[128,1024]{1,0:T(8,128)(2,1)S(1)}, bf16[128,1024]{1,0:T(8,128)(2,1)S(1)}, u32[]{:S(2)}, u32[]{:S(2)}) %collective-permute-start.17) | collective-permute-done | bytes 262176 | tf_op jit(solution)/shard_map/ppermute | solution.py:260
  134.8 0.7 copy-done.5
  135.5 2.2 %shard_map.78 = bf16[128,4096]{1,0:T(8,128)(2,1)} custom-call(s32[4]{0:T(128)} %and_select_fusion.3.starts, bf16[128,1024]{1,0:T(8,128)(2,1)} %copy-done.1, bf16[128,1024]{1,0:T(8,128)(2,1)} %copy-done.3, bf16[128,1024]{1,0:T(8,128)(2,1)} %copy-done.4, bf16[128,1024]{1,0:T(8,128)(2,1)} %copy-done.5), custom_call_target="tpu_custom_call" | custom-call | tf_op jit(solution)/shard_map/pallas_call | solution.py:195
  (63 shorter events, 2.2 us)
Async XLA Ops:
  0.0 0.9 copy-start
  0.0 12.2 %copy-start.7 = (s32[32,8]{0,1:T(8,128)S(1)}, s32[32,8]{0,1:T(8,128)}, u32[]{:S(2)}) copy-start(s32[32,8]{0,1:T(8,128)} %param.10) | copy-start | bytes 3076
  0.0 12.4 %copy-start.8 = (s32[32]{0:T(128)S(1)}, s32[32]{0:T(128)}, u32[]{:S(2)}) copy-start(s32[32]{0:T(128)} %param.11) | copy-start | bytes 388
  0.0 12.7 %copy-start.6 = (s32[32,24]{0,1:T(8,128)S(1)}, s32[32,24]{0,1:T(8,128)}, u32[]{:S(2)}) copy-start(s32[32,24]{0,1:T(8,128)} %param.12) | copy-start | bytes 9220
  0.0 12.9 %copy-start.9 = (s32[32]{0:T(128)S(1)}, s32[32]{0:T(128)}, u32[]{:S(2)}) copy-start(s32[32]{0:T(128)} %param.13) | copy-start | bytes 388
  0.9 13.9 %copy-start.2 = (bf16[128,4096]{1,0:T(8,128)(2,1)S(1)}, bf16[128,4096]{1,0:T(8,128)(2,1)}, u32[]{:S(2)}) copy-start(bf16[128,4096]{1,0:T(8,128)(2,1)} %param.7) | copy-start | bytes 3145732
  2.8 27.0 %all-to-all-start = ((bf16[8,2,128,128]{3,2,1,0:T(8,128)(2,1)}), bf16[8,2,128,128]{3,2,1,0:T(8,128)(2,1)S(1)}, u32[]{:S(2)}, u32[]{:S(2)}) async-start(bf16[8,2,128,128]{3,2,1,0:T(8,128)(2,1)} %maximum_maximum_fusion), calls=%async_computation | async-start | bytes 1048576 | tf_op jit(solution)/shard_map/all_to_all | solution.py:304
  29.8 12.5 %collective-permute-start = (bf16[2048,128]{1,0:T(8,128)(2,1)S(1)}, bf16[2048,128]{1,0:T(8,128)(2,1)S(1)}, u32[]{:S(2)}, u32[]{:S(2)}) collective-permute-start(bf16[2048,128]{1,0:T(8,128)(2,1)S(1)} %bitcast.32), channel_id=1, source_target_pairs={{0,1},{16,20},{1,2},{17,21},{2,3},{18,22},{3,0},{19,23},{4,5},{20,... | collective-permute-start | bytes 1572872 | tf_op jit(solution)/shard_map/ppermute | solution.py:260
  31.1 11.2 %collective-permute-start.1 = (bf16[2048,128]{1,0:T(8,128)(2,1)S(1)}, bf16[2048,128]{1,0:T(8,128)(2,1)S(1)}, u32[]{:S(2)}, u32[]{:S(2)}) collective-permute-start(bf16[2048,128]{1,0:T(8,128)(2,1)S(1)} %bitcast.33), channel_id=1, source_target_pairs={{0,3},{16,28},{1,0},{17,29},{2,1},{18,30},{3,2},{19,31},{4,7},{20,... | collective-permute-start | bytes 1572872 | tf_op jit(solution)/shard_map/ppermute | solution.py:260
  32.5 13.7 %collective-permute-start.2 = (bf16[2048,128]{1,0:T(8,128)(2,1)S(1)}, bf16[2048,128]{1,0:T(8,128)(2,1)S(1)}, u32[]{:S(2)}, u32[]{:S(2)}) collective-permute-start(bf16[2048,128]{1,0:T(8,128)(2,1)S(1)} %bitcast.34), channel_id=1, source_target_pairs={{0,2},{16,24},{1,3},{17,25},{2,0},{18,26},{3,1},{19,27},{4,6},{20,... | collective-permute-start | bytes 1572872 | tf_op jit(solution)/shard_map/ppermute | solution.py:260
  34.2 8.1 %collective-permute-start.3 = (bf16[128,1024]{1,0:T(8,128)(2,1)}, bf16[128,1024]{1,0:T(8,128)(2,1)S(1)}, u32[]{:S(2)}, u32[]{:S(2)}) collective-permute-start(bf16[128,1024]{1,0:T(8,128)(2,1)} %get-tuple-element.37), channel_id=1, source_target_pairs={{0,32},{16,48},{1,33},{17,49},{2,34},{18,50},{3,35},{19,51},{4,36}... | collective-permute-start | bytes 786440 | tf_op jit(solution)/shard_map/ppermute | solution.py:260
  34.2 8.0 %collective-permute-start.4 = (bf16[128,1024]{1,0:T(8,128)(2,1)}, bf16[128,1024]{1,0:T(8,128)(2,1)S(1)}, u32[]{:S(2)}, u32[]{:S(2)}) collective-permute-start(bf16[128,1024]{1,0:T(8,128)(2,1)} %get-tuple-element.38), channel_id=1, source_target_pairs={{0,224},{16,240},{1,225},{17,241},{2,226},{18,242},{3,227},{19,243... | collective-permute-start | bytes 786440 | tf_op jit(solution)/shard_map/ppermute | solution.py:260
  46.4 5.0 %collective-permute-start.8 = (bf16[8192,128]{1,0:T(8,128)(2,1)S(1)}, bf16[8192,128]{1,0:T(8,128)(2,1)S(1)}, u32[]{:S(2)}, u32[]{:S(2)}) collective-permute-start(bf16[8192,128]{1,0:T(8,128)(2,1)S(1)} %constant_dynamic-update-slice_fusion.refs_0_), channel_id=1, source_target_pairs={{0,16},{16,0},{1,17},{17,1},{2,18},{18,2},{3,19},{19,3},{4,20},{20... | collective-permute-start | bytes 6291464 | tf_op jit(solution)/shard_map/ppermute | solution.py:260
  47.6 26.4 %collective-permute-start.6 = (bf16[8192,128]{1,0:T(8,128)(2,1)S(1)}, bf16[8192,128]{1,0:T(8,128)(2,1)S(1)}, u32[]{:S(2)}, u32[]{:S(2)}) collective-permute-start(bf16[8192,128]{1,0:T(8,128)(2,1)S(1)} %constant_dynamic-update-slice_fusion.refs_0_), channel_id=1, source_target_pairs={{0,4},{16,17},{1,5},{17,18},{2,6},{18,19},{3,7},{19,16},{4,8},{20,... | collective-permute-start | bytes 6291464 | tf_op jit(solution)/shard_map/ppermute | solution.py:260
  48.7 25.3 %collective-permute-start.7 = (bf16[8192,128]{1,0:T(8,128)(2,1)S(1)}, bf16[8192,128]{1,0:T(8,128)(2,1)S(1)}, u32[]{:S(2)}, u32[]{:S(2)}) collective-permute-start(bf16[8192,128]{1,0:T(8,128)(2,1)S(1)} %constant_dynamic-update-slice_fusion.refs_0_), channel_id=1, source_target_pairs={{0,12},{16,19},{1,13},{17,16},{2,14},{18,17},{3,15},{19,18},{4,0},... | collective-permute-start | bytes 6291464 | tf_op jit(solution)/shard_map/ppermute | solution.py:260
  50.2 9.2 %collective-permute-start.5 = (bf16[128,1024]{1,0:T(8,128)(2,1)S(1)}, bf16[128,1024]{1,0:T(8,128)(2,1)S(1)}, u32[]{:S(2)}, u32[]{:S(2)}) collective-permute-start(bf16[128,1024]{1,0:T(8,128)(2,1)S(1)} %get-tuple-element.45), channel_id=1, source_target_pairs={{0,64},{16,208},{1,65},{17,209},{2,66},{18,210},{3,67},{19,211},{4... | collective-permute-start | bytes 786440 | tf_op jit(solution)/shard_map/ppermute | solution.py:260
  74.0 5.1 %collective-permute-start.11 = (bf16[8192,128]{1,0:T(8,128)(2,1)S(1)}, bf16[8192,128]{1,0:T(8,128)(2,1)S(1)}, u32[]{:S(2)}, u32[]{:S(2)}) collective-permute-start(bf16[8192,128]{1,0:T(8,128)(2,1)S(1)} %collective-permute-done.6.refs_0_), channel_id=1, source_target_pairs={{0,16},{16,0},{1,17},{17,1},{2,18},{18,2},{3,19},{19,3},{4,20},{20... | collective-permute-start | bytes 6291464 | tf_op jit(solution)/shard_map/ppermute | solution.py:260
  75.3 6.8 %collective-permute-start.12 = (bf16[8192,128]{1,0:T(8,128)(2,1)S(1)}, bf16[8192,128]{1,0:T(8,128)(2,1)S(1)}, u32[]{:S(2)}, u32[]{:S(2)}) collective-permute-start(bf16[8192,128]{1,0:T(8,128)(2,1)S(1)} %collective-permute-done.7.refs_1_), channel_id=1, source_target_pairs={{0,16},{16,0},{1,17},{17,1},{2,18},{18,2},{3,19},{19,3},{4,20},{20... | collective-permute-start | bytes 6291464 | tf_op jit(solution)/shard_map/ppermute | solution.py:260
  75.4 14.0 %collective-permute-start.10 = (bf16[4096,128]{1,0:T(8,128)(2,1)S(1)}, bf16[4096,128]{1,0:T(8,128)(2,1)S(1)}, u32[]{:S(2)}, u32[]{:S(2)}) collective-permute-start(bf16[4096,128]{1,0:T(8,128)(2,1)S(1)} %slice.7), channel_id=1, source_target_pairs={{0,12},{16,19},{1,13},{17,16},{2,14},{18,17},{3,15},{19,18},{4,0},... | collective-permute-start | bytes 3145736 | tf_op jit(solution)/shard_map/ppermute | solution.py:260
  77.5 15.2 %collective-permute-start.9 = (bf16[4096,128]{1,0:T(8,128)(2,1)S(1)}, bf16[4096,128]{1,0:T(8,128)(2,1)S(1)}, u32[]{:S(2)}, u32[]{:S(2)}) collective-permute-start(bf16[4096,128]{1,0:T(8,128)(2,1)S(1)} %slice.6), channel_id=1, source_target_pairs={{0,4},{16,17},{1,5},{17,18},{2,6},{18,19},{3,7},{19,16},{4,8},{20,... | collective-permute-start | bytes 3145736 | tf_op jit(solution)/shard_map/ppermute | solution.py:260
  92.6 4.5 %collective-permute-start.13 = (bf16[4096,128]{1,0:T(8,128)(2,1)S(1)}, bf16[4096,128]{1,0:T(8,128)(2,1)S(1)}, u32[]{:S(2)}, u32[]{:S(2)}) collective-permute-start(bf16[4096,128]{1,0:T(8,128)(2,1)S(1)} %collective-permute-done.9.refs_0_), channel_id=1, source_target_pairs={{0,16},{16,0},{1,17},{17,1},{2,18},{18,2},{3,19},{19,3},{4,20},{20... | collective-permute-start | bytes 3145736 | tf_op jit(solution)/shard_map/ppermute | solution.py:260
  94.9 3.8 %collective-permute-start.14 = (bf16[4096,128]{1,0:T(8,128)(2,1)S(1)}, bf16[4096,128]{1,0:T(8,128)(2,1)S(1)}, u32[]{:S(2)}, u32[]{:S(2)}) collective-permute-start(bf16[4096,128]{1,0:T(8,128)(2,1)S(1)} %collective-permute-done.10.refs_1_), channel_id=1, source_target_pairs={{0,16},{16,0},{1,17},{17,1},{2,18},{18,2},{3,19},{19,3},{4,20},{20... | collective-permute-start | bytes 3145736 | tf_op jit(solution)/shard_map/ppermute | solution.py:260
  114.8 0.7 copy-start.1
  115.5 7.0 %collective-permute-start.15 = (bf16[128,1024]{1,0:T(8,128)(2,1)S(1)}, bf16[128,1024]{1,0:T(8,128)(2,1)S(1)}, u32[]{:S(2)}, u32[]{:S(2)}) collective-permute-start(bf16[128,1024]{1,0:T(8,128)(2,1)S(1)} %get-tuple-element.62), channel_id=1, source_target_pairs={{0,224},{16,240},{1,225},{17,241},{2,226},{18,242},{3,227},{19,243... | collective-permute-start | bytes 786440 | tf_op jit(solution)/shard_map/ppermute | solution.py:260
  115.5 11.5 %collective-permute-start.16 = (bf16[128,1024]{1,0:T(8,128)(2,1)S(1)}, bf16[128,1024]{1,0:T(8,128)(2,1)S(1)}, u32[]{:S(2)}, u32[]{:S(2)}) collective-permute-start(bf16[128,1024]{1,0:T(8,128)(2,1)S(1)} %get-tuple-element.63), channel_id=1, source_target_pairs={{0,32},{16,48},{1,33},{17,49},{2,34},{18,50},{3,35},{19,51},{4,36}... | collective-permute-start | bytes 786440 | tf_op jit(solution)/shard_map/ppermute | solution.py:260
  116.9 17.9 %collective-permute-start.17 = (bf16[128,1024]{1,0:T(8,128)(2,1)S(1)}, bf16[128,1024]{1,0:T(8,128)(2,1)S(1)}, u32[]{:S(2)}, u32[]{:S(2)}) collective-permute-start(bf16[128,1024]{1,0:T(8,128)(2,1)S(1)} %get-tuple-element.64), channel_id=1, source_target_pairs={{0,192},{16,80},{1,193},{17,81},{2,194},{18,82},{3,195},{19,83},{4... | collective-permute-start | bytes 786440 | tf_op jit(solution)/shard_map/ppermute | solution.py:260
  122.5 12.3 %copy-start.3 = (bf16[128,1024]{1,0:T(8,128)(2,1)}, bf16[128,1024]{1,0:T(8,128)(2,1)S(1)}, u32[]{:S(2)}) copy-start(bf16[128,1024]{1,0:T(8,128)(2,1)S(1)} %collective-permute-done.15.refs_1_) | copy-start | bytes 786436
  126.9 7.9 %copy-start.4 = (bf16[128,1024]{1,0:T(8,128)(2,1)}, bf16[128,1024]{1,0:T(8,128)(2,1)S(1)}, u32[]{:S(2)}) copy-start(bf16[128,1024]{1,0:T(8,128)(2,1)S(1)} %collective-permute-done.16.refs_2_) | copy-start | bytes 786436
  134.8 0.7 copy-start.5

commit v6 on v5

--- a/solution.py
+++ b/solution.py
@@ -85,8 +85,8 @@
         def live(i):
             return counts[first_count + HG + h * QB + i]
 
-        def gather(i, c, ahead):
-            base = first_list + c * (CB * ITEMS) + (h * QB + i)
+        def gather(i, c, ahead, g=h):
+            base = first_list + c * (CB * ITEMS) + (g * QB + i)
             return jnp.concatenate(
                 [
                     pairs[
@@ -100,10 +100,10 @@
                 axis=0,
             )
 
-        def scores(i, c):
+        def scores(i, c, g=h):
             return lax.dot_general(
-                q_refs[i // 2][rows(i % 2), columns],
-                gather(i, c, 0),
+                q_refs[i // 2][rows(i % 2), pl.ds(pl.multiple_of(g * DH, DH), DH)],
+                gather(i, c, 0, g),
                 NT,
                 preferred_element_type=jnp.float32,
             )
@@ -134,22 +134,34 @@
             return jnp.concatenate([x.astype(jnp.bfloat16) for x in parts], axis=1), shrink
 
         first_chunk = 1 if part == 0 else 0
+        chunks = counts[first_count + h]
         if part == 0:
             opening = [scores(i, 0) for i in range(QB)]
-        for i in range(QB):
-            score_s[rows(i), :] = scores(i, first_chunk)
+            for i in range(QB):
+                score_s[rows(i), :] = scores(i, first_chunk)
+        else:
+            chunks = jnp.maximum(chunks, 1)
+
+            @pl.when(h == 0)
+            def _():
+                for i in range(QB):
+                    score_s[rows(i), :] = scores(i, 0)
+
         if part == 0:
             weights = [first_weights(i, s) for i, s in enumerate(opening)]
             for i, p in enumerate(weights):
                 acc_s[state(i), :] = weighted(i, 0, p)
 
         def chunk(c, _):
-            ahead = jnp.minimum(c + 1, CHUNKS - 1)
+            ahead, next_head = jnp.minimum(c + 1, CHUNKS - 1), h
+            if part:
+                ahead = jnp.where(c + 1 < chunks, c + 1, 0)
+                next_head = jnp.where(c + 1 < chunks, h, jnp.minimum(h + 1, HG - 1))
             held = {}
             for t in range(QB + SKEW):
                 if t < QB:
                     s = score_s[rows(t), :]
-                    score_s[rows(t), :] = scores(t, ahead)
+                    score_s[rows(t), :] = scores(t, ahead, next_head)
                     held[t] = next_weights(t, c, s)
                 i = t - SKEW
                 if i >= 0:
@@ -157,7 +169,7 @@
                     acc_s[state(i), :] = acc_s[state(i), :] * shrink + weighted(i, c, p)
             return 0
 
-        lax.fori_loop(first_chunk, counts[first_count + h], chunk, 0)
+        lax.fori_loop(first_chunk, chunks, chunk, 0)
         for i in range(QB if o_refs else 0):
             total = jnp.sum(sum_s[state(i), :], axis=1, keepdims=True)
             o_refs[i // 2][rows(i % 2), columns] = (acc_s[state(i), :] / total).astype(

time: 136 us -> 133 us (0.978); the launches traced: 138 us -> 131 us
  waiting for transfers between devices: 72.8 us -> 66 us
    ppermute x18, waiting for transfers between devices: 58.7 us -> 51.9 us  [send(): return lax.ppermute(array, AXES, pairs)]
  transfers between devices with their start and end apart: 19 -> 19, of which waited for: 15 -> 15; matrix products, arithmetic and copies ran while one was open for 3% -> 4% of each run, Pallas kernels for 7% -> 7%
where the time goes in v6:
time: 133 us; the launch traced here: 131 us
  waiting for transfers between devices  66 us (50%)
  Pallas kernels  28.4 us (21%)
  starting transfers between devices  27.2 us (20%)
  local copies, waits for them, and re-layouts  6.02 us (5%)
  other arithmetic  3.07 us (2%)
    ppermute x18, waiting for transfers between devices, send(): return lax.ppermute(array, AXES, pairs)  51.9 us
    pallas_call x2, Pallas kernels, attend(): pl.pallas_call(functools.partial(attend_kernel, part), out_shape=list(STA...  24.9 us
    ppermute x18, starting transfers between devices, send(): return lax.ppermute(array, AXES, pairs)  18.1 us
    all_to_all x1, waiting for transfers between devices, per_device(): lax.all_to_all(jnp.concatenate([pairs, pairs]), 'z', split_axis=0, concat...  14.1 us
    all_to_all x1, starting transfers between devices, per_device(): lax.all_to_all(jnp.concatenate([pairs, pairs]), 'z', split_axis=0, concat...  9.01 us
  transfers between devices with their start and end apart: 19, of which 15 were waited for; matrix products, arithmetic and copies ran while one was open for 4% of the time, Pallas kernels for 7%

profile of v6, /device:TPU:1, one launch (start us, length us, event | category | flops | bytes accessed | tf_op | source)
XLA Modules:
  0.0 131.0 jit_solution(13780915418819057571)
XLA Ops:
  0.0 0.9 copy-done
  0.9 1.0 bitcast_bitcast_fusion
  2.0 0.8 maximum_maximum_fusion
  2.8 9.0 %all-to-all-start = ((bf16[8,2,128,128]{3,2,1,0:T(8,128)(2,1)}), bf16[8,2,128,128]{3,2,1,0:T(8,128)(2,1)S(1)}, u32[]{:S(2)}, u32[]{:S(2)}) async-start(bf16[8,2,128,128]{3,2,1,0:T(8,128)(2,1)} %maximum_maximum_fusion), calls=%async_computation | async-start | bytes 1048576 | tf_op jit(solution)/shard_map/all_to_all | solution.py:316
  11.8 0.1 fusion.30
  12.9 0.1 dynamic_slice.30
  13.3 0.1 convert_reduce_fusion.3
  13.4 0.1 convert_reduce_fusion.2
  13.7 0.1 reduce_max.19
  13.8 0.1 reduce_max.18
  14.0 0.3 convert_reduce_fusion.1
  14.3 0.4 select_reduce_fusion.1
  14.8 0.9 constant_dynamic-slice_fusion
  15.6 14.1 %all-to-all-done = bf16[8,2,128,128]{3,2,1,0:T(8,128)(2,1)S(1)} async-done(((bf16[8,2,128,128]{3,2,1,0:T(8,128)(2,1)}), bf16[8,2,128,128]{3,2,1,0:T(8,128)(2,1)S(1)}, u32[]{:S(2)}, u32[]{:S(2)}) %all-to-all-start) | async-done | bytes 524320 | tf_op jit(solution)/shard_map/all_to_all | solution.py:316
  29.8 1.3 collective-permute-start
  31.1 1.4 %collective-permute-start.1 = (bf16[2048,128]{1,0:T(8,128)(2,1)S(1)}, bf16[2048,128]{1,0:T(8,128)(2,1)S(1)}, u32[]{:S(2)}, u32[]{:S(2)}) collective-permute-start(bf16[2048,128]{1,0:T(8,128)(2,1)S(1)} %bitcast.33), channel_id=1, source_target_pairs={{0,3},{16,28},{1,0},{17,29},{2,1},{18,30},{3,2},{19,31},{4,7},{20,... | collective-permute-start | bytes 1572872 | tf_op jit(solution)/shard_map/ppermute | solution.py:272
  32.5 1.6 %collective-permute-start.2 = (bf16[2048,128]{1,0:T(8,128)(2,1)S(1)}, bf16[2048,128]{1,0:T(8,128)(2,1)S(1)}, u32[]{:S(2)}, u32[]{:S(2)}) collective-permute-start(bf16[2048,128]{1,0:T(8,128)(2,1)S(1)} %bitcast.34), channel_id=1, source_target_pairs={{0,2},{16,24},{1,3},{17,25},{2,0},{18,26},{3,1},{19,27},{4,6},{20,... | collective-permute-start | bytes 1572872 | tf_op jit(solution)/shard_map/ppermute | solution.py:272
  34.2 2.7 %collective-permute-start.4 = (bf16[128,1024]{1,0:T(8,128)(2,1)}, bf16[128,1024]{1,0:T(8,128)(2,1)S(1)}, u32[]{:S(2)}, u32[]{:S(2)}) collective-permute-start(bf16[128,1024]{1,0:T(8,128)(2,1)} %get-tuple-element.38), channel_id=1, source_target_pairs={{0,224},{16,240},{1,225},{17,241},{2,226},{18,242},{3,227},{19,243... | collective-permute-start | bytes 786440 | tf_op jit(solution)/shard_map/ppermute | solution.py:272
  37.1 5.2 %collective-permute-done.3.refs_1_ = bf16[128,1024]{1,0:T(8,128)(2,1)S(1)} collective-permute-done((bf16[128,1024]{1,0:T(8,128)(2,1)}, bf16[128,1024]{1,0:T(8,128)(2,1)S(1)}, u32[]{:S(2)}, u32[]{:S(2)}) %collective-permute-start.3) | collective-permute-done | bytes 262176 | tf_op jit(solution)/shard_map/ppermute | solution.py:272
  42.3 3.9 %collective-permute-done.2 = bf16[2048,128]{1,0:T(8,128)(2,1)S(1)} collective-permute-done((bf16[2048,128]{1,0:T(8,128)(2,1)S(1)}, bf16[2048,128]{1,0:T(8,128)(2,1)S(1)}, u32[]{:S(2)}, u32[]{:S(2)}) %collective-permute-start.2) | collective-permute-done | bytes 524320 | tf_op jit(solution)/shard_map/ppermute | solution.py:272
  46.4 1.2 collective-permute-start.8
  47.6 1.1 collective-permute-start.6
  48.7 1.5 %collective-permute-start.7 = (bf16[8192,128]{1,0:T(8,128)(2,1)S(1)}, bf16[8192,128]{1,0:T(8,128)(2,1)S(1)}, u32[]{:S(2)}, u32[]{:S(2)}) collective-permute-start(bf16[8192,128]{1,0:T(8,128)(2,1)S(1)} %constant_dynamic-update-slice_fusion.refs_0_), channel_id=1, source_target_pairs={{0,12},{16,19},{1,13},{17,16},{2,14},{18,17},{3,15},{19,18},{4,0},... | collective-permute-start | bytes 6291464 | tf_op jit(solution)/shard_map/ppermute | solution.py:272
  50.3 1.0 collective-permute-done.8.refs_1_
  51.3 0.3 shard_map.73.refs_4_
  51.7 7.8 %collective-permute-done.5.refs_3_ = bf16[128,1024]{1,0:T(8,128)(2,1)S(1)} collective-permute-done((bf16[128,1024]{1,0:T(8,128)(2,1)S(1)}, bf16[128,1024]{1,0:T(8,128)(2,1)S(1)}, u32[]{:S(2)}, u32[]{:S(2)}) %collective-permute-start.5) | collective-permute-done | bytes 262176 | tf_op jit(solution)/shard_map/ppermute | solution.py:272
  59.5 8.7 %shard_map.74 = (f32[4096,128]{1,0:T(8,128)S(1)}, f32[4096,128]{1,0:T(8,128)S(1)}, f32[4096,128]{1,0:T(8,128)S(1)}) custom-call(s32[4608]{0:T(1024)S(1)} %reshape.689.lists, s32[144]{0:T(256)S(1)} %pad_add_fusion.3.counts, bf16[128,1024]{1,0:T(8,128)(2,1)S(1)} %get-tuple-element.42.refs_0_, bf16[128,1024]{1,0:T(8,128)(2,1)S(1)} %collective-permute-done.3.refs_1_, ...), custom_call_target="tpu_custom_call" | custom-call | flops 3000000000 | bytes 30000000 | tf_op jit(solution)/shard_map/pallas_call | solution.py:185
  68.2 5.8 %collective-permute-done.6.refs_0_ = bf16[8192,128]{1,0:T(8,128)(2,1)S(1)} collective-permute-done((bf16[8192,128]{1,0:T(8,128)(2,1)S(1)}, bf16[8192,128]{1,0:T(8,128)(2,1)S(1)}, u32[]{:S(2)}, u32[]{:S(2)}) %collective-permute-start.6) | collective-permute-done | bytes 2097184 | tf_op jit(solution)/shard_map/ppermute | solution.py:272
  74.0 1.3 collective-permute-start.11
  75.4 2.1 %collective-permute-start.10 = (bf16[4096,128]{1,0:T(8,128)(2,1)S(1)}, bf16[4096,128]{1,0:T(8,128)(2,1)S(1)}, u32[]{:S(2)}, u32[]{:S(2)}) collective-permute-start(bf16[4096,128]{1,0:T(8,128)(2,1)S(1)} %slice.7), channel_id=1, source_target_pairs={{0,12},{16,19},{1,13},{17,16},{2,14},{18,17},{3,15},{19,18},{4,0},... | collective-permute-start | bytes 3145736 | tf_op jit(solution)/shard_map/ppermute | solution.py:272
  77.5 1.6 %collective-permute-done.11.refs_2_ = bf16[8192,128]{1,0:T(8,128)(2,1)S(1)} collective-permute-done((bf16[8192,128]{1,0:T(8,128)(2,1)S(1)}, bf16[8192,128]{1,0:T(8,128)(2,1)S(1)}, u32[]{:S(2)}, u32[]{:S(2)}) %collective-permute-start.11) | collective-permute-done | bytes 2097184 | tf_op jit(solution)/shard_map/ppermute | solution.py:272
  79.0 3.0 %collective-permute-done.12.refs_3_ = bf16[8192,128]{1,0:T(8,128)(2,1)S(1)} collective-permute-done((bf16[8192,128]{1,0:T(8,128)(2,1)S(1)}, bf16[8192,128]{1,0:T(8,128)(2,1)S(1)}, u32[]{:S(2)}, u32[]{:S(2)}) %collective-permute-start.12) | collective-permute-done | bytes 2097184 | tf_op jit(solution)/shard_map/ppermute | solution.py:272
  82.0 0.6 shard_map.75.refs_4_
  82.7 6.8 %collective-permute-done.10.refs_1_ = bf16[4096,128]{1,0:T(8,128)(2,1)S(1)} collective-permute-done((bf16[4096,128]{1,0:T(8,128)(2,1)S(1)}, bf16[4096,128]{1,0:T(8,128)(2,1)S(1)}, u32[]{:S(2)}, u32[]{:S(2)}) %collective-permute-start.10) | collective-permute-done | bytes 1048608 | tf_op jit(solution)/shard_map/ppermute | solution.py:272
  89.4 3.2 %collective-permute-done.9.refs_0_ = bf16[4096,128]{1,0:T(8,128)(2,1)S(1)} collective-permute-done((bf16[4096,128]{1,0:T(8,128)(2,1)S(1)}, bf16[4096,128]{1,0:T(8,128)(2,1)S(1)}, u32[]{:S(2)}, u32[]{:S(2)}) %collective-permute-start.9) | collective-permute-done | bytes 1048608 | tf_op jit(solution)/shard_map/ppermute | solution.py:272
  92.6 2.3 %collective-permute-start.13 = (bf16[4096,128]{1,0:T(8,128)(2,1)S(1)}, bf16[4096,128]{1,0:T(8,128)(2,1)S(1)}, u32[]{:S(2)}, u32[]{:S(2)}) collective-permute-start(bf16[4096,128]{1,0:T(8,128)(2,1)S(1)} %collective-permute-done.9.refs_0_), channel_id=1, source_target_pairs={{0,16},{16,0},{1,17},{17,1},{2,18},{18,2},{3,19},{19,3},{4,20},{20... | collective-permute-start | bytes 3145736 | tf_op jit(solution)/shard_map/ppermute | solution.py:272
  94.9 2.3 %collective-permute-done.13.refs_2_ = bf16[4096,128]{1,0:T(8,128)(2,1)S(1)} collective-permute-done((bf16[4096,128]{1,0:T(8,128)(2,1)S(1)}, bf16[4096,128]{1,0:T(8,128)(2,1)S(1)}, u32[]{:S(2)}, u32[]{:S(2)}) %collective-permute-start.13) | collective-permute-done | bytes 1048608 | tf_op jit(solution)/shard_map/ppermute | solution.py:272
  97.2 1.5 %collective-permute-done.14.refs_3_ = bf16[4096,128]{1,0:T(8,128)(2,1)S(1)} collective-permute-done((bf16[4096,128]{1,0:T(8,128)(2,1)S(1)}, bf16[4096,128]{1,0:T(8,128)(2,1)S(1)}, u32[]{:S(2)}, u32[]{:S(2)}) %collective-permute-start.14) | collective-permute-done | bytes 1048608 | tf_op jit(solution)/shard_map/ppermute | solution.py:272
  98.7 0.3 shard_map.76.refs_4_
  99.0 16.2 %shard_map.77 = (f32[4096,128]{1,0:T(8,128)S(1)}, f32[4096,128]{1,0:T(8,128)S(1)}, f32[4096,128]{1,0:T(8,128)S(1)}, bf16[128,1024]{1,0:T(8,128)(2,1)S(1)}, bf16[...) custom-call(s32[4608]{0:T(1024)S(1)} %reshape.689.lists, ...), custom_call_target="tpu_custom_call", output_to_operand_aliasing={{0}: (7, {}), {1}: (8, {}), {2}: (9, {})} | custom-call | flops 3000000000 | bytes 30000000 | tf_op jit(solution)/shard_map/pallas_call | solution.py:185
  115.2 0.7 copy-done.1
  115.9 1.5 %collective-permute-start.16 = (bf16[128,1024]{1,0:T(8,128)(2,1)S(1)}, bf16[128,1024]{1,0:T(8,128)(2,1)S(1)}, u32[]{:S(2)}, u32[]{:S(2)}) collective-permute-start(bf16[128,1024]{1,0:T(8,128)(2,1)S(1)} %get-tuple-element.63), channel_id=1, source_target_pairs={{0,32},{16,48},{1,33},{17,49},{2,34},{18,50},{3,35},{19,51},{4,36}... | collective-permute-start | bytes 786440 | tf_op jit(solution)/shard_map/ppermute | solution.py:272
  117.4 0.7 and_select_fusion.3.starts
  118.1 4.4 %collective-permute-done.15.refs_1_ = bf16[128,1024]{1,0:T(8,128)(2,1)S(1)} collective-permute-done((bf16[128,1024]{1,0:T(8,128)(2,1)S(1)}, bf16[128,1024]{1,0:T(8,128)(2,1)S(1)}, u32[]{:S(2)}, u32[]{:S(2)}) %collective-permute-start.15) | collective-permute-done | bytes 262176 | tf_op jit(solution)/shard_map/ppermute | solution.py:272
  122.5 1.2 collective-permute-done.16.refs_2_
  123.7 4.3 %collective-permute-done.17.refs_3_ = bf16[128,1024]{1,0:T(8,128)(2,1)S(1)} collective-permute-done((bf16[128,1024]{1,0:T(8,128)(2,1)S(1)}, bf16[128,1024]{1,0:T(8,128)(2,1)S(1)}, u32[]{:S(2)}, u32[]{:S(2)}) %collective-permute-start.17) | collective-permute-done | bytes 262176 | tf_op jit(solution)/shard_map/ppermute | solution.py:272
  128.0 0.7 copy-done.5
  128.7 2.2 %shard_map.78 = bf16[128,4096]{1,0:T(8,128)(2,1)} custom-call(s32[4]{0:T(128)} %and_select_fusion.3.starts, bf16[128,1024]{1,0:T(8,128)(2,1)} %copy-done.1, bf16[128,1024]{1,0:T(8,128)(2,1)} %copy-done.3, bf16[128,1024]{1,0:T(8,128)(2,1)} %copy-done.4, bf16[128,1024]{1,0:T(8,128)(2,1)} %copy-done.5), custom_call_target="tpu_custom_call" | custom-call | tf_op jit(solution)/shard_map/pallas_call | solution.py:207
  (63 shorter events, 2.2 us)
Async XLA Ops:
  0.0 0.9 copy-start
  0.0 12.2 %copy-start.7 = (s32[32,8]{0,1:T(8,128)S(1)}, s32[32,8]{0,1:T(8,128)}, u32[]{:S(2)}) copy-start(s32[32,8]{0,1:T(8,128)} %param.10) | copy-start | bytes 3076
  0.0 12.4 %copy-start.8 = (s32[32]{0:T(128)S(1)}, s32[32]{0:T(128)}, u32[]{:S(2)}) copy-start(s32[32]{0:T(128)} %param.11) | copy-start | bytes 388
  0.0 12.7 %copy-start.6 = (s32[32,24]{0,1:T(8,128)S(1)}, s32[32,24]{0,1:T(8,128)}, u32[]{:S(2)}) copy-start(s32[32,24]{0,1:T(8,128)} %param.12) | copy-start | bytes 9220
  0.0 12.9 %copy-start.9 = (s32[32]{0:T(128)S(1)}, s32[32]{0:T(128)}, u32[]{:S(2)}) copy-start(s32[32]{0:T(128)} %param.13) | copy-start | bytes 388
  0.9 13.9 %copy-start.2 = (bf16[128,4096]{1,0:T(8,128)(2,1)S(1)}, bf16[128,4096]{1,0:T(8,128)(2,1)}, u32[]{:S(2)}) copy-start(bf16[128,4096]{1,0:T(8,128)(2,1)} %param.7) | copy-start | bytes 3145732
  2.8 27.0 %all-to-all-start = ((bf16[8,2,128,128]{3,2,1,0:T(8,128)(2,1)}), bf16[8,2,128,128]{3,2,1,0:T(8,128)(2,1)S(1)}, u32[]{:S(2)}, u32[]{:S(2)}) async-start(bf16[8,2,128,128]{3,2,1,0:T(8,128)(2,1)} %maximum_maximum_fusion), calls=%async_computation | async-start | bytes 1048576 | tf_op jit(solution)/shard_map/all_to_all | solution.py:316
  29.8 12.5 %collective-permute-start = (bf16[2048,128]{1,0:T(8,128)(2,1)S(1)}, bf16[2048,128]{1,0:T(8,128)(2,1)S(1)}, u32[]{:S(2)}, u32[]{:S(2)}) collective-permute-start(bf16[2048,128]{1,0:T(8,128)(2,1)S(1)} %bitcast.32), channel_id=1, source_target_pairs={{0,1},{16,20},{1,2},{17,21},{2,3},{18,22},{3,0},{19,23},{4,5},{20,... | collective-permute-start | bytes 1572872 | tf_op jit(solution)/shard_map/ppermute | solution.py:272
  31.1 11.2 %collective-permute-start.1 = (bf16[2048,128]{1,0:T(8,128)(2,1)S(1)}, bf16[2048,128]{1,0:T(8,128)(2,1)S(1)}, u32[]{:S(2)}, u32[]{:S(2)}) collective-permute-start(bf16[2048,128]{1,0:T(8,128)(2,1)S(1)} %bitcast.33), channel_id=1, source_target_pairs={{0,3},{16,28},{1,0},{17,29},{2,1},{18,30},{3,2},{19,31},{4,7},{20,... | collective-permute-start | bytes 1572872 | tf_op jit(solution)/shard_map/ppermute | solution.py:272
  32.5 13.7 %collective-permute-start.2 = (bf16[2048,128]{1,0:T(8,128)(2,1)S(1)}, bf16[2048,128]{1,0:T(8,128)(2,1)S(1)}, u32[]{:S(2)}, u32[]{:S(2)}) collective-permute-start(bf16[2048,128]{1,0:T(8,128)(2,1)S(1)} %bitcast.34), channel_id=1, source_target_pairs={{0,2},{16,24},{1,3},{17,25},{2,0},{18,26},{3,1},{19,27},{4,6},{20,... | collective-permute-start | bytes 1572872 | tf_op jit(solution)/shard_map/ppermute | solution.py:272
  34.2 8.1 %collective-permute-start.3 = (bf16[128,1024]{1,0:T(8,128)(2,1)}, bf16[128,1024]{1,0:T(8,128)(2,1)S(1)}, u32[]{:S(2)}, u32[]{:S(2)}) collective-permute-start(bf16[128,1024]{1,0:T(8,128)(2,1)} %get-tuple-element.37), channel_id=1, source_target_pairs={{0,32},{16,48},{1,33},{17,49},{2,34},{18,50},{3,35},{19,51},{4,36}... | collective-permute-start | bytes 786440 | tf_op jit(solution)/shard_map/ppermute | solution.py:272
  34.2 8.0 %collective-permute-start.4 = (bf16[128,1024]{1,0:T(8,128)(2,1)}, bf16[128,1024]{1,0:T(8,128)(2,1)S(1)}, u32[]{:S(2)}, u32[]{:S(2)}) collective-permute-start(bf16[128,1024]{1,0:T(8,128)(2,1)} %get-tuple-element.38), channel_id=1, source_target_pairs={{0,224},{16,240},{1,225},{17,241},{2,226},{18,242},{3,227},{19,243... | collective-permute-start | bytes 786440 | tf_op jit(solution)/shard_map/ppermute | solution.py:272
  46.4 5.0 %collective-permute-start.8 = (bf16[8192,128]{1,0:T(8,128)(2,1)S(1)}, bf16[8192,128]{1,0:T(8,128)(2,1)S(1)}, u32[]{:S(2)}, u32[]{:S(2)}) collective-permute-start(bf16[8192,128]{1,0:T(8,128)(2,1)S(1)} %constant_dynamic-update-slice_fusion.refs_0_), channel_id=1, source_target_pairs={{0,16},{16,0},{1,17},{17,1},{2,18},{18,2},{3,19},{19,3},{4,20},{20... | collective-permute-start | bytes 6291464 | tf_op jit(solution)/shard_map/ppermute | solution.py:272
  47.6 26.4 %collective-permute-start.6 = (bf16[8192,128]{1,0:T(8,128)(2,1)S(1)}, bf16[8192,128]{1,0:T(8,128)(2,1)S(1)}, u32[]{:S(2)}, u32[]{:S(2)}) collective-permute-start(bf16[8192,128]{1,0:T(8,128)(2,1)S(1)} %constant_dynamic-update-slice_fusion.refs_0_), channel_id=1, source_target_pairs={{0,4},{16,17},{1,5},{17,18},{2,6},{18,19},{3,7},{19,16},{4,8},{20,... | collective-permute-start | bytes 6291464 | tf_op jit(solution)/shard_map/ppermute | solution.py:272
  48.7 25.3 %collective-permute-start.7 = (bf16[8192,128]{1,0:T(8,128)(2,1)S(1)}, bf16[8192,128]{1,0:T(8,128)(2,1)S(1)}, u32[]{:S(2)}, u32[]{:S(2)}) collective-permute-start(bf16[8192,128]{1,0:T(8,128)(2,1)S(1)} %constant_dynamic-update-slice_fusion.refs_0_), channel_id=1, source_target_pairs={{0,12},{16,19},{1,13},{17,16},{2,14},{18,17},{3,15},{19,18},{4,0},... | collective-permute-start | bytes 6291464 | tf_op jit(solution)/shard_map/ppermute | solution.py:272
  50.2 9.2 %collective-permute-start.5 = (bf16[128,1024]{1,0:T(8,128)(2,1)S(1)}, bf16[128,1024]{1,0:T(8,128)(2,1)S(1)}, u32[]{:S(2)}, u32[]{:S(2)}) collective-permute-start(bf16[128,1024]{1,0:T(8,128)(2,1)S(1)} %get-tuple-element.45), channel_id=1, source_target_pairs={{0,64},{16,208},{1,65},{17,209},{2,66},{18,210},{3,67},{19,211},{4... | collective-permute-start | bytes 786440 | tf_op jit(solution)/shard_map/ppermute | solution.py:272
  74.0 5.1 %collective-permute-start.11 = (bf16[8192,128]{1,0:T(8,128)(2,1)S(1)}, bf16[8192,128]{1,0:T(8,128)(2,1)S(1)}, u32[]{:S(2)}, u32[]{:S(2)}) collective-permute-start(bf16[8192,128]{1,0:T(8,128)(2,1)S(1)} %collective-permute-done.6.refs_0_), channel_id=1, source_target_pairs={{0,16},{16,0},{1,17},{17,1},{2,18},{18,2},{3,19},{19,3},{4,20},{20... | collective-permute-start | bytes 6291464 | tf_op jit(solution)/shard_map/ppermute | solution.py:272
  75.3 6.8 %collective-permute-start.12 = (bf16[8192,128]{1,0:T(8,128)(2,1)S(1)}, bf16[8192,128]{1,0:T(8,128)(2,1)S(1)}, u32[]{:S(2)}, u32[]{:S(2)}) collective-permute-start(bf16[8192,128]{1,0:T(8,128)(2,1)S(1)} %collective-permute-done.7.refs_1_), channel_id=1, source_target_pairs={{0,16},{16,0},{1,17},{17,1},{2,18},{18,2},{3,19},{19,3},{4,20},{20... | collective-permute-start | bytes 6291464 | tf_op jit(solution)/shard_map/ppermute | solution.py:272
  75.4 14.0 %collective-permute-start.10 = (bf16[4096,128]{1,0:T(8,128)(2,1)S(1)}, bf16[4096,128]{1,0:T(8,128)(2,1)S(1)}, u32[]{:S(2)}, u32[]{:S(2)}) collective-permute-start(bf16[4096,128]{1,0:T(8,128)(2,1)S(1)} %slice.7), channel_id=1, source_target_pairs={{0,12},{16,19},{1,13},{17,16},{2,14},{18,17},{3,15},{19,18},{4,0},... | collective-permute-start | bytes 3145736 | tf_op jit(solution)/shard_map/ppermute | solution.py:272
  77.5 15.2 %collective-permute-start.9 = (bf16[4096,128]{1,0:T(8,128)(2,1)S(1)}, bf16[4096,128]{1,0:T(8,128)(2,1)S(1)}, u32[]{:S(2)}, u32[]{:S(2)}) collective-permute-start(bf16[4096,128]{1,0:T(8,128)(2,1)S(1)} %slice.6), channel_id=1, source_target_pairs={{0,4},{16,17},{1,5},{17,18},{2,6},{18,19},{3,7},{19,16},{4,8},{20,... | collective-permute-start | bytes 3145736 | tf_op jit(solution)/shard_map/ppermute | solution.py:272
  92.6 4.5 %collective-permute-start.13 = (bf16[4096,128]{1,0:T(8,128)(2,1)S(1)}, bf16[4096,128]{1,0:T(8,128)(2,1)S(1)}, u32[]{:S(2)}, u32[]{:S(2)}) collective-permute-start(bf16[4096,128]{1,0:T(8,128)(2,1)S(1)} %collective-permute-done.9.refs_0_), channel_id=1, source_target_pairs={{0,16},{16,0},{1,17},{17,1},{2,18},{18,2},{3,19},{19,3},{4,20},{20... | collective-permute-start | bytes 3145736 | tf_op jit(solution)/shard_map/ppermute | solution.py:272
  94.9 3.8 %collective-permute-start.14 = (bf16[4096,128]{1,0:T(8,128)(2,1)S(1)}, bf16[4096,128]{1,0:T(8,128)(2,1)S(1)}, u32[]{:S(2)}, u32[]{:S(2)}) collective-permute-start(bf16[4096,128]{1,0:T(8,128)(2,1)S(1)} %collective-permute-done.10.refs_1_), channel_id=1, source_target_pairs={{0,16},{16,0},{1,17},{17,1},{2,18},{18,2},{3,19},{19,3},{4,20},{20... | collective-permute-start | bytes 3145736 | tf_op jit(solution)/shard_map/ppermute | solution.py:272
  115.2 0.7 copy-start.1
  115.9 6.6 %collective-permute-start.15 = (bf16[128,1024]{1,0:T(8,128)(2,1)S(1)}, bf16[128,1024]{1,0:T(8,128)(2,1)S(1)}, u32[]{:S(2)}, u32[]{:S(2)}) collective-permute-start(bf16[128,1024]{1,0:T(8,128)(2,1)S(1)} %get-tuple-element.62), channel_id=1, source_target_pairs={{0,224},{16,240},{1,225},{17,241},{2,226},{18,242},{3,227},{19,243... | collective-permute-start | bytes 786440 | tf_op jit(solution)/shard_map/ppermute | solution.py:272
  115.9 7.8 %collective-permute-start.16 = (bf16[128,1024]{1,0:T(8,128)(2,1)S(1)}, bf16[128,1024]{1,0:T(8,128)(2,1)S(1)}, u32[]{:S(2)}, u32[]{:S(2)}) collective-permute-start(bf16[128,1024]{1,0:T(8,128)(2,1)S(1)} %get-tuple-element.63), channel_id=1, source_target_pairs={{0,32},{16,48},{1,33},{17,49},{2,34},{18,50},{3,35},{19,51},{4,36}... | collective-permute-start | bytes 786440 | tf_op jit(solution)/shard_map/ppermute | solution.py:272
  117.4 10.6 %collective-permute-start.17 = (bf16[128,1024]{1,0:T(8,128)(2,1)S(1)}, bf16[128,1024]{1,0:T(8,128)(2,1)S(1)}, u32[]{:S(2)}, u32[]{:S(2)}) collective-permute-start(bf16[128,1024]{1,0:T(8,128)(2,1)S(1)} %get-tuple-element.64), channel_id=1, source_target_pairs={{0,192},{16,80},{1,193},{17,81},{2,194},{18,82},{3,195},{19,83},{4... | collective-permute-start | bytes 786440 | tf_op jit(solution)/shard_map/ppermute | solution.py:272
  122.5 5.6 %copy-start.3 = (bf16[128,1024]{1,0:T(8,128)(2,1)}, bf16[128,1024]{1,0:T(8,128)(2,1)S(1)}, u32[]{:S(2)}) copy-start(bf16[128,1024]{1,0:T(8,128)(2,1)S(1)} %collective-permute-done.15.refs_1_) | copy-start | bytes 786436
  123.7 4.3 %copy-start.4 = (bf16[128,1024]{1,0:T(8,128)(2,1)}, bf16[128,1024]{1,0:T(8,128)(2,1)S(1)}, u32[]{:S(2)}) copy-start(bf16[128,1024]{1,0:T(8,128)(2,1)S(1)} %collective-permute-done.16.refs_2_) | copy-start | bytes 786436
  128.0 0.7 copy-start.5
